TPU v7x, 128 devices: a whole 4x4x4 slice. The times are simulated.
128 devices in a mesh: band: 16 (over z, y_lo, core), blk: 8 (over x, y_hi).
Axes of the slice: x: 4, y: 4 (y_hi: 2, y_lo: 2; y = y_hi * 2 + y_lo), z: 4, core: 2. Of those that a mesh axis runs over, the one named last changes fastest.
Arguments:
- steering: bfloat16 [8, 12288, 512], P('blk', 'band'), may hold values from -1.4 to 1.4
- estimates: bfloat16 [8, 12288], P('blk', 'band'), may hold values from 0 to 1
- spectra: float32 [8, 256, 512], P('blk', 'band'), may hold values from -768 to 8151
Outputs:
- updated: float32 [8, 12288], P('blk', 'band')
- broadband: float32 [12288], P('band')
All inputs are finite; a program needn't handle non-finite values.
Results may differ from a plain program's by a relative error of at most 0.0003.
Values may be sent and summed in bfloat16 or wider, within the bound.
No kernel may reach another device: no remote copies, remote signals or barrier semaphores. Data moves between devices by JAX's collectives and lax.ppermute only.
A program may use at most 192 MiB of HBM per device.

v0:
```python
import jax
import jax.numpy as jnp
from jax import lax
from jax.sharding import PartitionSpec as P

CHANNELS = 256


def body(steering, estimates, spectra):
    width = CHANNELS
    steer_wide = steering.astype(jnp.float32)
    turned = jnp.concatenate([-steering[..., width:], steering[..., :width]], axis=2)
    mine_values = estimates.astype(jnp.float32)
    piece = lax.all_gather(spectra, "band", axis=1, tiled=True)
    cross_real = piece[..., :width]
    cross_imag = piece[..., width:]
    kernel_real = jnp.concatenate([cross_real, -cross_imag], axis=2)
    kernel_imag = jnp.concatenate([cross_imag, cross_real], axis=2)
    real_part = jnp.einsum(
        "bgk,brk->bgr",
        steer_wide,
        kernel_real,
        precision=lax.Precision.HIGHEST,
        preferred_element_type=jnp.float32,
    )
    imag_part = jnp.einsum(
        "bgk,brk->bgr",
        steer_wide,
        kernel_imag,
        precision=lax.Precision.HIGHEST,
        preferred_element_type=jnp.float32,
    )
    count = piece.shape[1]
    weight_real = lax.slice_in_dim(steer_wide, 0, count, axis=2)
    weight_imag = lax.dynamic_slice_in_dim(steer_wide, width, count, 2)
    beam = jnp.sum(weight_real * real_part + weight_imag * imag_part, axis=2) / (width * width)
    blocks = lax.all_gather(steering, "band", axis=1, tiled=True)
    values = lax.all_gather(estimates, "band", axis=1, tiled=True)
    real_sum = jnp.einsum("bgk,bhk->bgh", steering, blocks, preferred_element_type=jnp.float32)
    imag_sum = jnp.einsum("bgk,bhk->bgh", turned, blocks, preferred_element_type=jnp.float32)
    tile = (real_sum * real_sum + imag_sum * imag_sum) / (width * width)
    applied = jnp.einsum(
        "bgh,bh->bg",
        tile,
        values.astype(jnp.float32),
        precision=lax.Precision.HIGHEST,
        preferred_element_type=jnp.float32,
    )
    power = jnp.sum(steer_wide * steer_wide, axis=2)
    diag = power * power / (width * width)
    updated = jnp.maximum(mine_values + (beam - applied) / diag, 0.0)
    broadband = lax.psum(jnp.sum(updated, axis=0), "blk")
    return (updated, broadband)


def solution(mesh):
    return jax.shard_map(
        body,
        mesh=mesh,
        in_specs=(P("blk", "band", None), P("blk", "band"), P("blk", "band", None)),
        out_specs=(P("blk", "band"), P("band")),
        check_vma=False,
    )
```

profile of v0, /device:TPU:0, one launch (start us, length us, event | category | flops | bytes accessed | tf_op | source)
XLA Modules:
  0.0 193.6 jit_solution(9137169835309598195)
XLA Ops:
  7.2 0.0 copy-start
  7.2 0.0 all-gather.2.cloned.1.call-start
  7.2 0.7 all-gather.2.cloned.1.call-update
  7.9 1.4 copy.5
  9.3 0.1 convert_element_type.8
  9.4 21.6 %all_gather.11 = bf16[1,12288]{1,0:T(2,128)(2,1)S(1)} all-gather(bf16[1,768]{1,0:T(2,128)(2,1)} %param.4), channel_id=1, replica_groups=mesh['band'=16,'blk'=8] {'band'}, dimensions={1}, use_global_device_ids=true | all-gather | bytes 26112 | tf_op jit(solution)/shard_map/all_gather | solution.py:38
  31.0 0.2 multiply_reduce_fusion
  31.2 23.5 %all_gather.9 = f32[1,256,512]{2,1,0:T(8,128)S(1)} all-gather(f32[1,16,512]{2,1,0:T(8,128)} %param.5), channel_id=1, replica_groups=mesh['band'=16,'blk'=8] {'band'}, dimensions={1}, use_global_device_ids=true | all-gather | bytes 557056 | tf_op jit(solution)/shard_map/all_gather | solution.py:14
  54.8 0.1 slice_negate_fusion.1
  54.8 2.0 %fusion.12 = f32[1,768,256]{1,2,0:T(8,128)S(1)} fusion(f32[1,768,512]{1,2,0:T(8,128)S(1)} %convert_element_type.8, bf16[1,768,512]{2,1,0:T(8,128)(2,1)} %param.3, f32[1,256,256]{2,1,0:T(8,128)S(1)} %get-tuple-element.8, f32[1,256,256]{2,1,0:T(8,128)S(1)} %get-tuple-element.7), kind=kOutput, calls=%fused_computation.15 | convolution fusion | flops 1208287232 | bytes 2883584 | tf_op jit(solution)/shard_map/bgk,brk->bgr/dot_general | solution.py:26
  56.8 2.0 %fusion.13 = f32[768]{0:T(1024)S(1)} fusion(f32[1,768,256]{1,2,0:T(8,128)S(1)} %fusion.12, f32[1,768,512]{1,2,0:T(8,128)S(1)} %convert_element_type.8, bf16[1,768,512]{2,1,0:T(8,128)(2,1)} %param.3, f32[1,256,256]{2,1,0:T(8,128)S(1)} %get-tuple-element.6, f32[1,256,256]{2,1,0:T(8,128)S(1)} %get-tuple-element.8), kind=kOutput, calls=%fused_computation.16 | convolution fusion | flops 1208679680 | bytes 2886656 | tf_op jit(solution)/shard_map/bgk,brk->bgr/dot_general | solution.py:19
  58.8 0.0 copy-done
  58.8 0.1 slice_negate_fusion
  58.8 30.1 %all-gather.2.cloned.1.call-done = bf16[1,12288,512]{2,1,0:T(8,128)(2,1)} async-done(((bf16[1,768,512]{2,1,0:T(8,128)(2,1)}), bf16[1,12288,512]{2,1,0:T(8,128)(2,1)}) %all-gather.2.cloned.1.call-update) | async-done | bytes 12582928 | tf_op jit(solution)/shard_map/all_gather | solution.py:37
  88.9 21.7 %fusion.8 = f32[768,12288]{1,0:T(8,128)} fusion(bf16[1,12288,512]{2,1,0:T(8,128)(2,1)} %all-gather.2.cloned.1.call-done, bf16[1,768,512]{2,1,0:T(8,128)(2,1)S(1)} %copy-done), kind=kOutput, calls=%fused_computation.8 | convolution fusion | flops 9663676416 | bytes 51118080 | tf_op jit(solution)/shard_map/bgk,bhk->bgh/dot_general | solution.py:39
  110.6 21.7 %fusion.6 = f32[768,12288]{1,0:T(8,128)} fusion(bf16[1,12288,512]{2,1,0:T(8,128)(2,1)} %all-gather.2.cloned.1.call-done, bf16[1,768,256]{2,1,0:T(8,128)(2,1)S(1)} %get-tuple-element.5, bf16[1,768,256]{2,1,0:T(8,128)(2,1)S(1)} %get-tuple-element.4), kind=kOutput, calls=%fused_computation.6 | convolution fusion | flops 9665249280 | bytes 51118080 | tf_op jit(solution)/shard_map/bgk,bhk->bgh/dot_general | solution.py:40
  132.3 0.0 copy-start.1
  132.3 29.5 %fusion.14 = f32[768]{0:T(1024)S(1)} fusion(f32[768,12288]{1,0:T(8,128)} %fusion.6, f32[768,12288]{1,0:T(8,128)} %fusion.8, bf16[1,12288]{1,0:T(2,128)(2,1)S(1)} %all_gather.11), kind=kOutput, calls=%fused_computation.17 | convolution fusion | flops 150994944 | bytes 75525120 | tf_op jit(solution)/shard_map/bgh,bh->bg/dot_general | solution.py:42
  161.8 0.0 copy-done.1
  161.8 0.6 fusion.31
  162.4 24.4 %psum.7 = f32[768]{0:T(1024)} all-reduce(f32[768]{0:T(1024)S(1)} %get-tuple-element.2), channel_id=1, replica_groups=mesh['band'=16,'blk'=8] {'blk'}, use_global_device_ids=true, to_apply=%region_2.0 | all-reduce | flops 768 | bytes 6144 | tf_op jit(solution)/shard_map/psum | solution.py:52
  (1 shorter events, 0.0 us)
Async XLA Ops:
  7.2 51.6 %copy-start = (bf16[1,768,512]{2,1,0:T(8,128)(2,1)S(1)}, bf16[1,768,512]{2,1,0:T(8,128)(2,1)}, u32[]{:S(2)}) copy-start(bf16[1,768,512]{2,1,0:T(8,128)(2,1)} %param.3) | copy-start | bytes 2359300
  7.2 81.7 %all-gather.2.cloned.1.call-start = ((), (), s32[]{:S(2)}) async-start(), calls=%async_computation | async-start | bytes 13369344 | tf_op jit(solution)/shard_map/all_gather | solution.py:37
  132.3 29.5 %copy-start.1 = (bf16[1,768]{1,0:T(2,128)(2,1)S(1)}, bf16[1,768]{1,0:T(2,128)(2,1)}, u32[]{:S(2)}) copy-start(bf16[1,768]{1,0:T(2,128)(2,1)} %param.4) | copy-start | bytes 4612
Sparse Core Ops, SparseCore 0:
  9.7 79.1 all-gather.1
where the time goes:
time: 194 us
  matrix products  76.8 us (40%)
  blocking collectives  69.5 us (36%)
  waiting for transfers between devices  30.8 us (16%)
  between operations  14.1 us (7%)
    all_gather x1, waiting for transfers between devices, body(): blocks = lax.all_gather(steering, 'band', axis=1, tiled=True)  30.1 us
    dot_general x1, matrix products, body(): jnp.einsum('bgh,bh->bg', tile, values.astype(jnp.float32), precision=lax....  29.5 us
    psum x1, blocking collectives, body(): broadband = lax.psum(jnp.sum(updated, axis=0), 'blk')  24.4 us
    all_gather x1, blocking collectives, body(): piece = lax.all_gather(spectra, 'band', axis=1, tiled=True)  23.5 us
    dot_general x1, matrix products, body(): jnp.einsum('bgk,bhk->bgh', turned, blocks, preferred_element_type=jnp.flo...  21.7 us
    dot_general x1, matrix products, body(): jnp.einsum('bgk,bhk->bgh', steering, blocks, preferred_element_type=jnp.f...  21.7 us
    all_gather x1, blocking collectives, body(): values = lax.all_gather(estimates, 'band', axis=1, tiled=True)  21.6 us
  transfers between devices with their start and end apart: 1, of which 1 were waited for; matrix products, arithmetic and copies ran while one was open for 3% of the time, Pallas kernels for 0%

commit v1 on v0

v1 whole, which is shorter than its diff:
```python
import jax
import jax.numpy as jnp
from jax import lax
from jax.sharding import PartitionSpec as P

CHANNELS = 256


def exchange(value, axis, size, bit):
    return lax.ppermute(value, axis, [(i, i ^ bit) for i in range(size)])


def split_dot(exact, wide, contract):
    high = lax.reduce_precision(wide, 8, 7)
    low = (wide - high).astype(jnp.bfloat16)
    high = high.astype(jnp.bfloat16)
    dims = ((contract, (0,)), ((), ()))
    total = lax.dot_general(exact, high, dims, preferred_element_type=jnp.float32)
    return total + lax.dot_general(exact, low, dims, preferred_element_type=jnp.float32)


def body(steering, estimates, spectra):
    width = CHANNELS
    steering, spectra = steering[0], spectra[0]
    count = spectra.shape[0]
    index = lax.axis_index("band")
    core = lax.rem(index, 2)
    real, imag = steering[:, :width], steering[:, width:]
    real_wide, imag_wide = real.astype(jnp.float32), imag.astype(jnp.float32)
    values = estimates[0].astype(jnp.float32)
    minus, plus = real_wide - imag_wide, real_wide + imag_wide
    both = jnp.concatenate([real, imag], axis=0)
    mixed = jnp.concatenate([minus, plus], axis=0)
    twice = jnp.concatenate([values, values])[:, None]
    own = split_dot(both, mixed * twice, (0,))
    rows = (spectra[:, :width] + spectra[:, width:]) * 0.5
    columns = (spectra[:, :width] - spectra[:, width:]) * 0.5
    empty = jnp.zeros((width, width), jnp.float32)
    start = index * count
    placed = lax.dynamic_update_slice(empty, rows, (start, 0))
    turned = lax.dynamic_update_slice(empty, columns, (start, 0)).T
    packed = placed + turned - own
    half = width // 2
    send = lax.dynamic_slice_in_dim(packed, (1 - core) * half, half, 0)
    keep = lax.dynamic_slice_in_dim(packed, core * half, half, 0)
    keep = keep + exchange(send, "band", 16, 1)
    for bit in (2, 4, 8):
        keep = keep + exchange(keep, "band", 16, bit)
    other = exchange(keep, "band", 16, 1)
    low_half = jnp.where(core == 0, keep, other)
    high_half = jnp.where(core == 0, other, keep)
    packed = jnp.concatenate([low_half, high_half], axis=0)
    form = jnp.sum(split_dot(both, packed, (1,)) * mixed, axis=1)
    form = form[: values.shape[0]] + form[values.shape[0] :]
    scale = 1.0 / (width * width)
    power = jnp.sum(real_wide * real_wide + imag_wide * imag_wide, axis=1)
    diag = power * power * scale
    updated = jnp.maximum(values + form * scale / diag, 0.0)
    total = updated
    for bit in (1, 2, 4):
        total = total + exchange(total, "blk", 8, bit)
    return updated[None], total


def solution(mesh):
    return jax.shard_map(
        body,
        mesh=mesh,
        in_specs=(P("blk", "band", None), P("blk", "band"), P("blk", "band", None)),
        out_specs=(P("blk", "band"), P("band")),
        check_vma=False,
    )
```

time: 194 us -> 41.2 us (0.21)
  matrix products: 76.8 us -> 1.7 us
  blocking collectives: 69.5 us -> 0 us
  starting transfers between devices: 0.04 us -> 15.6 us
  between operations: 14.1 us -> 0.81 us
  waiting for transfers between devices: 30.8 us -> 18.1 us
  local copies, waits for them, and re-layouts: 1.42 us -> 3.79 us
    dot_general x5 -> x4, matrix products: 76.8 us -> 1.7 us  [the longest x2 0.89 us: split_dot(): lax.dot_general(exact, low, dims, preferred_element_type=jnp.float32)]
    all_gather x2 -> x0, blocking collectives: 45.1 us -> none  [the longest x1 23.5 us: body(): piece = lax.all_gather(spectra, 'band', axis=1, tiled=True)]
    all_gather x1 -> x0, waiting for transfers between devices: 30.1 us -> none  [body(): blocks = lax.all_gather(steering, 'band', axis=1, tiled=True)]
    psum x1 -> x0, blocking collectives: 24.4 us -> none  [body(): broadband = lax.psum(jnp.sum(updated, axis=0), 'blk')]
    ppermute x0 -> x8, waiting for transfers between devices: none -> 18.1 us  [exchange(): return lax.ppermute(value, axis, [(i, i ^ bit) for i in range(size)])]
    ppermute x0 -> x8, starting transfers between devices: none -> 15.6 us  [exchange(): return lax.ppermute(value, axis, [(i, i ^ bit) for i in range(size)])]
  transfers between devices with their start and end apart: 1 -> 8, of which waited for: 1 -> 8; matrix products, arithmetic and copies ran while one was open for 3% -> 1% of each run, Pallas kernels for 0% -> 0%
where the time goes in v1:
time: 41.2 us; the launch traced here: 40.9 us
  waiting for transfers between devices  18.1 us (44%)
  starting transfers between devices  15.6 us (38%)
  local copies, waits for them, and re-layouts  3.79 us (9%)
  matrix products  1.7 us (4%)
  other arithmetic  0.95 us (2%)
  between operations  0.81 us (2%)
    ppermute x8, waiting for transfers between devices, exchange(): return lax.ppermute(value, axis, [(i, i ^ bit) for i in range(size)])  18.1 us
    ppermute x8, starting transfers between devices, exchange(): return lax.ppermute(value, axis, [(i, i ^ bit) for i in range(size)])  15.6 us
    unnamed x6, local copies, waits for them, and re-layouts  1.93 us
    dynamic_update_slice x1, local copies, waits for them, and re-layouts, body(): turned = lax.dynamic_update_slice(empty, columns, (start, 0)).T  1.08 us
    dot_general x2, matrix products, split_dot(): lax.dot_general(exact, low, dims, preferred_element_type=jnp.float32)  0.89 us
  transfers between devices with their start and end apart: 8, of which 8 were waited for; matrix products, arithmetic and copies ran while one was open for 1% of the time, Pallas kernels for 0%

profile of v1, /device:TPU:0, one launch (start us, length us, event | category | flops | bytes accessed | tf_op | source)
XLA Modules:
  0.0 40.9 jit_solution(3549940124670970646)
XLA Ops:
  0.6 1.4 %copy.5 = bf16[1,768,512]{1,2,0:T(8,128)(2,1)S(1)} copy(bf16[1,768,512]{2,1,0:T(8,128)(2,1)} %param.3) | data formatting | bytes 1572864 | tf_op args[0]
  2.1 0.2 fusion.5
  2.4 0.4 %copy-done.1 = bf16[1,768]{1,0:T(2,128)(2,1)S(1)} copy-done((bf16[1,768]{1,0:T(2,128)(2,1)S(1)}, bf16[1,768]{1,0:T(2,128)(2,1)}, u32[]{:S(2)}) %copy-start.1) | copy-done | bytes 1560
  3.0 1.1 %dynamic_update_slice.6 = f32[256,256]{0,1:T(8,128)S(1)} dynamic-update-slice(f32[256,256]{0,1:T(8,128)S(1)} %broadcast_in_dim.7, f32[16,256]{0,1:T(8,128)S(1)} %copy.6, s32[]{:T(128)S(6)} %select_n.23, s32[]{:T(128)} %constant.12.clone.1) | dynamic-update-slice | bytes 32772 | tf_op jit(solution)/shard_map/dynamic_update_slice | solution.py:41
  4.2 0.4 %fusion.7 = f32[256,256]{1,0:T(8,128)S(1)} fusion(f32[768,256]{0,1:T(8,128)S(1)} %get-tuple-element.4, f32[768,256]{0,1:T(8,128)S(1)} %get-tuple-element.3, f32[1536]{0:T(1024)S(1)} %pad_maximum_fusion.3, bf16[768,256]{0,1:T(8,128)(2,1)S(1)} %get-tuple-element.6, bf16[768,256]{0,1:T(8,128)(2,1)S(1)} %get-tuple-element.5), kind=kOutput, calls=%fused_computation.15 | convolution fusion | flops 204472320 | bytes 2627584 | tf_op jit(solution)/shard_map/dot_general | solution.py:18
  4.6 0.4 %fusion.3 = f32[256,256]{1,0:T(8,128)S(1)} fusion(f32[256,256]{1,0:T(8,128)S(1)} %fusion.13, f32[256,256]{1,0:T(8,128)S(1)} %fusion.7, f32[768,256]{0,1:T(8,128)S(1)} %get-tuple-element.4, f32[768,256]{0,1:T(8,128)S(1)} %get-tuple-element.3, f32[1536]{0:T(1024)S(1)} %pad_maximum_fusion.3, bf16[768,256]{0,1:T(8,128)(2,1)S(1)} %get-tuple-element.6, ...), kind=kOutput, calls=%fused_computation.12 | convolution fusion | flops 204996608 | bytes 3151872 | tf_op jit(solution)/shard_map/dot_general | solution.py:19
  5.1 1.3 %collective-permute-done = f32[128,256]{1,0:T(8,128)S(1)} collective-permute-done((f32[128,256]{1,0:T(8,128)S(1)}, f32[128,256]{1,0:T(8,128)S(1)}, u32[]{:S(2)}, u32[]{:S(2)}) %collective-permute-start) | collective-permute-done | bytes 131104 | tf_op jit(solution)/shard_map/ppermute | solution.py:10
  6.5 2.0 %collective-permute-start.1 = (f32[128,256]{1,0:T(8,128)S(1)}, f32[128,256]{1,0:T(8,128)S(1)}, u32[]{:S(2)}, u32[]{:S(2)}) collective-permute-start(f32[128,256]{1,0:T(8,128)S(1)} %dynamic-slice_add_fusion), channel_id=1, source_target_pairs={{0,16},{8,24},{16,0},{24,8},{32,48},{40,56},{48,32},{56,40},{64,80... | collective-permute-start | bytes 393224 | tf_op jit(solution)/shard_map/ppermute | solution.py:10
  8.5 3.8 %collective-permute-done.1 = f32[128,256]{1,0:T(8,128)S(1)} collective-permute-done((f32[128,256]{1,0:T(8,128)S(1)}, f32[128,256]{1,0:T(8,128)S(1)}, u32[]{:S(2)}, u32[]{:S(2)}) %collective-permute-start.1) | collective-permute-done | bytes 131104 | tf_op jit(solution)/shard_map/ppermute | solution.py:10
  12.3 2.2 %collective-permute-start.2 = (f32[128,256]{1,0:T(8,128)S(1)}, f32[128,256]{1,0:T(8,128)S(1)}, u32[]{:S(2)}, u32[]{:S(2)}) collective-permute-start(f32[128,256]{1,0:T(8,128)S(1)} %add.64), channel_id=1, source_target_pairs={{0,32},{8,40},{16,48},{24,56},{32,0},{40,8},{48,16},{56,24},{64,96... | collective-permute-start | bytes 393224 | tf_op jit(solution)/shard_map/ppermute | solution.py:10
  14.5 3.0 %collective-permute-done.2 = f32[128,256]{1,0:T(8,128)S(1)} collective-permute-done((f32[128,256]{1,0:T(8,128)S(1)}, f32[128,256]{1,0:T(8,128)S(1)}, u32[]{:S(2)}, u32[]{:S(2)}) %collective-permute-start.2) | collective-permute-done | bytes 131104 | tf_op jit(solution)/shard_map/ppermute | solution.py:10
  17.5 3.4 %collective-permute-start.3 = (f32[128,256]{1,0:T(8,128)S(1)}, f32[128,256]{1,0:T(8,128)S(1)}, u32[]{:S(2)}, u32[]{:S(2)}) collective-permute-start(f32[128,256]{1,0:T(8,128)S(1)} %add.65), channel_id=1, source_target_pairs={{0,64},{8,72},{16,80},{24,88},{32,96},{40,104},{48,112},{56,120},{... | collective-permute-start | bytes 393224 | tf_op jit(solution)/shard_map/ppermute | solution.py:10
  20.9 3.1 %collective-permute-done.3 = f32[128,256]{1,0:T(8,128)S(1)} collective-permute-done((f32[128,256]{1,0:T(8,128)S(1)}, f32[128,256]{1,0:T(8,128)S(1)}, u32[]{:S(2)}, u32[]{:S(2)}) %collective-permute-start.3) | collective-permute-done | bytes 131104 | tf_op jit(solution)/shard_map/ppermute | solution.py:10
  24.1 1.3 %collective-permute-done.4 = f32[128,256]{1,0:T(8,128)S(1)} collective-permute-done((f32[128,256]{1,0:T(8,128)S(1)}, f32[128,256]{1,0:T(8,128)S(1)}, u32[]{:S(2)}, u32[]{:S(2)}) %collective-permute-start.4) | collective-permute-done | bytes 131104 | tf_op jit(solution)/shard_map/ppermute | solution.py:10
  25.5 0.4 fusion.12
  25.9 0.5 %fusion.2 = f32[1536]{0:T(1024)S(1)} fusion(f32[1536,256]{0,1:T(8,128)S(1)} %fusion.12, f32[768,256]{0,1:T(8,128)S(1)} %get-tuple-element.4, f32[768,256]{0,1:T(8,128)S(1)} %get-tuple-element.3, f32[128,256]{1,0:T(8,128)S(1)} %get-tuple-element.8, f32[128,256]{1,0:T(8,128)S(1)} %get-tuple-element.7, bf16[768,256]{0,1:T(8,128)(2,1)S(1)} %get-tuple-element.6, ...), kind=kOutput, calls=%fused_computation.6 | convolution fusion | flops 204732928 | bytes 4200448 | tf_op jit(solution)/shard_map/dot_general | solution.py:19
  26.4 3.3 %collective-permute-start.5 = (f32[768]{0:T(1024)S(1)}, f32[768]{0:T(1024)S(1)}, u32[]{:S(2)}, u32[]{:S(2)}) collective-permute-start(f32[768]{0:T(1024)S(1)} %fusion.17), channel_id=1, source_target_pairs={{0,1},{1,0},{2,3},{3,2},{4,5},{5,4},{6,7},{7,6},{8,9},{9,8},{10,11... | collective-permute-start | bytes 9224 | tf_op jit(solution)/shard_map/ppermute | solution.py:10
  29.7 1.9 %collective-permute-done.5 = f32[768]{0:T(1024)S(1)} collective-permute-done((f32[768]{0:T(1024)S(1)}, f32[768]{0:T(1024)S(1)}, u32[]{:S(2)}, u32[]{:S(2)}) %collective-permute-start.5) | collective-permute-done | bytes 3104 | tf_op jit(solution)/shard_map/ppermute | solution.py:10
  31.6 1.5 %collective-permute-start.6 = (f32[768]{0:T(1024)S(1)}, f32[768]{0:T(1024)S(1)}, u32[]{:S(2)}, u32[]{:S(2)}) collective-permute-start(f32[768]{0:T(1024)S(1)} %add.71), channel_id=1, source_target_pairs={{0,2},{1,3},{2,0},{3,1},{4,6},{5,7},{6,4},{7,5},{8,10},{9,11},{10,... | collective-permute-start | bytes 9224 | tf_op jit(solution)/shard_map/ppermute | solution.py:10
  33.1 2.1 %collective-permute-done.6 = f32[768]{0:T(1024)S(1)} collective-permute-done((f32[768]{0:T(1024)S(1)}, f32[768]{0:T(1024)S(1)}, u32[]{:S(2)}, u32[]{:S(2)}) %collective-permute-start.6) | collective-permute-done | bytes 3104 | tf_op jit(solution)/shard_map/ppermute | solution.py:10
  35.2 3.0 %collective-permute-start.7 = (f32[768]{0:T(1024)S(1)}, f32[768]{0:T(1024)S(1)}, u32[]{:S(2)}, u32[]{:S(2)}) collective-permute-start(f32[768]{0:T(1024)S(1)} %add.72), channel_id=1, source_target_pairs={{0,4},{1,5},{2,6},{3,7},{4,0},{5,1},{6,2},{7,3},{8,12},{9,13},{10,... | collective-permute-start | bytes 9224 | tf_op jit(solution)/shard_map/ppermute | solution.py:10
  38.2 0.6 %broadcast_in_dim.8 = f32[1,768]{1,0:T(1,128)} reshape(f32[768]{0:T(1024)S(1)} %fusion.17) | data formatting | bytes 6144 | tf_op jit(solution)/shard_map/broadcast_in_dim | solution.py:62
  38.8 1.5 %collective-permute-done.7 = f32[768]{0:T(1024)S(1)} collective-permute-done((f32[768]{0:T(1024)S(1)}, f32[768]{0:T(1024)S(1)}, u32[]{:S(2)}, u32[]{:S(2)}) %collective-permute-start.7) | collective-permute-done | bytes 3104 | tf_op jit(solution)/shard_map/ppermute | solution.py:10
  40.3 0.6 %add.73 = f32[768]{0:T(1024)} add(f32[768]{0:T(1024)S(1)} %add.72, f32[768]{0:T(1024)S(1)} %collective-permute-done.7) | non-fusion elementwise | flops 768 | bytes 9216 | tf_op jit(solution)/shard_map/add | solution.py:61
  (22 shorter events, 0.6 us)
Async XLA Ops:
  2.1 0.7 %copy-start.1 = (bf16[1,768]{1,0:T(2,128)(2,1)S(1)}, bf16[1,768]{1,0:T(2,128)(2,1)}, u32[]{:S(2)}) copy-start(bf16[1,768]{1,0:T(2,128)(2,1)} %param.4) | copy-start | bytes 4612
  2.1 0.8 %copy-start = (f32[1,16,512]{2,1,0:T(8,128)S(1)}, f32[1,16,512]{2,1,0:T(8,128)}, u32[]{:S(2)}) copy-start(f32[1,16,512]{2,1,0:T(8,128)} %param.5) | copy-start | bytes 98308
  5.0 1.4 %collective-permute-start = (f32[128,256]{1,0:T(8,128)S(1)}, f32[128,256]{1,0:T(8,128)S(1)}, u32[]{:S(2)}, u32[]{:S(2)}) collective-permute-start(f32[128,256]{1,0:T(8,128)S(1)} %constant_dynamic-slice_fusion), channel_id=1, source_target_pairs={{0,8},{8,0},{16,24},{24,16},{32,40},{40,32},{48,56},{56,48},{64,72... | collective-permute-start | bytes 393224 | tf_op jit(solution)/shard_map/ppermute | solution.py:10
  6.5 5.8 %collective-permute-start.1 = (f32[128,256]{1,0:T(8,128)S(1)}, f32[128,256]{1,0:T(8,128)S(1)}, u32[]{:S(2)}, u32[]{:S(2)}) collective-permute-start(f32[128,256]{1,0:T(8,128)S(1)} %dynamic-slice_add_fusion), channel_id=1, source_target_pairs={{0,16},{8,24},{16,0},{24,8},{32,48},{40,56},{48,32},{56,40},{64,80... | collective-permute-start | bytes 393224 | tf_op jit(solution)/shard_map/ppermute | solution.py:10
  12.3 5.1 %collective-permute-start.2 = (f32[128,256]{1,0:T(8,128)S(1)}, f32[128,256]{1,0:T(8,128)S(1)}, u32[]{:S(2)}, u32[]{:S(2)}) collective-permute-start(f32[128,256]{1,0:T(8,128)S(1)} %add.64), channel_id=1, source_target_pairs={{0,32},{8,40},{16,48},{24,56},{32,0},{40,8},{48,16},{56,24},{64,96... | collective-permute-start | bytes 393224 | tf_op jit(solution)/shard_map/ppermute | solution.py:10
  17.5 6.6 %collective-permute-start.3 = (f32[128,256]{1,0:T(8,128)S(1)}, f32[128,256]{1,0:T(8,128)S(1)}, u32[]{:S(2)}, u32[]{:S(2)}) collective-permute-start(f32[128,256]{1,0:T(8,128)S(1)} %add.65), channel_id=1, source_target_pairs={{0,64},{8,72},{16,80},{24,88},{32,96},{40,104},{48,112},{56,120},{... | collective-permute-start | bytes 393224 | tf_op jit(solution)/shard_map/ppermute | solution.py:10
  24.0 1.4 %collective-permute-start.4 = (f32[128,256]{1,0:T(8,128)S(1)}, f32[128,256]{1,0:T(8,128)S(1)}, u32[]{:S(2)}, u32[]{:S(2)}) collective-permute-start(f32[128,256]{1,0:T(8,128)S(1)} %add.66), channel_id=1, source_target_pairs={{0,8},{8,0},{16,24},{24,16},{32,40},{40,32},{48,56},{56,48},{64,72... | collective-permute-start | bytes 393224 | tf_op jit(solution)/shard_map/ppermute | solution.py:10
  26.4 5.2 %collective-permute-start.5 = (f32[768]{0:T(1024)S(1)}, f32[768]{0:T(1024)S(1)}, u32[]{:S(2)}, u32[]{:S(2)}) collective-permute-start(f32[768]{0:T(1024)S(1)} %fusion.17), channel_id=1, source_target_pairs={{0,1},{1,0},{2,3},{3,2},{4,5},{5,4},{6,7},{7,6},{8,9},{9,8},{10,11... | collective-permute-start | bytes 9224 | tf_op jit(solution)/shard_map/ppermute | solution.py:10
  31.6 3.6 %collective-permute-start.6 = (f32[768]{0:T(1024)S(1)}, f32[768]{0:T(1024)S(1)}, u32[]{:S(2)}, u32[]{:S(2)}) collective-permute-start(f32[768]{0:T(1024)S(1)} %add.71), channel_id=1, source_target_pairs={{0,2},{1,3},{2,0},{3,1},{4,6},{5,7},{6,4},{7,5},{8,10},{9,11},{10,... | collective-permute-start | bytes 9224 | tf_op jit(solution)/shard_map/ppermute | solution.py:10
  35.2 5.1 %collective-permute-start.7 = (f32[768]{0:T(1024)S(1)}, f32[768]{0:T(1024)S(1)}, u32[]{:S(2)}, u32[]{:S(2)}) collective-permute-start(f32[768]{0:T(1024)S(1)} %add.72), channel_id=1, source_target_pairs={{0,4},{1,5},{2,6},{3,7},{4,0},{5,1},{6,2},{7,3},{8,12},{9,13},{10,... | collective-permute-start | bytes 9224 | tf_op jit(solution)/shard_map/ppermute | solution.py:10

commit v2 on v0

v2 whole, which is shorter than its diff:
```python
import functools

import jax
import jax.numpy as jnp
from jax import lax
from jax.experimental import pallas as pl
from jax.experimental.pallas import tpu as pltpu
from jax.sharding import PartitionSpec as P

CHANNELS = 256
HALF = CHANNELS // 2
CHUNK = 256
ORDER = ((0, 1, 3), (1, 3, 0))
VMEM = pl.BlockSpec(memory_space=pltpu.VMEM)
ANY = pl.BlockSpec(memory_space=pl.ANY)


def wide(*shape):
    return jax.ShapeDtypeStruct(shape, jnp.float32)


def call(kernel, out_shape, operands, scratch=(), flops=1 << 28, spec=VMEM, room=24):
    return pl.pallas_call(
        kernel,
        out_shape=out_shape,
        in_specs=[spec] * len(operands),
        out_specs=jax.tree.map(lambda _: VMEM, out_shape),
        scratch_shapes=list(scratch),
        compiler_params=pltpu.CompilerParams(vmem_limit_bytes=room << 20),
        cost_estimate=pl.CostEstimate(flops=flops, bytes_accessed=1 << 20, transcendentals=0),
    )(*operands)


def parts(value):
    high = value.astype(jnp.bfloat16)
    low = (value - high.astype(jnp.float32)).astype(jnp.bfloat16)
    return jnp.concatenate([high, low], axis=0)


def dot(left, right, contract):
    dims = (((1,), (contract,)), ((), ()))
    return lax.dot_general(left, right, dims, preferred_element_type=jnp.float32)


def folded(both):
    rows = both.shape[0] // 2
    return both[:rows] + both[rows:]


def place(index):
    return lax.rem(index + lax.div(index, 2) + lax.div(index, 4), 2)


def products(steering, values, first, rows):
    real = steering[rows, pl.ds(first, HALF)].T.astype(jnp.float32)
    imag = steering[rows, pl.ds(CHANNELS + first, HALF)].T.astype(jnp.float32)
    total = dot(parts((real - imag) * values), steering[rows, :CHANNELS], 0)
    return total + dot(parts((real + imag) * values), steering[rows, CHANNELS:], 0)


def cross_half(spectra, placed, half, own, out):
    count = spectra.shape[0]
    first = pl.multiple_of(half * HALF, HALF)
    row = pl.multiple_of(lax.axis_index("band") * count, count)
    cross_real, cross_imag = spectra[:, :CHANNELS], spectra[:, CHANNELS:]
    placed[...] = jnp.zeros_like(placed)
    placed[pl.ds(row, count), :] = (cross_real + cross_imag) * 0.5
    out[...] = placed[:, pl.ds(first, HALF)].T - own

    @pl.when(lax.div(row, HALF) == half)
    def _():
        here = pl.ds(pl.multiple_of(row - first, count), count)
        out[here, :] = out[here, :] + (cross_real - cross_imag) * 0.5


def first_kernel(steering_far, estimates_far, spectra_far, out, steering, estimates, spectra, placed, sems):
    starts = range(0, steering.shape[0], CHUNK)
    loads = [
        pltpu.make_async_copy(estimates_far, estimates, sems.at[0]),
        pltpu.make_async_copy(spectra_far, spectra, sems.at[1]),
    ]
    chunks = [
        pltpu.make_async_copy(steering_far.at[pl.ds(s, CHUNK)], steering.at[pl.ds(s, CHUNK)], sems.at[2 + n])
        for n, s in enumerate(starts)
    ]
    loads[0].start()
    for chunk in chunks:
        chunk.start()
    loads[1].start()
    half = 1 - place(lax.axis_index("band"))
    first = pl.multiple_of(half * HALF, HALF)
    loads[0].wait()
    own = jnp.zeros((2 * HALF, CHANNELS), jnp.float32)
    for s, chunk in zip(starts, chunks):
        chunk.wait()
        values = estimates[:, s : s + CHUNK].astype(jnp.float32)
        own = own + products(steering, values, first, slice(s, s + CHUNK))
    loads[1].wait()
    cross_half(spectra, placed, half, folded(own), out)


def second_kernel(steering, estimates, spectra, out, placed):
    half = place(lax.axis_index("band"))
    values = estimates[...].astype(jnp.float32)
    own = products(steering, values, pl.multiple_of(half * HALF, HALF), slice(None))
    cross_half(spectra, placed, half, folded(own), out)


def ready_kernel(steering, minus, plus, power):
    real = steering[:, :CHANNELS].T.astype(jnp.float32)
    imag = steering[:, CHANNELS:].T.astype(jnp.float32)
    minus[...] = real - imag
    plus[...] = real + imag
    power[...] = jnp.sum(real * real + imag * imag, axis=0, keepdims=True)


def form_kernel(mine, other, steering, estimates, minus, plus, power, updated, again, packed):
    half = place(lax.axis_index("band"))
    packed[pl.ds(pl.multiple_of(half * HALF, HALF), HALF), :] = mine[...]
    packed[pl.ds(pl.multiple_of((1 - half) * HALF, HALF), HALF), :] = other[...]
    pieces = parts(packed[...])
    scale = 1.0 / (CHANNELS * CHANNELS)
    for s in range(0, steering.shape[0], CHUNK):
        here = slice(s, s + CHUNK)
        form = folded(dot(pieces, steering[here, :CHANNELS], 1)) * minus[:, here]
        form = form + folded(dot(pieces, steering[here, CHANNELS:], 1)) * plus[:, here]
        form = jnp.sum(form, axis=0, keepdims=True)
        diag = power[:, here] * power[:, here] * scale
        result = jnp.maximum(estimates[:, here].astype(jnp.float32) + form * scale / diag, 0.0)
        updated[:, here] = result
        again[:, here] = result


def partner(index, step):
    z, y, core = index // 4, index // 2 % 2, index % 2
    kind = ORDER[(z + y + core) % 2][step]
    z, y = (z, 1 - y) if kind == 0 else (z ^ kind, y)
    return (z * 2 + y) * 2 + 1 - core


def body(steering, estimates, spectra):
    points = steering.shape[1]
    steering, spectra = steering[0], spectra[0]
    scratch = [pltpu.VMEM((CHANNELS, CHANNELS), jnp.float32)]
    count = points // CHUNK
    send, steering, estimates, spectra = call(
        first_kernel,
        (wide(HALF, CHANNELS), *(jax.ShapeDtypeStruct(a.shape, a.dtype) for a in (steering, estimates, spectra))),
        tuple(pltpu.with_memory_space_constraint(a, pltpu.HBM) for a in (steering, estimates, spectra)),
        scratch + [pltpu.SemaphoreType.DMA((2 + count,))],
        spec=ANY,
        room=24,
    )
    keep = call(second_kernel, wide(HALF, CHANNELS), (steering, estimates, spectra), scratch)
    twins = [(i, i ^ 1) for i in range(16)]
    total = keep + lax.ppermute(send, "band", twins)
    later, total = lax.optimization_barrier((steering, total))
    flat = wide(CHANNELS, points)
    ready = call(ready_kernel, (flat, flat, wide(1, points)), (later,))
    for step in range(3):
        total = total + lax.ppermute(total, "band", [(i, partner(i, step)) for i in range(16)])
        if step == 0:
            total, ready = lax.optimization_barrier((total, ready))
    other = lax.ppermute(total, "band", twins)
    updated, broadband = call(
        form_kernel, (wide(1, points),) * 2, (total, other, steering, estimates, *ready), scratch
    )

    def across(value, bit):
        return lax.ppermute(value, "blk", [(i, i ^ bit) for i in range(8)])

    for bit in (1, 2, 6):
        broadband = broadband + across(broadband, bit)
    return updated, broadband[0]


def solution(mesh):
    return jax.shard_map(
        body,
        mesh=mesh,
        in_specs=(P("blk", "band", None), P("blk", "band"), P("blk", "band", None)),
        out_specs=(P("blk", "band"), P("band")),
        check_vma=False,
    )
```

time: 194 us -> 36.9 us (0.19)
  matrix products: 76.8 us -> 0 us
  blocking collectives: 69.5 us -> 0 us
  starting transfers between devices: 0.04 us -> 15.3 us
  waiting for transfers between devices: 30.8 us -> 16.1 us
  between operations: 14.1 us -> 0.68 us
  Pallas kernels: 0 us -> 4.03 us
    dot_general x5 -> x0, matrix products: 76.8 us -> none  [the longest x1 29.5 us: body(): jnp.einsum('bgh,bh->bg', tile, values.astype(jnp.float32), precision=lax....]
    all_gather x2 -> x0, blocking collectives: 45.1 us -> none  [the longest x1 23.5 us: body(): piece = lax.all_gather(spectra, 'band', axis=1, tiled=True)]
    all_gather x1 -> x0, waiting for transfers between devices: 30.1 us -> none  [body(): blocks = lax.all_gather(steering, 'band', axis=1, tiled=True)]
    psum x1 -> x0, blocking collectives: 24.4 us -> none  [body(): broadband = lax.psum(jnp.sum(updated, axis=0), 'blk')]
    ppermute x0 -> x8, waiting for transfers between devices: none -> 16.1 us  [the longest x3 7.91 us: body(): lax.ppermute(total, 'band', [(i, partner(i, step)) for i in range(16)])]
    ppermute x0 -> x8, starting transfers between devices: none -> 15.3 us  [the longest x3 7.55 us: body(): lax.ppermute(total, 'band', [(i, partner(i, step)) for i in range(16)])]
    pallas_call x0 -> x4, Pallas kernels: none -> 4.03 us  [call(): pl.pallas_call(kernel, out_shape=out_shape, in_specs=[spec] * len(operand...]
  transfers between devices with their start and end apart: 1 -> 8, of which waited for: 1 -> 8; matrix products, arithmetic and copies ran while one was open for 3% -> 0% of each run, Pallas kernels for 0% -> 2%
where the time goes in v2:
time: 36.9 us; the launch traced here: 36.7 us
  waiting for transfers between devices  16.1 us (44%)
  starting transfers between devices  15.3 us (41%)
  Pallas kernels  4.03 us (11%)
  other arithmetic  0.68 us (2%)
  between operations  0.68 us (2%)
    ppermute x3, waiting for transfers between devices, body(): lax.ppermute(total, 'band', [(i, partner(i, step)) for i in range(16)])  7.91 us
    ppermute x3, starting transfers between devices, body(): lax.ppermute(total, 'band', [(i, partner(i, step)) for i in range(16)])  7.55 us
    ppermute x3, starting transfers between devices, across(): return lax.ppermute(value, 'blk', [(i, i ^ bit) for i in range(8)])  7.45 us
    ppermute x3, waiting for transfers between devices, across(): return lax.ppermute(value, 'blk', [(i, i ^ bit) for i in range(8)])  6.05 us
    pallas_call x4, Pallas kernels, call(): pl.pallas_call(kernel, out_shape=out_shape, in_specs=[spec] * len(operand...  4.03 us
    ppermute x1, waiting for transfers between devices, body(): other = lax.ppermute(total, 'band', twins)  1.23 us
    ppermute x1, waiting for transfers between devices, body(): total = keep + lax.ppermute(send, 'band', twins)  0.87 us
  transfers between devices with their start and end apart: 8, of which 8 were waited for; matrix products, arithmetic and copies ran while one was open for 0% of the time, Pallas kernels for 2%

profile of v2, /device:TPU:0, one launch (start us, length us, event | category | flops | bytes accessed | tf_op | source)
XLA Modules:
  0.0 36.7 jit_solution(18015453247875123738)
XLA Ops:
  0.6 2.0 %shard_map.50 = (f32[128,256]{1,0:T(8,128)S(1)}, bf16[768,512]{1,0:T(8,128)(2,1)S(1)}, bf16[1,768]{1,0:T(2,128)(2,1)S(1)}, f32[16,512]{1,0:T(8,128)S(1)}) custom-call(bf16[768,512]{1,0:T(8,128)(2,1)} %bitcast.2, bf16[1,768]{1,0:T(2,128)(2,1)} %estimates_far.1, f32[16,512]{1,0:T(8,128)} %bitcast.3), custom_call_target="tpu_custom_call" | custom-call | flops 268435456 | bytes 1048576 | tf_op jit(solution)/shard_map/pallas_call | solution.py:23
  2.6 0.1 collective-permute-start
  2.7 0.5 %shard_map.51 = f32[128,256]{1,0:T(8,128)S(1)} custom-call(bf16[768,512]{1,0:T(8,128)(2,1)S(1)} %get-tuple-element.22.steering, bf16[1,768]{1,0:T(2,128)(2,1)S(1)} %get-tuple-element.18.estimates, f32[16,512]{1,0:T(8,128)S(1)} %get-tuple-element.19.spectra), custom_call_target="tpu_custom_call" | custom-call | flops 268435456 | bytes 1048576 | tf_op jit(solution)/shard_map/pallas_call | solution.py:23
  3.2 0.9 %collective-permute-done = f32[128,256]{1,0:T(8,128)S(1)} collective-permute-done((f32[128,256]{1,0:T(8,128)S(1)}, f32[128,256]{1,0:T(8,128)S(1)}, u32[]{:S(2)}, u32[]{:S(2)}) %collective-permute-start) | collective-permute-done | bytes 131104 | tf_op jit(solution)/shard_map/ppermute | solution.py:156
  4.1 1.5 %collective-permute-start.1 = (f32[128,256]{1,0:T(8,128)S(1)}, f32[128,256]{1,0:T(8,128)S(1)}, u32[]{:S(2)}, u32[]{:S(2)}) collective-permute-start(f32[128,256]{1,0:T(8,128)S(1)} %add.21), channel_id=1, source_target_pairs={{0,24},{8,32},{16,56},{24,0},{32,8},{40,48},{48,40},{56,16},{64,88... | collective-permute-start | bytes 393224 | tf_op jit(solution)/shard_map/ppermute | solution.py:161
  5.5 0.4 %shard_map.52 = (f32[256,768]{1,0:T(8,128)S(1)}, f32[256,768]{1,0:T(8,128)S(1)}, f32[1,768]{1,0:T(1,128)S(1)}) custom-call(bf16[768,512]{1,0:T(8,128)(2,1)S(1)} %get-tuple-element.22.steering), custom_call_target="tpu_custom_call" | custom-call | flops 268435456 | bytes 1048576 | tf_op jit(solution)/shard_map/pallas_call | solution.py:23
  5.9 2.6 %collective-permute-done.1 = f32[128,256]{1,0:T(8,128)S(1)} collective-permute-done((f32[128,256]{1,0:T(8,128)S(1)}, f32[128,256]{1,0:T(8,128)S(1)}, u32[]{:S(2)}, u32[]{:S(2)}) %collective-permute-start.1) | collective-permute-done | bytes 131104 | tf_op jit(solution)/shard_map/ppermute | solution.py:161
  8.6 1.8 %collective-permute-start.2 = (f32[128,256]{1,0:T(8,128)S(1)}, f32[128,256]{1,0:T(8,128)S(1)}, u32[]{:S(2)}, u32[]{:S(2)}) collective-permute-start(f32[128,256]{1,0:T(8,128)S(1)} %add.22), channel_id=1, source_target_pairs={{0,40},{8,96},{16,120},{24,48},{32,72},{40,0},{48,24},{56,80},{64,... | collective-permute-start | bytes 393224 | tf_op jit(solution)/shard_map/ppermute | solution.py:161
  10.4 2.7 %collective-permute-done.2 = f32[128,256]{1,0:T(8,128)S(1)} collective-permute-done((f32[128,256]{1,0:T(8,128)S(1)}, f32[128,256]{1,0:T(8,128)S(1)}, u32[]{:S(2)}, u32[]{:S(2)}) %collective-permute-start.2) | collective-permute-done | bytes 131104 | tf_op jit(solution)/shard_map/ppermute | solution.py:161
  13.1 4.2 %collective-permute-start.3 = (f32[128,256]{1,0:T(8,128)S(1)}, f32[128,256]{1,0:T(8,128)S(1)}, u32[]{:S(2)}, u32[]{:S(2)}) collective-permute-start(f32[128,256]{1,0:T(8,128)S(1)} %add.23), channel_id=1, source_target_pairs={{0,104},{8,16},{16,8},{24,112},{32,56},{40,64},{48,88},{56,32},{64... | collective-permute-start | bytes 393224 | tf_op jit(solution)/shard_map/ppermute | solution.py:161
  17.3 2.7 %collective-permute-done.3 = f32[128,256]{1,0:T(8,128)S(1)} collective-permute-done((f32[128,256]{1,0:T(8,128)S(1)}, f32[128,256]{1,0:T(8,128)S(1)}, u32[]{:S(2)}, u32[]{:S(2)}) %collective-permute-start.3) | collective-permute-done | bytes 131104 | tf_op jit(solution)/shard_map/ppermute | solution.py:161
  20.0 0.2 collective-permute-start.4
  20.2 1.2 %collective-permute-done.4.other = f32[128,256]{1,0:T(8,128)S(1)} collective-permute-done((f32[128,256]{1,0:T(8,128)S(1)}, f32[128,256]{1,0:T(8,128)S(1)}, u32[]{:S(2)}, u32[]{:S(2)}) %collective-permute-start.4) | collective-permute-done | bytes 131104 | tf_op jit(solution)/shard_map/ppermute | solution.py:164
  21.4 1.2 %shard_map.53 = (f32[1,768]{1,0:T(1,128)}, f32[1,768]{1,0:T(1,128)S(1)}) custom-call(f32[128,256]{1,0:T(8,128)S(1)} %add.24.mine, f32[128,256]{1,0:T(8,128)S(1)} %collective-permute-done.4.other, bf16[768,512]{1,0:T(8,128)(2,1)S(1)} %get-tuple-element.22.steering, bf16[1,768]{1,0:T(2,128)(2,1)S(1)} %get-tuple-element.18.estimates, ...), custom_call_target="tpu_custom_call" | custom-call | flops 268435456 | bytes 1048576 | tf_op jit(solution)/shard_map/pallas_call | solution.py:23
  22.6 3.2 %collective-permute-start.5 = (f32[1,768]{1,0:T(1,128)S(1)}, f32[1,768]{1,0:T(1,128)S(1)}, u32[]{:S(2)}, u32[]{:S(2)}) collective-permute-start(f32[1,768]{1,0:T(1,128)S(1)} %get-tuple-element.31), channel_id=1, source_target_pairs={{0,1},{1,0},{2,3},{3,2},{4,5},{5,4},{6,7},{7,6},{8,9},{9,8},{10,11... | collective-permute-start | bytes 9224 | tf_op jit(solution)/shard_map/ppermute | solution.py:170
  25.8 1.9 %collective-permute-done.5 = f32[1,768]{1,0:T(1,128)S(1)} collective-permute-done((f32[1,768]{1,0:T(1,128)S(1)}, f32[1,768]{1,0:T(1,128)S(1)}, u32[]{:S(2)}, u32[]{:S(2)}) %collective-permute-start.5) | collective-permute-done | bytes 3104 | tf_op jit(solution)/shard_map/ppermute | solution.py:170
  27.7 1.5 %collective-permute-start.6 = (f32[1,768]{1,0:T(1,128)S(1)}, f32[1,768]{1,0:T(1,128)S(1)}, u32[]{:S(2)}, u32[]{:S(2)}) collective-permute-start(f32[1,768]{1,0:T(1,128)S(1)} %add.25), channel_id=1, source_target_pairs={{0,2},{1,3},{2,0},{3,1},{4,6},{5,7},{6,4},{7,5},{8,10},{9,11},{10,... | collective-permute-start | bytes 9224 | tf_op jit(solution)/shard_map/ppermute | solution.py:170
  29.2 2.1 %collective-permute-done.6 = f32[1,768]{1,0:T(1,128)S(1)} collective-permute-done((f32[1,768]{1,0:T(1,128)S(1)}, f32[1,768]{1,0:T(1,128)S(1)}, u32[]{:S(2)}, u32[]{:S(2)}) %collective-permute-start.6) | collective-permute-done | bytes 3104 | tf_op jit(solution)/shard_map/ppermute | solution.py:170
  31.3 2.8 %collective-permute-start.7 = (f32[1,768]{1,0:T(1,128)S(1)}, f32[1,768]{1,0:T(1,128)S(1)}, u32[]{:S(2)}, u32[]{:S(2)}) collective-permute-start(f32[1,768]{1,0:T(1,128)S(1)} %add.26), channel_id=1, source_target_pairs={{0,6},{1,7},{2,4},{3,5},{4,2},{5,3},{6,0},{7,1},{8,14},{9,15},{10,... | collective-permute-start | bytes 9224 | tf_op jit(solution)/shard_map/ppermute | solution.py:170
  34.1 2.0 %collective-permute-done.7 = f32[1,768]{1,0:T(1,128)S(1)} collective-permute-done((f32[1,768]{1,0:T(1,128)S(1)}, f32[1,768]{1,0:T(1,128)S(1)}, u32[]{:S(2)}, u32[]{:S(2)}) %collective-permute-start.7) | collective-permute-done | bytes 3104 | tf_op jit(solution)/shard_map/ppermute | solution.py:170
  36.1 0.6 %add_reduce_fusion = f32[768]{0:T(1024)} fusion(f32[1,768]{1,0:T(1,128)S(1)} %add.26, f32[1,768]{1,0:T(1,128)S(1)} %collective-permute-done.7), kind=kLoop, calls=%fused_computation | loop fusion | flops 768 | bytes 9216 | tf_op jit(solution)/shard_map/add | solution.py:173
  (6 shorter events, 0.1 us)
Async XLA Ops:
  2.6 1.4 %collective-permute-start = (f32[128,256]{1,0:T(8,128)S(1)}, f32[128,256]{1,0:T(8,128)S(1)}, u32[]{:S(2)}, u32[]{:S(2)}) collective-permute-start(f32[128,256]{1,0:T(8,128)S(1)} %get-tuple-element.20), channel_id=1, source_target_pairs={{0,8},{8,0},{16,24},{24,16},{32,40},{40,32},{48,56},{56,48},{64,72... | collective-permute-start | bytes 393224 | tf_op jit(solution)/shard_map/ppermute | solution.py:156
  4.1 4.5 %collective-permute-start.1 = (f32[128,256]{1,0:T(8,128)S(1)}, f32[128,256]{1,0:T(8,128)S(1)}, u32[]{:S(2)}, u32[]{:S(2)}) collective-permute-start(f32[128,256]{1,0:T(8,128)S(1)} %add.21), channel_id=1, source_target_pairs={{0,24},{8,32},{16,56},{24,0},{32,8},{40,48},{48,40},{56,16},{64,88... | collective-permute-start | bytes 393224 | tf_op jit(solution)/shard_map/ppermute | solution.py:161
  8.6 4.5 %collective-permute-start.2 = (f32[128,256]{1,0:T(8,128)S(1)}, f32[128,256]{1,0:T(8,128)S(1)}, u32[]{:S(2)}, u32[]{:S(2)}) collective-permute-start(f32[128,256]{1,0:T(8,128)S(1)} %add.22), channel_id=1, source_target_pairs={{0,40},{8,96},{16,120},{24,48},{32,72},{40,0},{48,24},{56,80},{64,... | collective-permute-start | bytes 393224 | tf_op jit(solution)/shard_map/ppermute | solution.py:161
  13.1 6.9 %collective-permute-start.3 = (f32[128,256]{1,0:T(8,128)S(1)}, f32[128,256]{1,0:T(8,128)S(1)}, u32[]{:S(2)}, u32[]{:S(2)}) collective-permute-start(f32[128,256]{1,0:T(8,128)S(1)} %add.23), channel_id=1, source_target_pairs={{0,104},{8,16},{16,8},{24,112},{32,56},{40,64},{48,88},{56,32},{64... | collective-permute-start | bytes 393224 | tf_op jit(solution)/shard_map/ppermute | solution.py:161
  20.0 1.4 %collective-permute-start.4 = (f32[128,256]{1,0:T(8,128)S(1)}, f32[128,256]{1,0:T(8,128)S(1)}, u32[]{:S(2)}, u32[]{:S(2)}) collective-permute-start(f32[128,256]{1,0:T(8,128)S(1)} %add.24.mine), channel_id=1, source_target_pairs={{0,8},{8,0},{16,24},{24,16},{32,40},{40,32},{48,56},{56,48},{64,72... | collective-permute-start | bytes 393224 | tf_op jit(solution)/shard_map/ppermute | solution.py:164
  22.6 5.1 %collective-permute-start.5 = (f32[1,768]{1,0:T(1,128)S(1)}, f32[1,768]{1,0:T(1,128)S(1)}, u32[]{:S(2)}, u32[]{:S(2)}) collective-permute-start(f32[1,768]{1,0:T(1,128)S(1)} %get-tuple-element.31), channel_id=1, source_target_pairs={{0,1},{1,0},{2,3},{3,2},{4,5},{5,4},{6,7},{7,6},{8,9},{9,8},{10,11... | collective-permute-start | bytes 9224 | tf_op jit(solution)/shard_map/ppermute | solution.py:170
  27.7 3.6 %collective-permute-start.6 = (f32[1,768]{1,0:T(1,128)S(1)}, f32[1,768]{1,0:T(1,128)S(1)}, u32[]{:S(2)}, u32[]{:S(2)}) collective-permute-start(f32[1,768]{1,0:T(1,128)S(1)} %add.25), channel_id=1, source_target_pairs={{0,2},{1,3},{2,0},{3,1},{4,6},{5,7},{6,4},{7,5},{8,10},{9,11},{10,... | collective-permute-start | bytes 9224 | tf_op jit(solution)/shard_map/ppermute | solution.py:170
  31.3 4.8 %collective-permute-start.7 = (f32[1,768]{1,0:T(1,128)S(1)}, f32[1,768]{1,0:T(1,128)S(1)}, u32[]{:S(2)}, u32[]{:S(2)}) collective-permute-start(f32[1,768]{1,0:T(1,128)S(1)} %add.26), channel_id=1, source_target_pairs={{0,6},{1,7},{2,4},{3,5},{4,2},{5,3},{6,0},{7,1},{8,14},{9,15},{10,... | collective-permute-start | bytes 9224 | tf_op jit(solution)/shard_map/ppermute | solution.py:170

commit v3 on v2

--- a/solution.py
+++ b/solution.py
@@ -10,7 +10,9 @@
 CHANNELS = 256
 HALF = CHANNELS // 2
 CHUNK = 256
-ORDER = ((0, 1, 3), (1, 3, 0))
+FIRST = 768
+LANES = 128
+ORDER = ((0, 3, 1), (3, 1, 0))
 VMEM = pl.BlockSpec(memory_space=pltpu.VMEM)
 ANY = pl.BlockSpec(memory_space=pl.ANY)
 
@@ -58,14 +60,14 @@
     return total + dot(parts((real + imag) * values), steering[rows, CHANNELS:], 0)
 
 
-def cross_half(spectra, placed, half, own, out):
+def cross_half(spectra, placed, half, out):
     count = spectra.shape[0]
     first = pl.multiple_of(half * HALF, HALF)
     row = pl.multiple_of(lax.axis_index("band") * count, count)
     cross_real, cross_imag = spectra[:, :CHANNELS], spectra[:, CHANNELS:]
     placed[...] = jnp.zeros_like(placed)
     placed[pl.ds(row, count), :] = (cross_real + cross_imag) * 0.5
-    out[...] = placed[:, pl.ds(first, HALF)].T - own
+    out[...] = placed[:, pl.ds(first, HALF)].T
 
     @pl.when(lax.div(row, HALF) == half)
     def _():
@@ -74,36 +76,36 @@
 
 
 def first_kernel(steering_far, estimates_far, spectra_far, out, steering, estimates, spectra, placed, sems):
-    starts = range(0, steering.shape[0], CHUNK)
+    starts = range(0, steering.shape[0], FIRST)
     loads = [
         pltpu.make_async_copy(estimates_far, estimates, sems.at[0]),
         pltpu.make_async_copy(spectra_far, spectra, sems.at[1]),
     ]
     chunks = [
-        pltpu.make_async_copy(steering_far.at[pl.ds(s, CHUNK)], steering.at[pl.ds(s, CHUNK)], sems.at[2 + n])
+        pltpu.make_async_copy(steering_far.at[pl.ds(s, FIRST)], steering.at[pl.ds(s, FIRST)], sems.at[2 + n])
         for n, s in enumerate(starts)
     ]
-    loads[0].start()
-    for chunk in chunks:
-        chunk.start()
-    loads[1].start()
+    for load in loads + chunks:
+        load.start()
     half = 1 - place(lax.axis_index("band"))
     first = pl.multiple_of(half * HALF, HALF)
+    loads[1].wait()
+    cross_half(spectra, placed, half, out)
     loads[0].wait()
     own = jnp.zeros((2 * HALF, CHANNELS), jnp.float32)
     for s, chunk in zip(starts, chunks):
         chunk.wait()
-        values = estimates[:, s : s + CHUNK].astype(jnp.float32)
-        own = own + products(steering, values, first, slice(s, s + CHUNK))
-    loads[1].wait()
-    cross_half(spectra, placed, half, folded(own), out)
+        values = estimates[:, s : s + FIRST].astype(jnp.float32)
+        own = own + products(steering, values, first, slice(s, s + FIRST))
+    out[...] = out[...] - folded(own)
 
 
 def second_kernel(steering, estimates, spectra, out, placed):
     half = place(lax.axis_index("band"))
     values = estimates[...].astype(jnp.float32)
     own = products(steering, values, pl.multiple_of(half * HALF, HALF), slice(None))
-    cross_half(spectra, placed, half, folded(own), out)
+    cross_half(spectra, placed, half, out)
+    out[...] = out[...] - folded(own)
 
 
 def ready_kernel(steering, minus, plus, power):
@@ -114,21 +116,32 @@
     power[...] = jnp.sum(real * real + imag * imag, axis=0, keepdims=True)
 
 
-def form_kernel(mine, other, steering, estimates, minus, plus, power, updated, again, packed):
+def form(total, half, steering, minus, plus, here):
+    pieces = parts(total)
+    rows = pl.ds(pl.multiple_of(half * HALF, HALF), HALF)
+    terms = folded(dot(pieces, steering[here, :CHANNELS], 1)) * minus[rows, here]
+    terms = terms + folded(dot(pieces, steering[here, CHANNELS:], 1)) * plus[rows, here]
+    return jnp.sum(terms, axis=0, keepdims=True)
+
+
+def near_kernel(mine, steering, minus, plus, partial):
     half = place(lax.axis_index("band"))
-    packed[pl.ds(pl.multiple_of(half * HALF, HALF), HALF), :] = mine[...]
-    packed[pl.ds(pl.multiple_of((1 - half) * HALF, HALF), HALF), :] = other[...]
-    pieces = parts(packed[...])
+    for s in range(0, steering.shape[0], CHUNK):
+        here = slice(s, s + CHUNK)
+        partial[:, here] = form(mine[...], half, steering, minus, plus, here)
+
+
+def far_kernel(other, partial, steering, estimates, minus, plus, power, updated):
+    half = 1 - place(lax.axis_index("band"))
     scale = 1.0 / (CHANNELS * CHANNELS)
     for s in range(0, steering.shape[0], CHUNK):
         here = slice(s, s + CHUNK)
-        form = folded(dot(pieces, steering[here, :CHANNELS], 1)) * minus[:, here]
-        form = form + folded(dot(pieces, steering[here, CHANNELS:], 1)) * plus[:, here]
-        form = jnp.sum(form, axis=0, keepdims=True)
+        whole = partial[:, here] + form(other[...], half, steering, minus, plus, here)
         diag = power[:, here] * power[:, here] * scale
-        result = jnp.maximum(estimates[:, here].astype(jnp.float32) + form * scale / diag, 0.0)
-        updated[:, here] = result
-        again[:, here] = result
+        result = jnp.maximum(estimates[:, here].astype(jnp.float32) + whole * scale / diag, 0.0)
+        for t in range(0, CHUNK, LANES):
+            line = (s + t) // LANES
+            updated[line : line + 1, :] = result[:, t : t + LANES]
 
 
 def partner(index, step):
@@ -142,7 +155,7 @@
     points = steering.shape[1]
     steering, spectra = steering[0], spectra[0]
     scratch = [pltpu.VMEM((CHANNELS, CHANNELS), jnp.float32)]
-    count = points // CHUNK
+    count = points // FIRST
     send, steering, estimates, spectra = call(
         first_kernel,
         (wide(HALF, CHANNELS), *(jax.ShapeDtypeStruct(a.shape, a.dtype) for a in (steering, estimates, spectra))),
@@ -162,16 +175,16 @@
         if step == 0:
             total, ready = lax.optimization_barrier((total, ready))
     other = lax.ppermute(total, "band", twins)
-    updated, broadband = call(
-        form_kernel, (wide(1, points),) * 2, (total, other, steering, estimates, *ready), scratch
-    )
+    partial = call(near_kernel, wide(1, points), (total, steering, *ready[:2]))
+    updated = call(far_kernel, wide(points // LANES, LANES), (other, partial, steering, estimates, *ready))
+    broadband = updated
 
     def across(value, bit):
         return lax.ppermute(value, "blk", [(i, i ^ bit) for i in range(8)])
 
     for bit in (1, 2, 6):
         broadband = broadband + across(broadband, bit)
-    return updated, broadband[0]
+    return updated.reshape(1, points), broadband.reshape(points)
 
 
 def solution(mesh):

time: 36.9 us -> 35.8 us (0.970)
  starting transfers between devices: 15.3 us -> 13.6 us
  Pallas kernels: 4.03 us -> 3.31 us
  waiting for transfers between devices: 16.1 us -> 16.8 us
  local copies, waits for them, and re-layouts: 0 us -> 0.58 us
    ppermute x3, waiting for transfers between devices: 7.91 us -> 9.65 us  [body(): lax.ppermute(total, 'band', [(i, partner(i, step)) for i in range(16)])]
    ppermute x3, starting transfers between devices: 7.55 us -> 5.82 us  [body(): lax.ppermute(total, 'band', [(i, partner(i, step)) for i in range(16)])]
    pallas_call x4 -> x5, Pallas kernels: 4.03 us -> 3.31 us  [call(): pl.pallas_call(kernel, out_shape=out_shape, in_specs=[spec] * len(operand...]
    add x3 -> x2, other arithmetic: 0.62 us -> 0.01 us  [body(): broadband = broadband + across(broadband, bit)]
    reshape x0 -> x1, other arithmetic: none -> 0.6 us  [body(): return (updated.reshape(1, points), broadband.reshape(points))]
    unnamed x0 -> x1, local copies, waits for them, and re-layouts: none -> 0.58 us
    ppermute x3, waiting for transfers between devices: 6.05 us -> 5.52 us  [across(): return lax.ppermute(value, 'blk', [(i, i ^ bit) for i in range(8)])]
    ppermute x1, waiting for transfers between devices: 1.23 us -> 0.81 us  [body(): other = lax.ppermute(total, 'band', twins)]
  transfers between devices with their start and end apart: 8 -> 8, of which waited for: 8 -> 8; matrix products, arithmetic and copies ran while one was open for 0% -> 2% of each run, Pallas kernels for 2% -> 4%
where the time goes in v3:
time: 35.8 us; the launch traced here: 35.7 us
  waiting for transfers between devices  16.8 us (47%)
  starting transfers between devices  13.6 us (38%)
  Pallas kernels  3.31 us (9%)
  between operations  0.69 us (2%)
  other arithmetic  0.67 us (2%)
  local copies, waits for them, and re-layouts  0.58 us (2%)
    ppermute x3, waiting for transfers between devices, body(): lax.ppermute(total, 'band', [(i, partner(i, step)) for i in range(16)])  9.65 us
    ppermute x3, starting transfers between devices, across(): return lax.ppermute(value, 'blk', [(i, i ^ bit) for i in range(8)])  7.51 us
    ppermute x3, starting transfers between devices, body(): lax.ppermute(total, 'band', [(i, partner(i, step)) for i in range(16)])  5.82 us
    ppermute x3, waiting for transfers between devices, across(): return lax.ppermute(value, 'blk', [(i, i ^ bit) for i in range(8)])  5.52 us
    pallas_call x5, Pallas kernels, call(): pl.pallas_call(kernel, out_shape=out_shape, in_specs=[spec] * len(operand...  3.31 us
    ppermute x1, waiting for transfers between devices, body(): total = keep + lax.ppermute(send, 'band', twins)  0.85 us
    ppermute x1, waiting for transfers between devices, body(): other = lax.ppermute(total, 'band', twins)  0.81 us
  transfers between devices with their start and end apart: 8, of which 8 were waited for; matrix products, arithmetic and copies ran while one was open for 2% of the time, Pallas kernels for 4%

profile of v3, /device:TPU:0, one launch (start us, length us, event | category | flops | bytes accessed | tf_op | source)
XLA Modules:
  0.0 35.7 jit_solution(3346601847212868172)
XLA Ops:
  0.6 1.6 %shard_map.50 = (f32[128,256]{1,0:T(8,128)S(1)}, bf16[768,512]{1,0:T(8,128)(2,1)S(1)}, bf16[1,768]{1,0:T(2,128)(2,1)S(1)}, f32[16,512]{1,0:T(8,128)S(1)}) custom-call(bf16[768,512]{1,0:T(8,128)(2,1)} %bitcast.11, bf16[1,768]{1,0:T(2,128)(2,1)} %estimates_far.1, f32[16,512]{1,0:T(8,128)} %bitcast.12), custom_call_target="tpu_custom_call" | custom-call | flops 268435456 | bytes 1048576 | tf_op jit(solution)/shard_map/pallas_call | solution.py:25
  2.3 0.1 collective-permute-start
  2.4 0.5 %shard_map.51 = f32[128,256]{1,0:T(8,128)S(1)} custom-call(bf16[768,512]{1,0:T(8,128)(2,1)S(1)} %get-tuple-element.20.steering, bf16[1,768]{1,0:T(2,128)(2,1)S(1)} %get-tuple-element.16.estimates, f32[16,512]{1,0:T(8,128)S(1)} %get-tuple-element.17.spectra), custom_call_target="tpu_custom_call" | custom-call | flops 268435456 | bytes 1048576 | tf_op jit(solution)/shard_map/pallas_call | solution.py:25
  2.8 0.8 %collective-permute-done = f32[128,256]{1,0:T(8,128)S(1)} collective-permute-done((f32[128,256]{1,0:T(8,128)S(1)}, f32[128,256]{1,0:T(8,128)S(1)}, u32[]{:S(2)}, u32[]{:S(2)}) %collective-permute-start) | collective-permute-done | bytes 131104 | tf_op jit(solution)/shard_map/ppermute | solution.py:169
  3.7 1.5 %collective-permute-start.1 = (f32[128,256]{1,0:T(8,128)S(1)}, f32[128,256]{1,0:T(8,128)S(1)}, u32[]{:S(2)}, u32[]{:S(2)}) collective-permute-start(f32[128,256]{1,0:T(8,128)S(1)} %add.21), channel_id=1, source_target_pairs={{0,24},{8,96},{16,120},{24,0},{32,72},{40,48},{48,40},{56,80},{64,... | collective-permute-start | bytes 393224 | tf_op jit(solution)/shard_map/ppermute | solution.py:174
  5.2 0.4 %shard_map.52 = (f32[256,768]{1,0:T(8,128)S(1)}, f32[256,768]{1,0:T(8,128)S(1)}, f32[1,768]{1,0:T(1,128)S(1)}) custom-call(bf16[768,512]{1,0:T(8,128)(2,1)S(1)} %get-tuple-element.20.steering), custom_call_target="tpu_custom_call" | custom-call | flops 268435456 | bytes 1048576 | tf_op jit(solution)/shard_map/pallas_call | solution.py:25
  5.6 2.6 %collective-permute-done.1 = f32[128,256]{1,0:T(8,128)S(1)} collective-permute-done((f32[128,256]{1,0:T(8,128)S(1)}, f32[128,256]{1,0:T(8,128)S(1)}, u32[]{:S(2)}, u32[]{:S(2)}) %collective-permute-start.1) | collective-permute-done | bytes 131104 | tf_op jit(solution)/shard_map/ppermute | solution.py:174
  8.2 4.2 %collective-permute-start.2 = (f32[128,256]{1,0:T(8,128)S(1)}, f32[128,256]{1,0:T(8,128)S(1)}, u32[]{:S(2)}, u32[]{:S(2)}) collective-permute-start(f32[128,256]{1,0:T(8,128)S(1)} %add.22), channel_id=1, source_target_pairs={{0,104},{8,32},{16,56},{24,112},{32,8},{40,64},{48,88},{56,16},{64... | collective-permute-start | bytes 393224 | tf_op jit(solution)/shard_map/ppermute | solution.py:174
  12.5 2.7 %collective-permute-done.2 = f32[128,256]{1,0:T(8,128)S(1)} collective-permute-done((f32[128,256]{1,0:T(8,128)S(1)}, f32[128,256]{1,0:T(8,128)S(1)}, u32[]{:S(2)}, u32[]{:S(2)}) %collective-permute-start.2) | collective-permute-done | bytes 131104 | tf_op jit(solution)/shard_map/ppermute | solution.py:174
  15.1 0.1 collective-permute-start.3
  15.2 4.4 %collective-permute-done.3 = f32[128,256]{1,0:T(8,128)S(1)} collective-permute-done((f32[128,256]{1,0:T(8,128)S(1)}, f32[128,256]{1,0:T(8,128)S(1)}, u32[]{:S(2)}, u32[]{:S(2)}) %collective-permute-start.3) | collective-permute-done | bytes 131104 | tf_op jit(solution)/shard_map/ppermute | solution.py:174
  19.6 0.2 collective-permute-start.4
  19.8 0.4 %shard_map.53.partial = f32[1,768]{1,0:T(1,128)S(1)} custom-call(f32[128,256]{1,0:T(8,128)S(1)} %add.24.mine, bf16[768,512]{1,0:T(8,128)(2,1)S(1)} %get-tuple-element.20.steering, f32[256,768]{1,0:T(8,128)S(1)} %get-tuple-element.25.minus, f32[256,768]{1,0:T(8,128)S(1)} %get-tuple-element.26.plus), custom_call_target="tpu_custom_call" | custom-call | flops 268435456 | bytes 1048576 | tf_op jit(solution)/shard_map/pallas_call | solution.py:25
  20.2 0.8 %collective-permute-done.4.other = f32[128,256]{1,0:T(8,128)S(1)} collective-permute-done((f32[128,256]{1,0:T(8,128)S(1)}, f32[128,256]{1,0:T(8,128)S(1)}, u32[]{:S(2)}, u32[]{:S(2)}) %collective-permute-start.4) | collective-permute-done | bytes 131104 | tf_op jit(solution)/shard_map/ppermute | solution.py:177
  21.1 0.4 %shard_map.54 = f32[6,128]{1,0:T(8,128)S(1)} custom-call(f32[128,256]{1,0:T(8,128)S(1)} %collective-permute-done.4.other, f32[1,768]{1,0:T(1,128)S(1)} %shard_map.53.partial, bf16[768,512]{1,0:T(8,128)(2,1)S(1)} %get-tuple-element.20.steering, bf16[1,768]{1,0:T(2,128)(2,1)S(1)} %get-tuple-element.16.estimates, f32[256,768]{1,0:T(8,128)S(1)} %get-tuple-element.25.minus, ...), custom_call_target="tpu_custom_call" | custom-call | flops 268435456 | bytes 1048576 | tf_op jit(solution)/shard_map/pallas_call | solution.py:25
  21.5 3.3 %collective-permute-start.5 = (f32[6,128]{1,0:T(8,128)S(1)}, f32[6,128]{1,0:T(8,128)S(1)}, u32[]{:S(2)}, u32[]{:S(2)}) collective-permute-start(f32[6,128]{1,0:T(8,128)S(1)} %shard_map.54), channel_id=1, source_target_pairs={{0,1},{1,0},{2,3},{3,2},{4,5},{5,4},{6,7},{7,6},{8,9},{9,8},{10,11... | collective-permute-start | bytes 9224 | tf_op jit(solution)/shard_map/ppermute | solution.py:183
  24.8 1.9 %collective-permute-done.5 = f32[6,128]{1,0:T(8,128)S(1)} collective-permute-done((f32[6,128]{1,0:T(8,128)S(1)}, f32[6,128]{1,0:T(8,128)S(1)}, u32[]{:S(2)}, u32[]{:S(2)}) %collective-permute-start.5) | collective-permute-done | bytes 3104 | tf_op jit(solution)/shard_map/ppermute | solution.py:183
  26.7 1.5 %collective-permute-start.6 = (f32[6,128]{1,0:T(8,128)S(1)}, f32[6,128]{1,0:T(8,128)S(1)}, u32[]{:S(2)}, u32[]{:S(2)}) collective-permute-start(f32[6,128]{1,0:T(8,128)S(1)} %add.25), channel_id=1, source_target_pairs={{0,2},{1,3},{2,0},{3,1},{4,6},{5,7},{6,4},{7,5},{8,10},{9,11},{10,... | collective-permute-start | bytes 9224 | tf_op jit(solution)/shard_map/ppermute | solution.py:183
  28.2 2.1 %collective-permute-done.6 = f32[6,128]{1,0:T(8,128)S(1)} collective-permute-done((f32[6,128]{1,0:T(8,128)S(1)}, f32[6,128]{1,0:T(8,128)S(1)}, u32[]{:S(2)}, u32[]{:S(2)}) %collective-permute-start.6) | collective-permute-done | bytes 3104 | tf_op jit(solution)/shard_map/ppermute | solution.py:183
  30.3 2.8 %collective-permute-start.7 = (f32[6,128]{1,0:T(8,128)S(1)}, f32[6,128]{1,0:T(8,128)S(1)}, u32[]{:S(2)}, u32[]{:S(2)}) collective-permute-start(f32[6,128]{1,0:T(8,128)S(1)} %add.26), channel_id=1, source_target_pairs={{0,6},{1,7},{2,4},{3,5},{4,2},{5,3},{6,0},{7,1},{8,14},{9,15},{10,... | collective-permute-start | bytes 9224 | tf_op jit(solution)/shard_map/ppermute | solution.py:183
  33.0 0.6 %copy.7 = f32[1,1,6,128]{3,1,2,0:T(1,128)} copy(f32[1,1,6,128]{3,2,1,0:T(8,128)S(1)} %bitcast.9) | data formatting | bytes 6144
  33.6 1.5 %collective-permute-done.7 = f32[6,128]{1,0:T(8,128)S(1)} collective-permute-done((f32[6,128]{1,0:T(8,128)S(1)}, f32[6,128]{1,0:T(8,128)S(1)}, u32[]{:S(2)}, u32[]{:S(2)}) %collective-permute-start.7) | collective-permute-done | bytes 3104 | tf_op jit(solution)/shard_map/ppermute | solution.py:183
  35.1 0.6 %add_bitcast_fusion = f32[768]{0:T(1024)} fusion(f32[6,128]{1,0:T(8,128)S(1)} %add.26, f32[6,128]{1,0:T(8,128)S(1)} %collective-permute-done.7), kind=kLoop, calls=%fused_computation | loop fusion | flops 768 | bytes 9216 | tf_op jit(solution)/shard_map/reshape | solution.py:187
  (6 shorter events, 0.1 us)
Async XLA Ops:
  2.3 1.4 %collective-permute-start = (f32[128,256]{1,0:T(8,128)S(1)}, f32[128,256]{1,0:T(8,128)S(1)}, u32[]{:S(2)}, u32[]{:S(2)}) collective-permute-start(f32[128,256]{1,0:T(8,128)S(1)} %get-tuple-element.18), channel_id=1, source_target_pairs={{0,8},{8,0},{16,24},{24,16},{32,40},{40,32},{48,56},{56,48},{64,72... | collective-permute-start | bytes 393224 | tf_op jit(solution)/shard_map/ppermute | solution.py:169
  3.7 4.5 %collective-permute-start.1 = (f32[128,256]{1,0:T(8,128)S(1)}, f32[128,256]{1,0:T(8,128)S(1)}, u32[]{:S(2)}, u32[]{:S(2)}) collective-permute-start(f32[128,256]{1,0:T(8,128)S(1)} %add.21), channel_id=1, source_target_pairs={{0,24},{8,96},{16,120},{24,0},{32,72},{40,48},{48,40},{56,80},{64,... | collective-permute-start | bytes 393224 | tf_op jit(solution)/shard_map/ppermute | solution.py:174
  8.2 6.9 %collective-permute-start.2 = (f32[128,256]{1,0:T(8,128)S(1)}, f32[128,256]{1,0:T(8,128)S(1)}, u32[]{:S(2)}, u32[]{:S(2)}) collective-permute-start(f32[128,256]{1,0:T(8,128)S(1)} %add.22), channel_id=1, source_target_pairs={{0,104},{8,32},{16,56},{24,112},{32,8},{40,64},{48,88},{56,16},{64... | collective-permute-start | bytes 393224 | tf_op jit(solution)/shard_map/ppermute | solution.py:174
  15.1 4.5 %collective-permute-start.3 = (f32[128,256]{1,0:T(8,128)S(1)}, f32[128,256]{1,0:T(8,128)S(1)}, u32[]{:S(2)}, u32[]{:S(2)}) collective-permute-start(f32[128,256]{1,0:T(8,128)S(1)} %add.23), channel_id=1, source_target_pairs={{0,40},{8,16},{16,8},{24,48},{32,56},{40,0},{48,24},{56,32},{64,10... | collective-permute-start | bytes 393224 | tf_op jit(solution)/shard_map/ppermute | solution.py:174
  19.6 1.4 %collective-permute-start.4 = (f32[128,256]{1,0:T(8,128)S(1)}, f32[128,256]{1,0:T(8,128)S(1)}, u32[]{:S(2)}, u32[]{:S(2)}) collective-permute-start(f32[128,256]{1,0:T(8,128)S(1)} %add.24.mine), channel_id=1, source_target_pairs={{0,8},{8,0},{16,24},{24,16},{32,40},{40,32},{48,56},{56,48},{64,72... | collective-permute-start | bytes 393224 | tf_op jit(solution)/shard_map/ppermute | solution.py:177
  21.5 5.2 %collective-permute-start.5 = (f32[6,128]{1,0:T(8,128)S(1)}, f32[6,128]{1,0:T(8,128)S(1)}, u32[]{:S(2)}, u32[]{:S(2)}) collective-permute-start(f32[6,128]{1,0:T(8,128)S(1)} %shard_map.54), channel_id=1, source_target_pairs={{0,1},{1,0},{2,3},{3,2},{4,5},{5,4},{6,7},{7,6},{8,9},{9,8},{10,11... | collective-permute-start | bytes 9224 | tf_op jit(solution)/shard_map/ppermute | solution.py:183
  26.7 3.6 %collective-permute-start.6 = (f32[6,128]{1,0:T(8,128)S(1)}, f32[6,128]{1,0:T(8,128)S(1)}, u32[]{:S(2)}, u32[]{:S(2)}) collective-permute-start(f32[6,128]{1,0:T(8,128)S(1)} %add.25), channel_id=1, source_target_pairs={{0,2},{1,3},{2,0},{3,1},{4,6},{5,7},{6,4},{7,5},{8,10},{9,11},{10,... | collective-permute-start | bytes 9224 | tf_op jit(solution)/shard_map/ppermute | solution.py:183
  30.3 4.8 %collective-permute-start.7 = (f32[6,128]{1,0:T(8,128)S(1)}, f32[6,128]{1,0:T(8,128)S(1)}, u32[]{:S(2)}, u32[]{:S(2)}) collective-permute-start(f32[6,128]{1,0:T(8,128)S(1)} %add.26), channel_id=1, source_target_pairs={{0,6},{1,7},{2,4},{3,5},{4,2},{5,3},{6,0},{7,1},{8,14},{9,15},{10,... | collective-permute-start | bytes 9224 | tf_op jit(solution)/shard_map/ppermute | solution.py:183

commit v4 on v3

--- a/solution.py
+++ b/solution.py
@@ -12,6 +12,9 @@
 CHUNK = 256
 FIRST = 768
 LANES = 128
+TAIL = 16
+FLIPPED = (1, 2)
+SUBLANES = 8
 ORDER = ((0, 3, 1), (3, 1, 0))
 VMEM = pl.BlockSpec(memory_space=pltpu.VMEM)
 ANY = pl.BlockSpec(memory_space=pl.ANY)
@@ -76,44 +79,46 @@
 
 
 def first_kernel(steering_far, estimates_far, spectra_far, out, steering, estimates, spectra, placed, sems):
-    starts = range(0, steering.shape[0], FIRST)
+    points = steering_far.shape[0]
+    whole = steering.at[pl.ds(0, points)]
     loads = [
         pltpu.make_async_copy(estimates_far, estimates, sems.at[0]),
         pltpu.make_async_copy(spectra_far, spectra, sems.at[1]),
+        pltpu.make_async_copy(steering_far, whole, sems.at[2]),
     ]
-    chunks = [
-        pltpu.make_async_copy(steering_far.at[pl.ds(s, FIRST)], steering.at[pl.ds(s, FIRST)], sems.at[2 + n])
-        for n, s in enumerate(starts)
-    ]
-    for load in loads + chunks:
+    for load in loads:
         load.start()
     half = 1 - place(lax.axis_index("band"))
-    first = pl.multiple_of(half * HALF, HALF)
     loads[1].wait()
     cross_half(spectra, placed, half, out)
     loads[0].wait()
-    own = jnp.zeros((2 * HALF, CHANNELS), jnp.float32)
-    for s, chunk in zip(starts, chunks):
-        chunk.wait()
-        values = estimates[:, s : s + FIRST].astype(jnp.float32)
-        own = own + products(steering, values, first, slice(s, s + FIRST))
+    values = estimates[...].astype(jnp.float32)
+    line = lax.broadcasted_iota(jnp.int32, (TAIL, 2 * CHANNELS), 0)
+    rest = jnp.zeros((1, 4 * CHANNELS - points), jnp.float32)
+    back = jnp.concatenate([values[:, 2 * CHANNELS :], rest], axis=1)
+    tail = jnp.where(line == 0, values[:, : 2 * CHANNELS], jnp.where(line == 1, back, 0.0))
+    steering[pl.ds(points, TAIL), :] = tail.astype(steering.dtype)
+    loads[2].wait()
+    own = products(steering, values, pl.multiple_of(half * HALF, HALF), slice(0, points))
     out[...] = out[...] - folded(own)
 
 
 def second_kernel(steering, estimates, spectra, out, placed):
     half = place(lax.axis_index("band"))
     values = estimates[...].astype(jnp.float32)
-    own = products(steering, values, pl.multiple_of(half * HALF, HALF), slice(None))
+    own = products(steering, values, pl.multiple_of(half * HALF, HALF), slice(0, estimates.shape[1]))
     cross_half(spectra, placed, half, out)
     out[...] = out[...] - folded(own)
 
 
-def ready_kernel(steering, minus, plus, power):
-    real = steering[:, :CHANNELS].T.astype(jnp.float32)
-    imag = steering[:, CHANNELS:].T.astype(jnp.float32)
-    minus[...] = real - imag
-    plus[...] = real + imag
-    power[...] = jnp.sum(real * real + imag * imag, axis=0, keepdims=True)
+def ready_kernel(steering, twin_steering, *outs):
+    for rows, (minus, plus, power) in ((steering, outs[:3]), (twin_steering, outs[3:])):
+        points = minus.shape[1]
+        real = rows[:points, :CHANNELS].T.astype(jnp.float32)
+        imag = rows[:points, CHANNELS:].T.astype(jnp.float32)
+        minus[...] = real - imag
+        plus[...] = real + imag
+        power[...] = jnp.sum(real * real + imag * imag, axis=0, keepdims=True)
 
 
 def form(total, half, steering, minus, plus, here):
@@ -124,24 +129,32 @@
     return jnp.sum(terms, axis=0, keepdims=True)
 
 
-def near_kernel(mine, steering, minus, plus, partial):
+def near_kernel(mine, *refs):
+    partial = refs[-1]
     half = place(lax.axis_index("band"))
-    for s in range(0, steering.shape[0], CHUNK):
-        here = slice(s, s + CHUNK)
-        partial[:, here] = form(mine[...], half, steering, minus, plus, here)
-
-
-def far_kernel(other, partial, steering, estimates, minus, plus, power, updated):
+    for side, (steering, minus, plus) in enumerate((refs[:3], refs[3:6])):
+        for s in range(0, minus.shape[1], CHUNK):
+            here = slice(s, s + CHUNK)
+            partial[side : side + 1, here] = form(mine[...], half, steering, minus, plus, here)
+
+
+def far_kernel(other, partial, *refs):
+    updated = refs[-1]
+    updated[...] = jnp.zeros_like(updated)
     half = 1 - place(lax.axis_index("band"))
     scale = 1.0 / (CHANNELS * CHANNELS)
-    for s in range(0, steering.shape[0], CHUNK):
-        here = slice(s, s + CHUNK)
-        whole = partial[:, here] + form(other[...], half, steering, minus, plus, here)
-        diag = power[:, here] * power[:, here] * scale
-        result = jnp.maximum(estimates[:, here].astype(jnp.float32) + whole * scale / diag, 0.0)
-        for t in range(0, CHUNK, LANES):
-            line = (s + t) // LANES
-            updated[line : line + 1, :] = result[:, t : t + LANES]
+    for side, (steering, minus, plus, power) in enumerate((refs[:4], refs[4:8])):
+        points = minus.shape[1]
+        tail = steering[points:, :].astype(jnp.float32)
+        estimates = jnp.concatenate([tail[:1], tail[1:2, : points - 2 * CHANNELS]], axis=1)
+        for s in range(0, points, CHUNK):
+            here = slice(s, s + CHUNK)
+            whole = partial[side : side + 1, here] + form(other[...], half, steering, minus, plus, here)
+            diag = power[:, here] * power[:, here] * scale
+            result = jnp.maximum(estimates[:, here] + whole * scale / diag, 0.0)
+            for t in range(0, CHUNK, LANES):
+                line = side * SUBLANES + (s + t) // LANES
+                updated[line : line + 1, :] = result[:, t : t + LANES]
 
 
 def partner(index, step):
@@ -151,40 +164,61 @@
     return (z * 2 + y) * 2 + 1 - core
 
 
+def across(value, bit):
+    flip = int(bit in FLIPPED)
+    pairs = [(b * 8 + k, (b ^ flip) * 8 + (k ^ bit)) for b in range(16) for k in range(8)]
+    moved = lax.ppermute(value, ("band", "blk"), pairs)
+    if flip:
+        moved = jnp.concatenate([moved[SUBLANES:], moved[:SUBLANES]], axis=0)
+    return value + moved
+
+
 def body(steering, estimates, spectra):
     points = steering.shape[1]
     steering, spectra = steering[0], spectra[0]
     scratch = [pltpu.VMEM((CHANNELS, CHANNELS), jnp.float32)]
-    count = points // FIRST
+    operands = tuple(pltpu.with_memory_space_constraint(a, pltpu.HBM) for a in (steering, estimates, spectra))
     send, steering, estimates, spectra = call(
         first_kernel,
-        (wide(HALF, CHANNELS), *(jax.ShapeDtypeStruct(a.shape, a.dtype) for a in (steering, estimates, spectra))),
-        tuple(pltpu.with_memory_space_constraint(a, pltpu.HBM) for a in (steering, estimates, spectra)),
-        scratch + [pltpu.SemaphoreType.DMA((2 + count,))],
+        (
+            wide(HALF, CHANNELS),
+            jax.ShapeDtypeStruct((points + TAIL, 2 * CHANNELS), steering.dtype),
+            jax.ShapeDtypeStruct(estimates.shape, estimates.dtype),
+            wide(*spectra.shape),
+        ),
+        operands,
+        scratch + [pltpu.SemaphoreType.DMA((3,))],
         spec=ANY,
-        room=24,
     )
     keep = call(second_kernel, wide(HALF, CHANNELS), (steering, estimates, spectra), scratch)
     twins = [(i, i ^ 1) for i in range(16)]
     total = keep + lax.ppermute(send, "band", twins)
     later, total = lax.optimization_barrier((steering, total))
+    twin_steering = lax.ppermute(later, "band", twins)
     flat = wide(CHANNELS, points)
-    ready = call(ready_kernel, (flat, flat, wide(1, points)), (later,))
+    shapes = (flat, flat, wide(1, points))
     for step in range(3):
         total = total + lax.ppermute(total, "band", [(i, partner(i, step)) for i in range(16)])
         if step == 0:
+            total, twin_steering = lax.optimization_barrier((total, twin_steering))
+            ready = call(ready_kernel, shapes * 2, (steering, twin_steering))
+        if step == 1:
             total, ready = lax.optimization_barrier((total, ready))
     other = lax.ppermute(total, "band", twins)
-    partial = call(near_kernel, wide(1, points), (total, steering, *ready[:2]))
-    updated = call(far_kernel, wide(points // LANES, LANES), (other, partial, steering, estimates, *ready))
-    broadband = updated
-
-    def across(value, bit):
-        return lax.ppermute(value, "blk", [(i, i ^ bit) for i in range(8)])
-
+    partial = call(
+        near_kernel, wide(2, points), (total, steering, *ready[:2], twin_steering, *ready[3:5])
+    )
+    lines = points // LANES
+    both = call(
+        far_kernel,
+        wide(2 * SUBLANES, LANES),
+        (other, partial, steering, *ready[:3], twin_steering, *ready[3:]),
+    )
+    updated = both[:lines].reshape(1, points)
+    summed = both
     for bit in (1, 2, 6):
-        broadband = broadband + across(broadband, bit)
-    return updated.reshape(1, points), broadband.reshape(points)
+        summed = across(summed, bit)
+    return updated, summed[:lines].reshape(points)
 
 
 def solution(mesh):

time: 35.8 us -> 35.4 us (0.989)
  waiting for transfers between devices: 16.8 us -> 15.6 us
  Pallas kernels: 3.31 us -> 4.03 us
    pallas_call x5, Pallas kernels: 3.31 us -> 4.03 us  [call(): pl.pallas_call(kernel, out_shape=out_shape, in_specs=[spec] * len(operand...]
    ppermute x3 -> x4, waiting for transfers between devices: 5.52 us -> 4.99 us  [the longest x3 4.98 us: across(): moved = lax.ppermute(value, ('band', 'blk'), pairs)]
    ppermute x3, waiting for transfers between devices: 9.65 us -> 9.19 us  [body(): lax.ppermute(total, 'band', [(i, partner(i, step)) for i in range(16)])]
    ppermute x3 -> x4, starting transfers between devices: 7.51 us -> 7.25 us  [the longest x3 7.02 us: across(): moved = lax.ppermute(value, ('band', 'blk'), pairs)]
  transfers between devices with their start and end apart: 8 -> 9, of which waited for: 8 -> 8; matrix products, arithmetic and copies ran while one was open for 2% -> 2% of each run, Pallas kernels for 4% -> 5%
where the time goes in v4:
time: 35.4 us; the launch traced here: 35.3 us
  waiting for transfers between devices  15.6 us (44%)
  starting transfers between devices  13.7 us (39%)
  Pallas kernels  4.03 us (11%)
  between operations  0.7 us (2%)
  other arithmetic  0.68 us (2%)
  local copies, waits for them, and re-layouts  0.59 us (2%)
    ppermute x3, waiting for transfers between devices, body(): lax.ppermute(total, 'band', [(i, partner(i, step)) for i in range(16)])  9.19 us
    ppermute x3, starting transfers between devices, across(): moved = lax.ppermute(value, ('band', 'blk'), pairs)  7.02 us
    ppermute x3, starting transfers between devices, body(): lax.ppermute(total, 'band', [(i, partner(i, step)) for i in range(16)])  6.16 us
    ppermute x3, waiting for transfers between devices, across(): moved = lax.ppermute(value, ('band', 'blk'), pairs)  4.98 us
    pallas_call x5, Pallas kernels, call(): pl.pallas_call(kernel, out_shape=out_shape, in_specs=[spec] * len(operand...  4.03 us
    ppermute x1, waiting for transfers between devices, body(): total = keep + lax.ppermute(send, 'band', twins)  0.85 us
  transfers between devices with their start and end apart: 9, of which 8 were waited for; matrix products, arithmetic and copies ran while one was open for 2% of the time, Pallas kernels for 5%

profile of v4, /device:TPU:0, one launch (start us, length us, event | category | flops | bytes accessed | tf_op | source)
XLA Modules:
  0.0 35.3 jit_solution(5231526965119966838)
XLA Ops:
  0.6 1.6 %shard_map.50 = (f32[128,256]{1,0:T(8,128)S(1)}, bf16[784,512]{1,0:T(8,128)(2,1)S(1)}, bf16[1,768]{1,0:T(2,128)(2,1)S(1)}, f32[16,512]{1,0:T(8,128)S(1)}) custom-call(bf16[768,512]{1,0:T(8,128)(2,1)} %bitcast.11, bf16[1,768]{1,0:T(2,128)(2,1)} %estimates_far.1, f32[16,512]{1,0:T(8,128)} %bitcast.12), custom_call_target="tpu_custom_call" | custom-call | flops 268435456 | bytes 1048576 | tf_op jit(solution)/shard_map/pallas_call | solution.py:28
  2.3 0.1 collective-permute-start
  2.4 0.5 %shard_map.51 = f32[128,256]{1,0:T(8,128)S(1)} custom-call(bf16[784,512]{1,0:T(8,128)(2,1)S(1)} %get-tuple-element.28.steering.refs_0_, bf16[1,768]{1,0:T(2,128)(2,1)S(1)} %get-tuple-element.24.estimates, f32[16,512]{1,0:T(8,128)S(1)} %get-tuple-element.25.spectra), custom_call_target="tpu_custom_call" | custom-call | flops 268435456 | bytes 1048576 | tf_op jit(solution)/shard_map/pallas_call | solution.py:28
  2.9 0.8 %collective-permute-done = f32[128,256]{1,0:T(8,128)S(1)} collective-permute-done((f32[128,256]{1,0:T(8,128)S(1)}, f32[128,256]{1,0:T(8,128)S(1)}, u32[]{:S(2)}, u32[]{:S(2)}) %collective-permute-start) | collective-permute-done | bytes 131104 | tf_op jit(solution)/shard_map/ppermute | solution.py:195
  3.7 0.2 collective-permute-start.2
  4.0 1.6 %collective-permute-start.1 = (f32[128,256]{1,0:T(8,128)S(1)}, f32[128,256]{1,0:T(8,128)S(1)}, u32[]{:S(2)}, u32[]{:S(2)}) collective-permute-start(f32[128,256]{1,0:T(8,128)S(1)} %add.21), channel_id=1, source_target_pairs={{0,24},{8,96},{16,120},{24,0},{32,72},{40,48},{48,40},{56,80},{64,... | collective-permute-start | bytes 393224 | tf_op jit(solution)/shard_map/ppermute | solution.py:201
  5.6 2.8 %collective-permute-done.1 = f32[128,256]{1,0:T(8,128)S(1)} collective-permute-done((f32[128,256]{1,0:T(8,128)S(1)}, f32[128,256]{1,0:T(8,128)S(1)}, u32[]{:S(2)}, u32[]{:S(2)}) %collective-permute-start.1) | collective-permute-done | bytes 131104 | tf_op jit(solution)/shard_map/ppermute | solution.py:201
  8.4 4.5 %collective-permute-start.3 = (f32[128,256]{1,0:T(8,128)S(1)}, f32[128,256]{1,0:T(8,128)S(1)}, u32[]{:S(2)}, u32[]{:S(2)}) collective-permute-start(f32[128,256]{1,0:T(8,128)S(1)} %add.22), channel_id=1, source_target_pairs={{0,104},{8,32},{16,56},{24,112},{32,8},{40,64},{48,88},{56,16},{64... | collective-permute-start | bytes 393224 | tf_op jit(solution)/shard_map/ppermute | solution.py:201
  12.8 0.6 %shard_map.52 = (f32[256,768]{1,0:T(8,128)S(1)}, f32[256,768]{1,0:T(8,128)S(1)}, f32[1,768]{1,0:T(1,128)S(1)}, f32[256,768]{1,0:T(8,128)S(1)}, f32[256,768]{1,0:T(8,128)S(1)}, /*index=5*/f32[1,768]{1,0:T(1,128)S(1)}) custom-call(bf16[784,512]{1,0:T(8,128)(2,1)S(1)} %get-tuple-element.28.steering.refs_0_, ...), custom_call_target="tpu_custom_call" | custom-call | flops 268435456 | bytes 1048576 | tf_op jit(solution)/shard_map/pallas_call | solution.py:28
  13.5 2.0 %collective-permute-done.3 = f32[128,256]{1,0:T(8,128)S(1)} collective-permute-done((f32[128,256]{1,0:T(8,128)S(1)}, f32[128,256]{1,0:T(8,128)S(1)}, u32[]{:S(2)}, u32[]{:S(2)}) %collective-permute-start.3) | collective-permute-done | bytes 131104 | tf_op jit(solution)/shard_map/ppermute | solution.py:201
  15.5 0.1 collective-permute-start.4
  15.6 4.4 %collective-permute-done.4 = f32[128,256]{1,0:T(8,128)S(1)} collective-permute-done((f32[128,256]{1,0:T(8,128)S(1)}, f32[128,256]{1,0:T(8,128)S(1)}, u32[]{:S(2)}, u32[]{:S(2)}) %collective-permute-start.4) | collective-permute-done | bytes 131104 | tf_op jit(solution)/shard_map/ppermute | solution.py:201
  20.0 0.2 collective-permute-start.5
  20.2 0.7 %shard_map.53.partial = f32[2,768]{1,0:T(2,128)S(1)} custom-call(f32[128,256]{1,0:T(8,128)S(1)} %add.24.mine, bf16[784,512]{1,0:T(8,128)(2,1)S(1)} %get-tuple-element.28.steering.refs_0_, f32[256,768]{1,0:T(8,128)S(1)} %get-tuple-element.38.refs_1_, f32[256,768]{1,0:T(8,128)S(1)} %get-tuple-element.39.refs_2_, ...), custom_call_target="tpu_custom_call" | custom-call | flops 268435456 | bytes 1048576 | tf_op jit(solution)/shard_map/pallas_call | solution.py:28
  20.9 0.6 %collective-permute-done.5.other = f32[128,256]{1,0:T(8,128)S(1)} collective-permute-done((f32[128,256]{1,0:T(8,128)S(1)}, f32[128,256]{1,0:T(8,128)S(1)}, u32[]{:S(2)}, u32[]{:S(2)}) %collective-permute-start.5) | collective-permute-done | bytes 131104 | tf_op jit(solution)/shard_map/ppermute | solution.py:207
  21.4 0.6 %shard_map.54 = f32[16,128]{1,0:T(8,128)S(1)} custom-call(f32[128,256]{1,0:T(8,128)S(1)} %collective-permute-done.5.other, f32[2,768]{1,0:T(2,128)S(1)} %shard_map.53.partial, bf16[784,512]{1,0:T(8,128)(2,1)S(1)} %get-tuple-element.28.steering.refs_0_, f32[256,768]{1,0:T(8,128)S(1)} %get-tuple-element.38.refs_1_, f32[256,768]{1,0:T(8,128)S(1)} %get-tuple-element.39.refs_2_, ...), custom_call_target="tpu_custom_call" | custom-call | flops 268435456 | bytes 1048576 | tf_op jit(solution)/shard_map/pallas_call | solution.py:28
  22.1 3.0 %collective-permute-start.6 = (f32[16,128]{1,0:T(8,128)S(1)}, f32[16,128]{1,0:T(8,128)S(1)}, u32[]{:S(2)}, u32[]{:S(2)}) collective-permute-start(f32[16,128]{1,0:T(8,128)S(1)} %shard_map.54), channel_id=1, source_target_pairs={{0,9},{1,8},{2,11},{3,10},{4,13},{5,12},{6,15},{7,14},{8,1},{9,0},... | collective-permute-start | bytes 24584 | tf_op jit(solution)/shard_map/ppermute | solution.py:170
  25.1 1.6 %collective-permute-done.6 = f32[16,128]{1,0:T(8,128)S(1)} collective-permute-done((f32[16,128]{1,0:T(8,128)S(1)}, f32[16,128]{1,0:T(8,128)S(1)}, u32[]{:S(2)}, u32[]{:S(2)}) %collective-permute-start.6) | collective-permute-done | bytes 8224 | tf_op jit(solution)/shard_map/ppermute | solution.py:170
  26.7 1.2 %collective-permute-start.7 = (f32[16,128]{1,0:T(8,128)S(1)}, f32[16,128]{1,0:T(8,128)S(1)}, u32[]{:S(2)}, u32[]{:S(2)}) collective-permute-start(f32[16,128]{1,0:T(8,128)S(1)} %maximum_add_fusion), channel_id=1, source_target_pairs={{0,10},{1,11},{2,8},{3,9},{4,14},{5,15},{6,12},{7,13},{8,2},{9,3},... | collective-permute-start | bytes 24584 | tf_op jit(solution)/shard_map/ppermute | solution.py:170
  28.0 1.8 %collective-permute-done.7 = f32[16,128]{1,0:T(8,128)S(1)} collective-permute-done((f32[16,128]{1,0:T(8,128)S(1)}, f32[16,128]{1,0:T(8,128)S(1)}, u32[]{:S(2)}, u32[]{:S(2)}) %collective-permute-start.7) | collective-permute-done | bytes 8224 | tf_op jit(solution)/shard_map/ppermute | solution.py:170
  29.8 2.8 %collective-permute-start.8 = (f32[16,128]{1,0:T(8,128)S(1)}, f32[16,128]{1,0:T(8,128)S(1)}, u32[]{:S(2)}, u32[]{:S(2)}) collective-permute-start(f32[16,128]{1,0:T(8,128)S(1)} %maximum_add_fusion.1), channel_id=1, source_target_pairs={{0,6},{1,7},{2,4},{3,5},{4,2},{5,3},{6,0},{7,1},{8,14},{9,15},{10,... | collective-permute-start | bytes 24584 | tf_op jit(solution)/shard_map/ppermute | solution.py:170
  32.6 0.6 %copy.7 = f32[1,1,6,128]{3,1,2,0:T(1,128)} copy(f32[1,1,6,128]{3,2,1,0:T(8,128)S(1)} %slice_bitcast_fusion) | data formatting | bytes 6144
  33.2 1.5 %collective-permute-done.8 = f32[16,128]{1,0:T(8,128)S(1)} collective-permute-done((f32[16,128]{1,0:T(8,128)S(1)}, f32[16,128]{1,0:T(8,128)S(1)}, u32[]{:S(2)}, u32[]{:S(2)}) %collective-permute-start.8) | collective-permute-done | bytes 8224 | tf_op jit(solution)/shard_map/ppermute | solution.py:170
  34.7 0.6 %fusion = f32[768]{0:T(1024)} fusion(f32[16,128]{1,0:T(8,128)S(1)} %collective-permute-done.8, f32[16,128]{1,0:T(8,128)S(1)} %maximum_add_fusion.1), kind=kLoop, calls=%fused_computation.3 | loop fusion | flops 768 | bytes 9216 | tf_op jit(solution)/shard_map/reshape | solution.py:221
  (10 shorter events, 0.1 us)
Async XLA Ops:
  2.3 1.4 %collective-permute-start = (f32[128,256]{1,0:T(8,128)S(1)}, f32[128,256]{1,0:T(8,128)S(1)}, u32[]{:S(2)}, u32[]{:S(2)}) collective-permute-start(f32[128,256]{1,0:T(8,128)S(1)} %get-tuple-element.26), channel_id=1, source_target_pairs={{0,8},{8,0},{16,24},{24,16},{32,40},{40,32},{48,56},{56,48},{64,72... | collective-permute-start | bytes 393224 | tf_op jit(solution)/shard_map/ppermute | solution.py:195
  3.7 4.6 %collective-permute-start.2 = (bf16[784,512]{1,0:T(8,128)(2,1)S(1)}, bf16[784,512]{1,0:T(8,128)(2,1)S(1)}, u32[]{:S(2)}, u32[]{:S(2)}) collective-permute-start(bf16[784,512]{1,0:T(8,128)(2,1)S(1)} %get-tuple-element.28.steering.refs_0_), channel_id=1, source_target_pairs={{0,8},{8,0},{16,24},{24,16},{32,40},{40,32},{48,56},{56,48},{64,72... | collective-permute-start | bytes 2408456 | tf_op jit(solution)/shard_map/ppermute | solution.py:197
  4.0 4.4 %collective-permute-start.1 = (f32[128,256]{1,0:T(8,128)S(1)}, f32[128,256]{1,0:T(8,128)S(1)}, u32[]{:S(2)}, u32[]{:S(2)}) collective-permute-start(f32[128,256]{1,0:T(8,128)S(1)} %add.21), channel_id=1, source_target_pairs={{0,24},{8,96},{16,120},{24,0},{32,72},{40,48},{48,40},{56,80},{64,... | collective-permute-start | bytes 393224 | tf_op jit(solution)/shard_map/ppermute | solution.py:201
  8.4 7.1 %collective-permute-start.3 = (f32[128,256]{1,0:T(8,128)S(1)}, f32[128,256]{1,0:T(8,128)S(1)}, u32[]{:S(2)}, u32[]{:S(2)}) collective-permute-start(f32[128,256]{1,0:T(8,128)S(1)} %add.22), channel_id=1, source_target_pairs={{0,104},{8,32},{16,56},{24,112},{32,8},{40,64},{48,88},{56,16},{64... | collective-permute-start | bytes 393224 | tf_op jit(solution)/shard_map/ppermute | solution.py:201
  15.5 4.5 %collective-permute-start.4 = (f32[128,256]{1,0:T(8,128)S(1)}, f32[128,256]{1,0:T(8,128)S(1)}, u32[]{:S(2)}, u32[]{:S(2)}) collective-permute-start(f32[128,256]{1,0:T(8,128)S(1)} %add.23), channel_id=1, source_target_pairs={{0,40},{8,16},{16,8},{24,48},{32,56},{40,0},{48,24},{56,32},{64,10... | collective-permute-start | bytes 393224 | tf_op jit(solution)/shard_map/ppermute | solution.py:201
  20.0 1.4 %collective-permute-start.5 = (f32[128,256]{1,0:T(8,128)S(1)}, f32[128,256]{1,0:T(8,128)S(1)}, u32[]{:S(2)}, u32[]{:S(2)}) collective-permute-start(f32[128,256]{1,0:T(8,128)S(1)} %add.24.mine), channel_id=1, source_target_pairs={{0,8},{8,0},{16,24},{24,16},{32,40},{40,32},{48,56},{56,48},{64,72... | collective-permute-start | bytes 393224 | tf_op jit(solution)/shard_map/ppermute | solution.py:207
  22.1 4.7 %collective-permute-start.6 = (f32[16,128]{1,0:T(8,128)S(1)}, f32[16,128]{1,0:T(8,128)S(1)}, u32[]{:S(2)}, u32[]{:S(2)}) collective-permute-start(f32[16,128]{1,0:T(8,128)S(1)} %shard_map.54), channel_id=1, source_target_pairs={{0,9},{1,8},{2,11},{3,10},{4,13},{5,12},{6,15},{7,14},{8,1},{9,0},... | collective-permute-start | bytes 24584 | tf_op jit(solution)/shard_map/ppermute | solution.py:170
  26.7 3.1 %collective-permute-start.7 = (f32[16,128]{1,0:T(8,128)S(1)}, f32[16,128]{1,0:T(8,128)S(1)}, u32[]{:S(2)}, u32[]{:S(2)}) collective-permute-start(f32[16,128]{1,0:T(8,128)S(1)} %maximum_add_fusion), channel_id=1, source_target_pairs={{0,10},{1,11},{2,8},{3,9},{4,14},{5,15},{6,12},{7,13},{8,2},{9,3},... | collective-permute-start | bytes 24584 | tf_op jit(solution)/shard_map/ppermute | solution.py:170
  29.8 4.9 %collective-permute-start.8 = (f32[16,128]{1,0:T(8,128)S(1)}, f32[16,128]{1,0:T(8,128)S(1)}, u32[]{:S(2)}, u32[]{:S(2)}) collective-permute-start(f32[16,128]{1,0:T(8,128)S(1)} %maximum_add_fusion.1), channel_id=1, source_target_pairs={{0,6},{1,7},{2,4},{3,5},{4,2},{5,3},{6,0},{7,1},{8,14},{9,15},{10,... | collective-permute-start | bytes 24584 | tf_op jit(solution)/shard_map/ppermute | solution.py:170

commit v5 on v4

--- a/solution.py
+++ b/solution.py
@@ -111,50 +111,41 @@
     out[...] = out[...] - folded(own)
 
 
-def ready_kernel(steering, twin_steering, *outs):
-    for rows, (minus, plus, power) in ((steering, outs[:3]), (twin_steering, outs[3:])):
-        points = minus.shape[1]
+def ready_kernel(steering, twin_steering, minus, plus, twin_minus, twin_plus, values, diag):
+    scale = 1.0 / (CHANNELS * CHANNELS)
+    values[...] = jnp.zeros_like(values)
+    diag[...] = jnp.ones_like(diag)
+    sides = ((steering, minus, plus), (twin_steering, twin_minus, twin_plus))
+    for side, (rows, less, more) in enumerate(sides):
+        points = less.shape[1]
         real = rows[:points, :CHANNELS].T.astype(jnp.float32)
         imag = rows[:points, CHANNELS:].T.astype(jnp.float32)
-        minus[...] = real - imag
-        plus[...] = real + imag
-        power[...] = jnp.sum(real * real + imag * imag, axis=0, keepdims=True)
-
-
-def form(total, half, steering, minus, plus, here):
-    pieces = parts(total)
+        less[...] = real - imag
+        more[...] = real + imag
+        power = jnp.sum(real * real + imag * imag, axis=0, keepdims=True)
+        tail = rows[points:, :].astype(jnp.float32)
+        estimates = jnp.concatenate([tail[:1], tail[1:2, : points - 2 * CHANNELS]], axis=1)
+        for t in range(0, points, LANES):
+            line = side * SUBLANES + t // LANES
+            values[line : line + 1, :] = estimates[:, t : t + LANES]
+            diag[line : line + 1, :] = power[:, t : t + LANES] * power[:, t : t + LANES] * scale
+
+
+def form_kernel(mine, steering, minus, plus, twin_steering, twin_minus, twin_plus, partial):
+    half = place(lax.axis_index("band"))
+    pieces = parts(mine[...])
     rows = pl.ds(pl.multiple_of(half * HALF, HALF), HALF)
-    terms = folded(dot(pieces, steering[here, :CHANNELS], 1)) * minus[rows, here]
-    terms = terms + folded(dot(pieces, steering[here, CHANNELS:], 1)) * plus[rows, here]
-    return jnp.sum(terms, axis=0, keepdims=True)
-
-
-def near_kernel(mine, *refs):
-    partial = refs[-1]
-    half = place(lax.axis_index("band"))
-    for side, (steering, minus, plus) in enumerate((refs[:3], refs[3:6])):
-        for s in range(0, minus.shape[1], CHUNK):
+    partial[...] = jnp.zeros_like(partial)
+    sides = ((steering, minus, plus), (twin_steering, twin_minus, twin_plus))
+    for side, (points, less, more) in enumerate(sides):
+        for s in range(0, less.shape[1], CHUNK):
             here = slice(s, s + CHUNK)
-            partial[side : side + 1, here] = form(mine[...], half, steering, minus, plus, here)
-
-
-def far_kernel(other, partial, *refs):
-    updated = refs[-1]
-    updated[...] = jnp.zeros_like(updated)
-    half = 1 - place(lax.axis_index("band"))
-    scale = 1.0 / (CHANNELS * CHANNELS)
-    for side, (steering, minus, plus, power) in enumerate((refs[:4], refs[4:8])):
-        points = minus.shape[1]
-        tail = steering[points:, :].astype(jnp.float32)
-        estimates = jnp.concatenate([tail[:1], tail[1:2, : points - 2 * CHANNELS]], axis=1)
-        for s in range(0, points, CHUNK):
-            here = slice(s, s + CHUNK)
-            whole = partial[side : side + 1, here] + form(other[...], half, steering, minus, plus, here)
-            diag = power[:, here] * power[:, here] * scale
-            result = jnp.maximum(estimates[:, here] + whole * scale / diag, 0.0)
+            terms = folded(dot(pieces, points[here, :CHANNELS], 1)) * less[rows, here]
+            terms = terms + folded(dot(pieces, points[here, CHANNELS:], 1)) * more[rows, here]
+            sums = jnp.sum(terms, axis=0, keepdims=True)
             for t in range(0, CHUNK, LANES):
                 line = side * SUBLANES + (s + t) // LANES
-                updated[line : line + 1, :] = result[:, t : t + LANES]
+                partial[line : line + 1, :] = sums[:, t : t + LANES]
 
 
 def partner(index, step):
@@ -164,13 +155,15 @@
     return (z * 2 + y) * 2 + 1 - core
 
 
+def swapped(value):
+    return jnp.concatenate([value[SUBLANES:], value[:SUBLANES]], axis=0)
+
+
 def across(value, bit):
     flip = int(bit in FLIPPED)
     pairs = [(b * 8 + k, (b ^ flip) * 8 + (k ^ bit)) for b in range(16) for k in range(8)]
     moved = lax.ppermute(value, ("band", "blk"), pairs)
-    if flip:
-        moved = jnp.concatenate([moved[SUBLANES:], moved[:SUBLANES]], axis=0)
-    return value + moved
+    return value + (swapped(moved) if flip else moved)
 
 
 def body(steering, estimates, spectra):
@@ -196,24 +189,19 @@
     later, total = lax.optimization_barrier((steering, total))
     twin_steering = lax.ppermute(later, "band", twins)
     flat = wide(CHANNELS, points)
-    shapes = (flat, flat, wide(1, points))
+    lined = wide(2 * SUBLANES, LANES)
     for step in range(3):
         total = total + lax.ppermute(total, "band", [(i, partner(i, step)) for i in range(16)])
         if step == 0:
             total, twin_steering = lax.optimization_barrier((total, twin_steering))
-            ready = call(ready_kernel, shapes * 2, (steering, twin_steering))
+            ready = call(ready_kernel, (flat,) * 4 + (lined,) * 2, (steering, twin_steering))
         if step == 1:
             total, ready = lax.optimization_barrier((total, ready))
-    other = lax.ppermute(total, "band", twins)
-    partial = call(
-        near_kernel, wide(2, points), (total, steering, *ready[:2], twin_steering, *ready[3:5])
-    )
+    minus, plus, twin_minus, twin_plus, values, diag = ready
+    partial = call(form_kernel, lined, (total, steering, minus, plus, twin_steering, twin_minus, twin_plus))
+    forms = partial + swapped(lax.ppermute(partial, "band", twins))
+    both = jnp.maximum(values + forms * (1.0 / (CHANNELS * CHANNELS)) / diag, 0.0)
     lines = points // LANES
-    both = call(
-        far_kernel,
-        wide(2 * SUBLANES, LANES),
-        (other, partial, steering, *ready[:3], twin_steering, *ready[3:]),
-    )
     updated = both[:lines].reshape(1, points)
     summed = both
     for bit in (1, 2, 6):

time: 35.4 us -> 35.2 us (level)
  Pallas kernels: 4.03 us -> 3.35 us
  waiting for transfers between devices: 15.6 us -> 16.1 us
    pallas_call x5 -> x4, Pallas kernels: 4.03 us -> 3.35 us  [call(): pl.pallas_call(kernel, out_shape=out_shape, in_specs=[spec] * len(operand...]
    ppermute x1, waiting for transfers between devices: 0.57 us -> 1.06 us  [body(): forms = partial + swapped(lax.ppermute(partial, 'band', twins))]
  transfers between devices with their start and end apart: 9 -> 9, of which waited for: 8 -> 8; matrix products, arithmetic and copies ran while one was open for 2% -> 2% of each run, Pallas kernels for 5% -> 3%
where the time goes in v5:
time: 35.2 us; the launch traced here: 35.1 us
  waiting for transfers between devices  16.1 us (46%)
  starting transfers between devices  13.7 us (39%)
  Pallas kernels  3.35 us (10%)
  between operations  0.71 us (2%)
  other arithmetic  0.69 us (2%)
  local copies, waits for them, and re-layouts  0.59 us (2%)
    ppermute x3, waiting for transfers between devices, body(): lax.ppermute(total, 'band', [(i, partner(i, step)) for i in range(16)])  9.18 us
    ppermute x3, starting transfers between devices, across(): moved = lax.ppermute(value, ('band', 'blk'), pairs)  7.05 us
    ppermute x3, starting transfers between devices, body(): lax.ppermute(total, 'band', [(i, partner(i, step)) for i in range(16)])  6.16 us
    ppermute x3, waiting for transfers between devices, across(): moved = lax.ppermute(value, ('band', 'blk'), pairs)  4.96 us
    pallas_call x4, Pallas kernels, call(): pl.pallas_call(kernel, out_shape=out_shape, in_specs=[spec] * len(operand...  3.35 us
    ppermute x1, waiting for transfers between devices, body(): forms = partial + swapped(lax.ppermute(partial, 'band', twins))  1.06 us
    ppermute x1, waiting for transfers between devices, body(): total = keep + lax.ppermute(send, 'band', twins)  0.85 us
  transfers between devices with their start and end apart: 9, of which 8 were waited for; matrix products, arithmetic and copies ran while one was open for 2% of the time, Pallas kernels for 3%

profile of v5, /device:TPU:0, one launch (start us, length us, event | category | flops | bytes accessed | tf_op | source)
XLA Modules:
  0.0 35.1 jit_solution(12857885580406382785)
XLA Ops:
  0.6 1.6 %shard_map.50 = (f32[128,256]{1,0:T(8,128)S(1)}, bf16[784,512]{1,0:T(8,128)(2,1)S(1)}, bf16[1,768]{1,0:T(2,128)(2,1)S(1)}, f32[16,512]{1,0:T(8,128)S(1)}) custom-call(bf16[768,512]{1,0:T(8,128)(2,1)} %bitcast.11, bf16[1,768]{1,0:T(2,128)(2,1)} %estimates_far.1, f32[16,512]{1,0:T(8,128)} %bitcast.12), custom_call_target="tpu_custom_call" | custom-call | flops 268435456 | bytes 1048576 | tf_op jit(solution)/shard_map/pallas_call | solution.py:28
  2.3 0.1 collective-permute-start
  2.4 0.5 %shard_map.51 = f32[128,256]{1,0:T(8,128)S(1)} custom-call(bf16[784,512]{1,0:T(8,128)(2,1)S(1)} %get-tuple-element.28.steering, bf16[1,768]{1,0:T(2,128)(2,1)S(1)} %get-tuple-element.24.estimates, f32[16,512]{1,0:T(8,128)S(1)} %get-tuple-element.25.spectra), custom_call_target="tpu_custom_call" | custom-call | flops 268435456 | bytes 1048576 | tf_op jit(solution)/shard_map/pallas_call | solution.py:28
  2.9 0.8 %collective-permute-done = f32[128,256]{1,0:T(8,128)S(1)} collective-permute-done((f32[128,256]{1,0:T(8,128)S(1)}, f32[128,256]{1,0:T(8,128)S(1)}, u32[]{:S(2)}, u32[]{:S(2)}) %collective-permute-start) | collective-permute-done | bytes 131104 | tf_op jit(solution)/shard_map/ppermute | solution.py:188
  3.7 0.2 collective-permute-start.2
  4.0 1.6 %collective-permute-start.1 = (f32[128,256]{1,0:T(8,128)S(1)}, f32[128,256]{1,0:T(8,128)S(1)}, u32[]{:S(2)}, u32[]{:S(2)}) collective-permute-start(f32[128,256]{1,0:T(8,128)S(1)} %add.27), channel_id=1, source_target_pairs={{0,24},{8,96},{16,120},{24,0},{32,72},{40,48},{48,40},{56,80},{64,... | collective-permute-start | bytes 393224 | tf_op jit(solution)/shard_map/ppermute | solution.py:194
  5.6 2.8 %collective-permute-done.1 = f32[128,256]{1,0:T(8,128)S(1)} collective-permute-done((f32[128,256]{1,0:T(8,128)S(1)}, f32[128,256]{1,0:T(8,128)S(1)}, u32[]{:S(2)}, u32[]{:S(2)}) %collective-permute-start.1) | collective-permute-done | bytes 131104 | tf_op jit(solution)/shard_map/ppermute | solution.py:194
  8.4 0.0 collective-permute-done.2.twin_steering
  8.4 4.5 %collective-permute-start.3 = (f32[128,256]{1,0:T(8,128)S(1)}, f32[128,256]{1,0:T(8,128)S(1)}, u32[]{:S(2)}, u32[]{:S(2)}) collective-permute-start(f32[128,256]{1,0:T(8,128)S(1)} %add.28), channel_id=1, source_target_pairs={{0,104},{8,32},{16,56},{24,112},{32,8},{40,64},{48,88},{56,16},{64... | collective-permute-start | bytes 393224 | tf_op jit(solution)/shard_map/ppermute | solution.py:194
  12.8 0.6 %shard_map.52 = (f32[256,768]{1,0:T(8,128)S(1)}, f32[256,768]{1,0:T(8,128)S(1)}, f32[256,768]{1,0:T(8,128)S(1)}, f32[256,768]{1,0:T(8,128)S(1)}, f32[16,128]{1,0:T(8,128)S(1)}, /*index=5*/f32[16,128]{1,0:T(8,128)S(1)}) custom-call(bf16[784,512]{1,0:T(8,128)(2,1)S(1)} %get-tuple-element.28.steering, bf16[784,512]{1,0:T(8,128)(2,1)S(1)} %collective-permute-done.2.twin_steering), custom_call_target="tpu_custom_call" | custom-call | flops 268435456 | bytes 1048576 | tf_op jit(solution)/shard_map/pallas_call | solution.py:28
  13.5 2.0 %collective-permute-done.3 = f32[128,256]{1,0:T(8,128)S(1)} collective-permute-done((f32[128,256]{1,0:T(8,128)S(1)}, f32[128,256]{1,0:T(8,128)S(1)}, u32[]{:S(2)}, u32[]{:S(2)}) %collective-permute-start.3) | collective-permute-done | bytes 131104 | tf_op jit(solution)/shard_map/ppermute | solution.py:194
  15.5 0.1 collective-permute-start.4
  15.6 4.4 %collective-permute-done.4 = f32[128,256]{1,0:T(8,128)S(1)} collective-permute-done((f32[128,256]{1,0:T(8,128)S(1)}, f32[128,256]{1,0:T(8,128)S(1)}, u32[]{:S(2)}, u32[]{:S(2)}) %collective-permute-start.4) | collective-permute-done | bytes 131104 | tf_op jit(solution)/shard_map/ppermute | solution.py:194
  20.0 0.6 %shard_map.53 = f32[16,128]{1,0:T(8,128)S(1)} custom-call(f32[128,256]{1,0:T(8,128)S(1)} %add.30.mine, bf16[784,512]{1,0:T(8,128)(2,1)S(1)} %get-tuple-element.28.steering, f32[256,768]{1,0:T(8,128)S(1)} %get-tuple-element.39.minus, f32[256,768]{1,0:T(8,128)S(1)} %get-tuple-element.40.plus, bf16[784,512]{1,0:T(8,128)(2,1)S(1)} %collective-permute-done.2.twin_steering, ...), custom_call_target="tpu_custom_call" | custom-call | flops 268435456 | bytes 1048576 | tf_op jit(solution)/shard_map/pallas_call | solution.py:28
  20.6 0.2 collective-permute-start.5
  20.8 1.1 %collective-permute-done.5 = f32[16,128]{1,0:T(8,128)S(1)} collective-permute-done((f32[16,128]{1,0:T(8,128)S(1)}, f32[16,128]{1,0:T(8,128)S(1)}, u32[]{:S(2)}, u32[]{:S(2)}) %collective-permute-start.5) | collective-permute-done | bytes 8224 | tf_op jit(solution)/shard_map/ppermute | solution.py:202
  21.9 3.0 %collective-permute-start.6 = (f32[16,128]{1,0:T(8,128)S(1)}, f32[16,128]{1,0:T(8,128)S(1)}, u32[]{:S(2)}, u32[]{:S(2)}) collective-permute-start(f32[16,128]{1,0:T(8,128)S(1)} %fusion.3), channel_id=1, source_target_pairs={{0,9},{1,8},{2,11},{3,10},{4,13},{5,12},{6,15},{7,14},{8,1},{9,0},... | collective-permute-start | bytes 24584 | tf_op jit(solution)/shard_map/ppermute | solution.py:165
  24.9 1.6 %collective-permute-done.6 = f32[16,128]{1,0:T(8,128)S(1)} collective-permute-done((f32[16,128]{1,0:T(8,128)S(1)}, f32[16,128]{1,0:T(8,128)S(1)}, u32[]{:S(2)}, u32[]{:S(2)}) %collective-permute-start.6) | collective-permute-done | bytes 8224 | tf_op jit(solution)/shard_map/ppermute | solution.py:165
  26.6 1.2 %collective-permute-start.7 = (f32[16,128]{1,0:T(8,128)S(1)}, f32[16,128]{1,0:T(8,128)S(1)}, u32[]{:S(2)}, u32[]{:S(2)}) collective-permute-start(f32[16,128]{1,0:T(8,128)S(1)} %maximum_add_fusion.1), channel_id=1, source_target_pairs={{0,10},{1,11},{2,8},{3,9},{4,14},{5,15},{6,12},{7,13},{8,2},{9,3},... | collective-permute-start | bytes 24584 | tf_op jit(solution)/shard_map/ppermute | solution.py:165
  27.8 1.8 %collective-permute-done.7 = f32[16,128]{1,0:T(8,128)S(1)} collective-permute-done((f32[16,128]{1,0:T(8,128)S(1)}, f32[16,128]{1,0:T(8,128)S(1)}, u32[]{:S(2)}, u32[]{:S(2)}) %collective-permute-start.7) | collective-permute-done | bytes 8224 | tf_op jit(solution)/shard_map/ppermute | solution.py:165
  29.7 2.8 %collective-permute-start.8 = (f32[16,128]{1,0:T(8,128)S(1)}, f32[16,128]{1,0:T(8,128)S(1)}, u32[]{:S(2)}, u32[]{:S(2)}) collective-permute-start(f32[16,128]{1,0:T(8,128)S(1)} %maximum_add_fusion.2), channel_id=1, source_target_pairs={{0,6},{1,7},{2,4},{3,5},{4,2},{5,3},{6,0},{7,1},{8,14},{9,15},{10,... | collective-permute-start | bytes 24584 | tf_op jit(solution)/shard_map/ppermute | solution.py:165
  32.4 0.6 %copy.7 = f32[1,1,6,128]{3,1,2,0:T(1,128)} copy(f32[1,1,6,128]{3,2,1,0:T(8,128)S(1)} %slice_bitcast_fusion) | data formatting | bytes 6144
  33.0 1.5 %collective-permute-done.8 = f32[16,128]{1,0:T(8,128)S(1)} collective-permute-done((f32[16,128]{1,0:T(8,128)S(1)}, f32[16,128]{1,0:T(8,128)S(1)}, u32[]{:S(2)}, u32[]{:S(2)}) %collective-permute-start.8) | collective-permute-done | bytes 8224 | tf_op jit(solution)/shard_map/ppermute | solution.py:165
  34.5 0.6 %fusion.4 = f32[768]{0:T(1024)} fusion(f32[16,128]{1,0:T(8,128)S(1)} %collective-permute-done.8, f32[16,128]{1,0:T(8,128)S(1)} %maximum_add_fusion.2), kind=kLoop, calls=%fused_computation.8 | loop fusion | flops 768 | bytes 9216 | tf_op jit(solution)/shard_map/reshape | solution.py:209
  (11 shorter events, 0.1 us)
Async XLA Ops:
  2.3 1.4 %collective-permute-start = (f32[128,256]{1,0:T(8,128)S(1)}, f32[128,256]{1,0:T(8,128)S(1)}, u32[]{:S(2)}, u32[]{:S(2)}) collective-permute-start(f32[128,256]{1,0:T(8,128)S(1)} %get-tuple-element.26), channel_id=1, source_target_pairs={{0,8},{8,0},{16,24},{24,16},{32,40},{40,32},{48,56},{56,48},{64,72... | collective-permute-start | bytes 393224 | tf_op jit(solution)/shard_map/ppermute | solution.py:188
  3.7 4.6 %collective-permute-start.2 = (bf16[784,512]{1,0:T(8,128)(2,1)S(1)}, bf16[784,512]{1,0:T(8,128)(2,1)S(1)}, u32[]{:S(2)}, u32[]{:S(2)}) collective-permute-start(bf16[784,512]{1,0:T(8,128)(2,1)S(1)} %get-tuple-element.28.steering), channel_id=1, source_target_pairs={{0,8},{8,0},{16,24},{24,16},{32,40},{40,32},{48,56},{56,48},{64,72... | collective-permute-start | bytes 2408456 | tf_op jit(solution)/shard_map/ppermute | solution.py:190
  4.0 4.4 %collective-permute-start.1 = (f32[128,256]{1,0:T(8,128)S(1)}, f32[128,256]{1,0:T(8,128)S(1)}, u32[]{:S(2)}, u32[]{:S(2)}) collective-permute-start(f32[128,256]{1,0:T(8,128)S(1)} %add.27), channel_id=1, source_target_pairs={{0,24},{8,96},{16,120},{24,0},{32,72},{40,48},{48,40},{56,80},{64,... | collective-permute-start | bytes 393224 | tf_op jit(solution)/shard_map/ppermute | solution.py:194
  8.4 7.1 %collective-permute-start.3 = (f32[128,256]{1,0:T(8,128)S(1)}, f32[128,256]{1,0:T(8,128)S(1)}, u32[]{:S(2)}, u32[]{:S(2)}) collective-permute-start(f32[128,256]{1,0:T(8,128)S(1)} %add.28), channel_id=1, source_target_pairs={{0,104},{8,32},{16,56},{24,112},{32,8},{40,64},{48,88},{56,16},{64... | collective-permute-start | bytes 393224 | tf_op jit(solution)/shard_map/ppermute | solution.py:194
  15.5 4.5 %collective-permute-start.4 = (f32[128,256]{1,0:T(8,128)S(1)}, f32[128,256]{1,0:T(8,128)S(1)}, u32[]{:S(2)}, u32[]{:S(2)}) collective-permute-start(f32[128,256]{1,0:T(8,128)S(1)} %add.29), channel_id=1, source_target_pairs={{0,40},{8,16},{16,8},{24,48},{32,56},{40,0},{48,24},{56,32},{64,10... | collective-permute-start | bytes 393224 | tf_op jit(solution)/shard_map/ppermute | solution.py:194
  20.6 1.3 %collective-permute-start.5 = (f32[16,128]{1,0:T(8,128)S(1)}, f32[16,128]{1,0:T(8,128)S(1)}, u32[]{:S(2)}, u32[]{:S(2)}) collective-permute-start(f32[16,128]{1,0:T(8,128)S(1)} %shard_map.53), channel_id=1, source_target_pairs={{0,8},{8,0},{16,24},{24,16},{32,40},{40,32},{48,56},{56,48},{64,72... | collective-permute-start | bytes 24584 | tf_op jit(solution)/shard_map/ppermute | solution.py:202
  21.9 4.7 %collective-permute-start.6 = (f32[16,128]{1,0:T(8,128)S(1)}, f32[16,128]{1,0:T(8,128)S(1)}, u32[]{:S(2)}, u32[]{:S(2)}) collective-permute-start(f32[16,128]{1,0:T(8,128)S(1)} %fusion.3), channel_id=1, source_target_pairs={{0,9},{1,8},{2,11},{3,10},{4,13},{5,12},{6,15},{7,14},{8,1},{9,0},... | collective-permute-start | bytes 24584 | tf_op jit(solution)/shard_map/ppermute | solution.py:165
  26.6 3.1 %collective-permute-start.7 = (f32[16,128]{1,0:T(8,128)S(1)}, f32[16,128]{1,0:T(8,128)S(1)}, u32[]{:S(2)}, u32[]{:S(2)}) collective-permute-start(f32[16,128]{1,0:T(8,128)S(1)} %maximum_add_fusion.1), channel_id=1, source_target_pairs={{0,10},{1,11},{2,8},{3,9},{4,14},{5,15},{6,12},{7,13},{8,2},{9,3},... | collective-permute-start | bytes 24584 | tf_op jit(solution)/shard_map/ppermute | solution.py:165
  29.7 4.9 %collective-permute-start.8 = (f32[16,128]{1,0:T(8,128)S(1)}, f32[16,128]{1,0:T(8,128)S(1)}, u32[]{:S(2)}, u32[]{:S(2)}) collective-permute-start(f32[16,128]{1,0:T(8,128)S(1)} %maximum_add_fusion.2), channel_id=1, source_target_pairs={{0,6},{1,7},{2,4},{3,5},{4,2},{5,3},{6,0},{7,1},{8,14},{9,15},{10,... | collective-permute-start | bytes 24584 | tf_op jit(solution)/shard_map/ppermute | solution.py:165

commit v6 on v5

--- a/solution.py
+++ b/solution.py
@@ -12,7 +12,6 @@
 CHUNK = 256
 FIRST = 768
 LANES = 128
-TAIL = 16
 FLIPPED = (1, 2)
 SUBLANES = 8
 ORDER = ((0, 3, 1), (3, 1, 0))
@@ -53,7 +52,7 @@
 
 
 def place(index):
-    return lax.rem(index + lax.div(index, 2) + lax.div(index, 4), 2)
+    return lax.rem(index + lax.div(index, 4), 2)
 
 
 def products(steering, values, first, rows):
@@ -63,14 +62,14 @@
     return total + dot(parts((real + imag) * values), steering[rows, CHANNELS:], 0)
 
 
-def cross_half(spectra, placed, half, out):
+def cross_half(spectra, index, placed, half, out):
     count = spectra.shape[0]
     first = pl.multiple_of(half * HALF, HALF)
-    row = pl.multiple_of(lax.axis_index("band") * count, count)
+    row = pl.multiple_of(index * count, count)
     cross_real, cross_imag = spectra[:, :CHANNELS], spectra[:, CHANNELS:]
     placed[...] = jnp.zeros_like(placed)
     placed[pl.ds(row, count), :] = (cross_real + cross_imag) * 0.5
-    out[...] = placed[:, pl.ds(first, HALF)].T
+    out[...] = out[...] + placed[:, pl.ds(first, HALF)].T
 
     @pl.when(lax.div(row, HALF) == half)
     def _():
@@ -78,56 +77,52 @@
         out[here, :] = out[here, :] + (cross_real - cross_imag) * 0.5
 
 
-def first_kernel(steering_far, estimates_far, spectra_far, out, steering, estimates, spectra, placed, sems):
-    points = steering_far.shape[0]
-    whole = steering.at[pl.ds(0, points)]
+def own_kernel(steering_far, estimates_far, spectra_far, out, steering, estimates, placed, spectra, sems):
     loads = [
         pltpu.make_async_copy(estimates_far, estimates, sems.at[0]),
         pltpu.make_async_copy(spectra_far, spectra, sems.at[1]),
-        pltpu.make_async_copy(steering_far, whole, sems.at[2]),
+        pltpu.make_async_copy(steering_far, steering, sems.at[2]),
     ]
     for load in loads:
         load.start()
-    half = 1 - place(lax.axis_index("band"))
+    index = lax.axis_index("band")
+    half = place(index)
+    out[...] = jnp.zeros_like(out)
     loads[1].wait()
-    cross_half(spectra, placed, half, out)
+    cross_half(spectra, index, placed, half, out)
     loads[0].wait()
     values = estimates[...].astype(jnp.float32)
-    line = lax.broadcasted_iota(jnp.int32, (TAIL, 2 * CHANNELS), 0)
-    rest = jnp.zeros((1, 4 * CHANNELS - points), jnp.float32)
-    back = jnp.concatenate([values[:, 2 * CHANNELS :], rest], axis=1)
-    tail = jnp.where(line == 0, values[:, : 2 * CHANNELS], jnp.where(line == 1, back, 0.0))
-    steering[pl.ds(points, TAIL), :] = tail.astype(steering.dtype)
     loads[2].wait()
-    own = products(steering, values, pl.multiple_of(half * HALF, HALF), slice(0, points))
+    own = products(steering, values, pl.multiple_of(half * HALF, HALF), slice(None))
     out[...] = out[...] - folded(own)
 
 
-def second_kernel(steering, estimates, spectra, out, placed):
-    half = place(lax.axis_index("band"))
+def twin_kernel(own, steering, estimates, spectra, out, placed):
+    index = lax.axis_index("band")
+    half = place(index)
+    out[...] = own[...]
+    cross_half(spectra, index + 1 - 2 * lax.rem(index, 2), placed, half, out)
     values = estimates[...].astype(jnp.float32)
-    own = products(steering, values, pl.multiple_of(half * HALF, HALF), slice(0, estimates.shape[1]))
-    cross_half(spectra, placed, half, out)
-    out[...] = out[...] - folded(own)
-
-
-def ready_kernel(steering, twin_steering, minus, plus, twin_minus, twin_plus, values, diag):
+    more = products(steering, values, pl.multiple_of(half * HALF, HALF), slice(None))
+    out[...] = out[...] - folded(more)
+
+
+def ready_kernel(steering, estimates, twin_steering, twin_estimates, minus, plus, twin_minus, twin_plus, values, diag):
     scale = 1.0 / (CHANNELS * CHANNELS)
     values[...] = jnp.zeros_like(values)
     diag[...] = jnp.ones_like(diag)
-    sides = ((steering, minus, plus), (twin_steering, twin_minus, twin_plus))
-    for side, (rows, less, more) in enumerate(sides):
+    sides = ((steering, estimates, minus, plus), (twin_steering, twin_estimates, twin_minus, twin_plus))
+    for side, (rows, levels, less, more) in enumerate(sides):
         points = less.shape[1]
-        real = rows[:points, :CHANNELS].T.astype(jnp.float32)
-        imag = rows[:points, CHANNELS:].T.astype(jnp.float32)
+        real = rows[:, :CHANNELS].T.astype(jnp.float32)
+        imag = rows[:, CHANNELS:].T.astype(jnp.float32)
         less[...] = real - imag
         more[...] = real + imag
         power = jnp.sum(real * real + imag * imag, axis=0, keepdims=True)
-        tail = rows[points:, :].astype(jnp.float32)
-        estimates = jnp.concatenate([tail[:1], tail[1:2, : points - 2 * CHANNELS]], axis=1)
+        level = levels[...].astype(jnp.float32)
         for t in range(0, points, LANES):
             line = side * SUBLANES + t // LANES
-            values[line : line + 1, :] = estimates[:, t : t + LANES]
+            values[line : line + 1, :] = level[:, t : t + LANES]
             diag[line : line + 1, :] = power[:, t : t + LANES] * power[:, t : t + LANES] * scale
 
 
@@ -150,9 +145,9 @@
 
 def partner(index, step):
     z, y, core = index // 4, index // 2 % 2, index % 2
-    kind = ORDER[(z + y + core) % 2][step]
+    kind = ORDER[(z + core) % 2][step]
     z, y = (z, 1 - y) if kind == 0 else (z ^ kind, y)
-    return (z * 2 + y) * 2 + 1 - core
+    return (z * 2 + y) * 2 + (core if kind == 0 else 1 - core)
 
 
 def swapped(value):
@@ -171,30 +166,26 @@
     steering, spectra = steering[0], spectra[0]
     scratch = [pltpu.VMEM((CHANNELS, CHANNELS), jnp.float32)]
     operands = tuple(pltpu.with_memory_space_constraint(a, pltpu.HBM) for a in (steering, estimates, spectra))
-    send, steering, estimates, spectra = call(
-        first_kernel,
-        (
-            wide(HALF, CHANNELS),
-            jax.ShapeDtypeStruct((points + TAIL, 2 * CHANNELS), steering.dtype),
-            jax.ShapeDtypeStruct(estimates.shape, estimates.dtype),
-            wide(*spectra.shape),
-        ),
+    twins = [(i, i ^ 1) for i in range(16)]
+    twin_steering, twin_estimates, twin_spectra = (
+        pltpu.with_memory_space_constraint(lax.ppermute(a, "band", twins), pltpu.VMEM) for a in operands
+    )
+    own, steering, estimates = call(
+        own_kernel,
+        (wide(HALF, CHANNELS), *(jax.ShapeDtypeStruct(a.shape, a.dtype) for a in (steering, estimates))),
         operands,
-        scratch + [pltpu.SemaphoreType.DMA((3,))],
+        scratch + [pltpu.VMEM(spectra.shape, jnp.float32), pltpu.SemaphoreType.DMA((3,))],
         spec=ANY,
     )
-    keep = call(second_kernel, wide(HALF, CHANNELS), (steering, estimates, spectra), scratch)
-    twins = [(i, i ^ 1) for i in range(16)]
-    total = keep + lax.ppermute(send, "band", twins)
-    later, total = lax.optimization_barrier((steering, total))
-    twin_steering = lax.ppermute(later, "band", twins)
+    twin_operands = (twin_steering, twin_estimates, twin_spectra)
+    total = call(twin_kernel, wide(HALF, CHANNELS), (own, *twin_operands), scratch)
     flat = wide(CHANNELS, points)
     lined = wide(2 * SUBLANES, LANES)
     for step in range(3):
         total = total + lax.ppermute(total, "band", [(i, partner(i, step)) for i in range(16)])
         if step == 0:
-            total, twin_steering = lax.optimization_barrier((total, twin_steering))
-            ready = call(ready_kernel, (flat,) * 4 + (lined,) * 2, (steering, twin_steering))
+            total, later = lax.optimization_barrier((total, twin_steering))
+            ready = call(ready_kernel, (flat,) * 4 + (lined,) * 2, (steering, estimates, later, twin_estimates))
         if step == 1:
             total, ready = lax.optimization_barrier((total, ready))
     minus, plus, twin_minus, twin_plus, values, diag = ready

time: 35.2 us -> 34.5 us (0.980)
  waiting for transfers between devices: 16.1 us -> 15.5 us
    ppermute x3, starting transfers between devices: 6.16 us -> 5.53 us  [body(): lax.ppermute(total, 'band', [(i, partner(i, step)) for i in range(16)])]
    ppermute x2 -> x3, waiting for transfers between devices: 0.85 us -> 0.31 us  [body(): lax.ppermute(a, 'band', twins)]
  transfers between devices with their start and end apart: 9 -> 10, of which waited for: 8 -> 9; matrix products, arithmetic and copies ran while one was open for 2% -> 2% of each run, Pallas kernels for 3% -> 7%
where the time goes in v6:
time: 34.5 us; the launch traced here: 34.3 us
  waiting for transfers between devices  15.5 us (45%)
  starting transfers between devices  13.4 us (39%)
  Pallas kernels  3.42 us (10%)
  between operations  0.7 us (2%)
  local copies, waits for them, and re-layouts  0.68 us (2%)
  other arithmetic  0.67 us (2%)
    ppermute x3, waiting for transfers between devices, body(): lax.ppermute(total, 'band', [(i, partner(i, step)) for i in range(16)])  9.18 us
    ppermute x3, starting transfers between devices, across(): moved = lax.ppermute(value, ('band', 'blk'), pairs)  7.08 us
    ppermute x3, starting transfers between devices, body(): lax.ppermute(total, 'band', [(i, partner(i, step)) for i in range(16)])  5.53 us
    ppermute x3, waiting for transfers between devices, across(): moved = lax.ppermute(value, ('band', 'blk'), pairs)  4.93 us
    pallas_call x4, Pallas kernels, call(): pl.pallas_call(kernel, out_shape=out_shape, in_specs=[spec] * len(operand...  3.42 us
    ppermute x1, waiting for transfers between devices, body(): forms = partial + swapped(lax.ppermute(partial, 'band', twins))  1.06 us
  transfers between devices with their start and end apart: 10, of which 9 were waited for; matrix products, arithmetic and copies ran while one was open for 2% of the time, Pallas kernels for 7%

profile of v6, /device:TPU:0, one launch (start us, length us, event | category | flops | bytes accessed | tf_op | source)
XLA Modules:
  0.0 34.3 jit_solution(16361978121016408692)
XLA Ops:
  0.6 0.1 collective-permute-start
  0.7 0.5 %collective-permute-start.2 = (f32[16,512]{1,0:T(8,128)}, f32[16,512]{1,0:T(8,128)S(1)}, u32[]{:S(2)}, u32[]{:S(2)}) collective-permute-start(f32[16,512]{1,0:T(8,128)} %bitcast.13), channel_id=1, source_target_pairs={{0,8},{8,0},{16,24},{24,16},{32,40},{40,32},{48,56},{56,48},{64,72... | collective-permute-start | bytes 98312 | tf_op jit(solution)/shard_map/ppermute | solution.py:171
  1.2 0.1 copy-done
  1.3 1.6 %shard_map.50 = (f32[128,256]{1,0:T(8,128)S(1)}, bf16[768,512]{1,0:T(8,128)(2,1)S(1)}, bf16[1,768]{1,0:T(2,128)(2,1)S(1)}) custom-call(bf16[768,512]{1,0:T(8,128)(2,1)} %bitcast.12, bf16[1,768]{1,0:T(2,128)(2,1)} %estimates_far.1, f32[16,512]{1,0:T(8,128)} %bitcast.14), custom_call_target="tpu_custom_call" | custom-call | flops 268435456 | bytes 1048576 | tf_op jit(solution)/shard_map/pallas_call | solution.py:27
  3.0 0.3 collective-permute-done.2.spectra
  3.3 0.6 %shard_map.51 = f32[128,256]{1,0:T(8,128)S(1)} custom-call(f32[128,256]{1,0:T(8,128)S(1)} %get-tuple-element.20.own, bf16[768,512]{1,0:T(8,128)(2,1)S(1)} %collective-permute-done.steering.twin_steering, bf16[1,768]{1,0:T(2,128)(2,1)S(1)} %collective-permute-done.1.estimates.twin_estimates, f32[16,512]{1,0:T(8,128)S(1)} %collective-permute-done.2.spectra), custom_call_target="tpu_custom_call" | custom-call | flops 268435456 | bytes 1048576 | tf_op jit(solution)/shard_map/pallas_call | solution.py:27
  3.8 1.7 %collective-permute-start.3 = (f32[128,256]{1,0:T(8,128)S(1)}, f32[128,256]{1,0:T(8,128)S(1)}, u32[]{:S(2)}, u32[]{:S(2)}) collective-permute-start(f32[128,256]{1,0:T(8,128)S(1)} %shard_map.51), channel_id=1, source_target_pairs={{0,16},{8,96},{16,0},{24,112},{32,72},{40,56},{48,88},{56,40},{64,... | collective-permute-start | bytes 393224 | tf_op jit(solution)/shard_map/ppermute | solution.py:185
  5.6 3.3 %collective-permute-done.3 = f32[128,256]{1,0:T(8,128)S(1)} collective-permute-done((f32[128,256]{1,0:T(8,128)S(1)}, f32[128,256]{1,0:T(8,128)S(1)}, u32[]{:S(2)}, u32[]{:S(2)}) %collective-permute-start.3) | collective-permute-done | bytes 131104 | tf_op jit(solution)/shard_map/ppermute | solution.py:185
  8.9 3.2 %collective-permute-start.4 = (f32[128,256]{1,0:T(8,128)S(1)}, f32[128,256]{1,0:T(8,128)S(1)}, u32[]{:S(2)}, u32[]{:S(2)}) collective-permute-start(f32[128,256]{1,0:T(8,128)S(1)} %add.24), channel_id=1, source_target_pairs={{0,104},{8,32},{16,120},{24,48},{32,8},{40,64},{48,24},{56,80},{64... | collective-permute-start | bytes 393224 | tf_op jit(solution)/shard_map/ppermute | solution.py:185
  12.1 0.6 %shard_map.52 = (f32[256,768]{1,0:T(8,128)S(1)}, f32[256,768]{1,0:T(8,128)S(1)}, f32[256,768]{1,0:T(8,128)S(1)}, f32[256,768]{1,0:T(8,128)S(1)}, f32[16,128]{1,0:T(8,128)S(1)}, /*index=5*/f32[16,128]{1,0:T(8,128)S(1)}) custom-call(bf16[768,512]{1,0:T(8,128)(2,1)S(1)} %get-tuple-element.22.steering, bf16[1,768]{1,0:T(2,128)(2,1)S(1)} %get-tuple-element.23.estimates, ...), custom_call_target="tpu_custom_call" | custom-call | flops 268435456 | bytes 1048576 | tf_op jit(solution)/shard_map/pallas_call | solution.py:27
  12.7 2.0 %collective-permute-done.4 = f32[128,256]{1,0:T(8,128)S(1)} collective-permute-done((f32[128,256]{1,0:T(8,128)S(1)}, f32[128,256]{1,0:T(8,128)S(1)}, u32[]{:S(2)}, u32[]{:S(2)}) %collective-permute-start.4) | collective-permute-done | bytes 131104 | tf_op jit(solution)/shard_map/ppermute | solution.py:185
  14.7 0.6 %collective-permute-start.5 = (f32[128,256]{1,0:T(8,128)S(1)}, f32[128,256]{1,0:T(8,128)S(1)}, u32[]{:S(2)}, u32[]{:S(2)}) collective-permute-start(f32[128,256]{1,0:T(8,128)S(1)} %add.25), channel_id=1, source_target_pairs={{0,40},{8,24},{16,56},{24,8},{32,48},{40,0},{48,32},{56,16},{64,10... | collective-permute-start | bytes 393224 | tf_op jit(solution)/shard_map/ppermute | solution.py:185
  15.4 3.8 %collective-permute-done.5 = f32[128,256]{1,0:T(8,128)S(1)} collective-permute-done((f32[128,256]{1,0:T(8,128)S(1)}, f32[128,256]{1,0:T(8,128)S(1)}, u32[]{:S(2)}, u32[]{:S(2)}) %collective-permute-start.5) | collective-permute-done | bytes 131104 | tf_op jit(solution)/shard_map/ppermute | solution.py:185
  19.2 0.6 %shard_map.53 = f32[16,128]{1,0:T(8,128)S(1)} custom-call(f32[128,256]{1,0:T(8,128)S(1)} %add.26.mine, bf16[768,512]{1,0:T(8,128)(2,1)S(1)} %get-tuple-element.22.steering, f32[256,768]{1,0:T(8,128)S(1)} %get-tuple-element.33.minus, f32[256,768]{1,0:T(8,128)S(1)} %get-tuple-element.34.plus, bf16[768,512]{1,0:T(8,128)(2,1)S(1)} %collective-permute-done.steering.twin_steering, ...), custom_call_target="tpu_custom_call" | custom-call | flops 268435456 | bytes 1048576 | tf_op jit(solution)/shard_map/pallas_call | solution.py:27
  19.9 0.2 collective-permute-start.6
  20.1 1.1 %collective-permute-done.6 = f32[16,128]{1,0:T(8,128)S(1)} collective-permute-done((f32[16,128]{1,0:T(8,128)S(1)}, f32[16,128]{1,0:T(8,128)S(1)}, u32[]{:S(2)}, u32[]{:S(2)}) %collective-permute-start.6) | collective-permute-done | bytes 8224 | tf_op jit(solution)/shard_map/ppermute | solution.py:193
  21.1 3.1 %collective-permute-start.7 = (f32[16,128]{1,0:T(8,128)S(1)}, f32[16,128]{1,0:T(8,128)S(1)}, u32[]{:S(2)}, u32[]{:S(2)}) collective-permute-start(f32[16,128]{1,0:T(8,128)S(1)} %fusion.3), channel_id=1, source_target_pairs={{0,9},{1,8},{2,11},{3,10},{4,13},{5,12},{6,15},{7,14},{8,1},{9,0},... | collective-permute-start | bytes 24584 | tf_op jit(solution)/shard_map/ppermute | solution.py:160
  24.2 1.6 %collective-permute-done.7 = f32[16,128]{1,0:T(8,128)S(1)} collective-permute-done((f32[16,128]{1,0:T(8,128)S(1)}, f32[16,128]{1,0:T(8,128)S(1)}, u32[]{:S(2)}, u32[]{:S(2)}) %collective-permute-start.7) | collective-permute-done | bytes 8224 | tf_op jit(solution)/shard_map/ppermute | solution.py:160
  25.8 1.3 %collective-permute-start.8 = (f32[16,128]{1,0:T(8,128)S(1)}, f32[16,128]{1,0:T(8,128)S(1)}, u32[]{:S(2)}, u32[]{:S(2)}) collective-permute-start(f32[16,128]{1,0:T(8,128)S(1)} %maximum_add_fusion.1), channel_id=1, source_target_pairs={{0,10},{1,11},{2,8},{3,9},{4,14},{5,15},{6,12},{7,13},{8,2},{9,3},... | collective-permute-start | bytes 24584 | tf_op jit(solution)/shard_map/ppermute | solution.py:160
  27.1 1.8 %collective-permute-done.8 = f32[16,128]{1,0:T(8,128)S(1)} collective-permute-done((f32[16,128]{1,0:T(8,128)S(1)}, f32[16,128]{1,0:T(8,128)S(1)}, u32[]{:S(2)}, u32[]{:S(2)}) %collective-permute-start.8) | collective-permute-done | bytes 8224 | tf_op jit(solution)/shard_map/ppermute | solution.py:160
  28.9 2.8 %collective-permute-start.9 = (f32[16,128]{1,0:T(8,128)S(1)}, f32[16,128]{1,0:T(8,128)S(1)}, u32[]{:S(2)}, u32[]{:S(2)}) collective-permute-start(f32[16,128]{1,0:T(8,128)S(1)} %maximum_add_fusion.2), channel_id=1, source_target_pairs={{0,6},{1,7},{2,4},{3,5},{4,2},{5,3},{6,0},{7,1},{8,14},{9,15},{10,... | collective-permute-start | bytes 24584 | tf_op jit(solution)/shard_map/ppermute | solution.py:160
  31.7 0.6 %copy.7 = f32[1,1,6,128]{3,1,2,0:T(1,128)} copy(f32[1,1,6,128]{3,2,1,0:T(8,128)S(1)} %slice_bitcast_fusion) | data formatting | bytes 6144
  32.2 1.5 %collective-permute-done.9 = f32[16,128]{1,0:T(8,128)S(1)} collective-permute-done((f32[16,128]{1,0:T(8,128)S(1)}, f32[16,128]{1,0:T(8,128)S(1)}, u32[]{:S(2)}, u32[]{:S(2)}) %collective-permute-start.9) | collective-permute-done | bytes 8224 | tf_op jit(solution)/shard_map/ppermute | solution.py:160
  33.7 0.6 %fusion.4 = f32[768]{0:T(1024)} fusion(f32[16,128]{1,0:T(8,128)S(1)} %collective-permute-done.9, f32[16,128]{1,0:T(8,128)S(1)} %maximum_add_fusion.2), kind=kLoop, calls=%fused_computation.8 | loop fusion | flops 768 | bytes 9216 | tf_op jit(solution)/shard_map/reshape | solution.py:200
  (14 shorter events, 0.2 us)
Async XLA Ops:
  0.6 0.7 %copy-start = (bf16[1,768]{1,0:T(2,128)(2,1)S(1)}, bf16[1,768]{1,0:T(2,128)(2,1)}, u32[]{:S(2)}) copy-start(bf16[1,768]{1,0:T(2,128)(2,1)} %estimates_far.1) | copy-start | bytes 4612
  0.6 2.6 %collective-permute-start = (bf16[768,512]{1,0:T(8,128)(2,1)}, bf16[768,512]{1,0:T(8,128)(2,1)S(1)}, u32[]{:S(2)}, u32[]{:S(2)}) collective-permute-start(bf16[768,512]{1,0:T(8,128)(2,1)} %bitcast.11), channel_id=1, source_target_pairs={{0,8},{8,0},{16,24},{24,16},{32,40},{40,32},{48,56},{56,48},{64,72... | collective-permute-start | bytes 2359304 | tf_op jit(solution)/shard_map/ppermute | solution.py:171
  0.7 2.5 %collective-permute-start.2 = (f32[16,512]{1,0:T(8,128)}, f32[16,512]{1,0:T(8,128)S(1)}, u32[]{:S(2)}, u32[]{:S(2)}) collective-permute-start(f32[16,512]{1,0:T(8,128)} %bitcast.13), channel_id=1, source_target_pairs={{0,8},{8,0},{16,24},{24,16},{32,40},{40,32},{48,56},{56,48},{64,72... | collective-permute-start | bytes 98312 | tf_op jit(solution)/shard_map/ppermute | solution.py:171
  1.3 1.7 %collective-permute-start.1 = (bf16[1,768]{1,0:T(2,128)(2,1)S(1)}, bf16[1,768]{1,0:T(2,128)(2,1)S(1)}, u32[]{:S(2)}, u32[]{:S(2)}) collective-permute-start(bf16[1,768]{1,0:T(2,128)(2,1)S(1)} %copy-done), channel_id=1, source_target_pairs={{0,8},{8,0},{16,24},{24,16},{32,40},{40,32},{48,56},{56,48},{64,72... | collective-permute-start | bytes 4616 | tf_op jit(solution)/shard_map/ppermute | solution.py:171
  3.8 5.0 %collective-permute-start.3 = (f32[128,256]{1,0:T(8,128)S(1)}, f32[128,256]{1,0:T(8,128)S(1)}, u32[]{:S(2)}, u32[]{:S(2)}) collective-permute-start(f32[128,256]{1,0:T(8,128)S(1)} %shard_map.51), channel_id=1, source_target_pairs={{0,16},{8,96},{16,0},{24,112},{32,72},{40,56},{48,88},{56,40},{64,... | collective-permute-start | bytes 393224 | tf_op jit(solution)/shard_map/ppermute | solution.py:185
  8.9 5.8 %collective-permute-start.4 = (f32[128,256]{1,0:T(8,128)S(1)}, f32[128,256]{1,0:T(8,128)S(1)}, u32[]{:S(2)}, u32[]{:S(2)}) collective-permute-start(f32[128,256]{1,0:T(8,128)S(1)} %add.24), channel_id=1, source_target_pairs={{0,104},{8,32},{16,120},{24,48},{32,8},{40,64},{48,24},{56,80},{64... | collective-permute-start | bytes 393224 | tf_op jit(solution)/shard_map/ppermute | solution.py:185
  14.7 4.5 %collective-permute-start.5 = (f32[128,256]{1,0:T(8,128)S(1)}, f32[128,256]{1,0:T(8,128)S(1)}, u32[]{:S(2)}, u32[]{:S(2)}) collective-permute-start(f32[128,256]{1,0:T(8,128)S(1)} %add.25), channel_id=1, source_target_pairs={{0,40},{8,24},{16,56},{24,8},{32,48},{40,0},{48,32},{56,16},{64,10... | collective-permute-start | bytes 393224 | tf_op jit(solution)/shard_map/ppermute | solution.py:185
  19.9 1.3 %collective-permute-start.6 = (f32[16,128]{1,0:T(8,128)S(1)}, f32[16,128]{1,0:T(8,128)S(1)}, u32[]{:S(2)}, u32[]{:S(2)}) collective-permute-start(f32[16,128]{1,0:T(8,128)S(1)} %shard_map.53), channel_id=1, source_target_pairs={{0,8},{8,0},{16,24},{24,16},{32,40},{40,32},{48,56},{56,48},{64,72... | collective-permute-start | bytes 24584 | tf_op jit(solution)/shard_map/ppermute | solution.py:193
  21.1 4.7 %collective-permute-start.7 = (f32[16,128]{1,0:T(8,128)S(1)}, f32[16,128]{1,0:T(8,128)S(1)}, u32[]{:S(2)}, u32[]{:S(2)}) collective-permute-start(f32[16,128]{1,0:T(8,128)S(1)} %fusion.3), channel_id=1, source_target_pairs={{0,9},{1,8},{2,11},{3,10},{4,13},{5,12},{6,15},{7,14},{8,1},{9,0},... | collective-permute-start | bytes 24584 | tf_op jit(solution)/shard_map/ppermute | solution.py:160
  25.8 3.1 %collective-permute-start.8 = (f32[16,128]{1,0:T(8,128)S(1)}, f32[16,128]{1,0:T(8,128)S(1)}, u32[]{:S(2)}, u32[]{:S(2)}) collective-permute-start(f32[16,128]{1,0:T(8,128)S(1)} %maximum_add_fusion.1), channel_id=1, source_target_pairs={{0,10},{1,11},{2,8},{3,9},{4,14},{5,15},{6,12},{7,13},{8,2},{9,3},... | collective-permute-start | bytes 24584 | tf_op jit(solution)/shard_map/ppermute | solution.py:160
  28.9 4.9 %collective-permute-start.9 = (f32[16,128]{1,0:T(8,128)S(1)}, f32[16,128]{1,0:T(8,128)S(1)}, u32[]{:S(2)}, u32[]{:S(2)}) collective-permute-start(f32[16,128]{1,0:T(8,128)S(1)} %maximum_add_fusion.2), channel_id=1, source_target_pairs={{0,6},{1,7},{2,4},{3,5},{4,2},{5,3},{6,0},{7,1},{8,14},{9,15},{10,... | collective-permute-start | bytes 24584 | tf_op jit(solution)/shard_map/ppermute | solution.py:160

commit v7 on v6

--- a/solution.py
+++ b/solution.py
@@ -12,7 +12,7 @@
 CHUNK = 256
 FIRST = 768
 LANES = 128
-FLIPPED = (1, 2)
+FLIPPED = (1, 6)
 SUBLANES = 8
 ORDER = ((0, 3, 1), (3, 1, 0))
 VMEM = pl.BlockSpec(memory_space=pltpu.VMEM)
@@ -195,7 +195,7 @@
     lines = points // LANES
     updated = both[:lines].reshape(1, points)
     summed = both
-    for bit in (1, 2, 6):
+    for bit in (6, 1, 2):
         summed = across(summed, bit)
     return updated, summed[:lines].reshape(points)
 

time: 34.5 us -> 34.5 us (level)
  starting transfers between devices: 13.4 us -> 12.2 us
  waiting for transfers between devices: 15.5 us -> 16.7 us
    ppermute x3, starting transfers between devices: 7.08 us -> 5.87 us  [across(): moved = lax.ppermute(value, ('band', 'blk'), pairs)]
    ppermute x3, waiting for transfers between devices: 4.93 us -> 6.14 us  [across(): moved = lax.ppermute(value, ('band', 'blk'), pairs)]
where the time goes in v7:
time: 34.5 us; the launch traced here: 34.3 us
  waiting for transfers between devices  16.7 us (48%)
  starting transfers between devices  12.2 us (35%)
  Pallas kernels  3.42 us (10%)
  between operations  0.7 us (2%)
  local copies, waits for them, and re-layouts  0.68 us (2%)
  other arithmetic  0.67 us (2%)
    ppermute x3, waiting for transfers between devices, body(): lax.ppermute(total, 'band', [(i, partner(i, step)) for i in range(16)])  9.18 us
    ppermute x3, waiting for transfers between devices, across(): moved = lax.ppermute(value, ('band', 'blk'), pairs)  6.14 us
    ppermute x3, starting transfers between devices, across(): moved = lax.ppermute(value, ('band', 'blk'), pairs)  5.87 us
    ppermute x3, starting transfers between devices, body(): lax.ppermute(total, 'band', [(i, partner(i, step)) for i in range(16)])  5.53 us
    pallas_call x4, Pallas kernels, call(): pl.pallas_call(kernel, out_shape=out_shape, in_specs=[spec] * len(operand...  3.42 us
    ppermute x1, waiting for transfers between devices, body(): forms = partial + swapped(lax.ppermute(partial, 'band', twins))  1.06 us
  transfers between devices with their start and end apart: 10, of which 9 were waited for; matrix products, arithmetic and copies ran while one was open for 2% of the time, Pallas kernels for 7%

profile of v7, /device:TPU:0, one launch (start us, length us, event | category | flops | bytes accessed | tf_op | source)
XLA Modules:
  0.0 34.3 jit_solution(14494062559584138346)
XLA Ops:
  0.6 0.1 collective-permute-start
  0.7 0.5 %collective-permute-start.2 = (f32[16,512]{1,0:T(8,128)}, f32[16,512]{1,0:T(8,128)S(1)}, u32[]{:S(2)}, u32[]{:S(2)}) collective-permute-start(f32[16,512]{1,0:T(8,128)} %bitcast.13), channel_id=1, source_target_pairs={{0,8},{8,0},{16,24},{24,16},{32,40},{40,32},{48,56},{56,48},{64,72... | collective-permute-start | bytes 98312 | tf_op jit(solution)/shard_map/ppermute | solution.py:171
  1.2 0.1 copy-done
  1.3 1.6 %shard_map.50 = (f32[128,256]{1,0:T(8,128)S(1)}, bf16[768,512]{1,0:T(8,128)(2,1)S(1)}, bf16[1,768]{1,0:T(2,128)(2,1)S(1)}) custom-call(bf16[768,512]{1,0:T(8,128)(2,1)} %bitcast.12, bf16[1,768]{1,0:T(2,128)(2,1)} %estimates_far.1, f32[16,512]{1,0:T(8,128)} %bitcast.14), custom_call_target="tpu_custom_call" | custom-call | flops 268435456 | bytes 1048576 | tf_op jit(solution)/shard_map/pallas_call | solution.py:27
  3.0 0.3 collective-permute-done.2.spectra
  3.3 0.6 %shard_map.51 = f32[128,256]{1,0:T(8,128)S(1)} custom-call(f32[128,256]{1,0:T(8,128)S(1)} %get-tuple-element.20.own, bf16[768,512]{1,0:T(8,128)(2,1)S(1)} %collective-permute-done.steering.twin_steering, bf16[1,768]{1,0:T(2,128)(2,1)S(1)} %collective-permute-done.1.estimates.twin_estimates, f32[16,512]{1,0:T(8,128)S(1)} %collective-permute-done.2.spectra), custom_call_target="tpu_custom_call" | custom-call | flops 268435456 | bytes 1048576 | tf_op jit(solution)/shard_map/pallas_call | solution.py:27
  3.8 1.7 %collective-permute-start.3 = (f32[128,256]{1,0:T(8,128)S(1)}, f32[128,256]{1,0:T(8,128)S(1)}, u32[]{:S(2)}, u32[]{:S(2)}) collective-permute-start(f32[128,256]{1,0:T(8,128)S(1)} %shard_map.51), channel_id=1, source_target_pairs={{0,16},{8,96},{16,0},{24,112},{32,72},{40,56},{48,88},{56,40},{64,... | collective-permute-start | bytes 393224 | tf_op jit(solution)/shard_map/ppermute | solution.py:185
  5.6 3.3 %collective-permute-done.3 = f32[128,256]{1,0:T(8,128)S(1)} collective-permute-done((f32[128,256]{1,0:T(8,128)S(1)}, f32[128,256]{1,0:T(8,128)S(1)}, u32[]{:S(2)}, u32[]{:S(2)}) %collective-permute-start.3) | collective-permute-done | bytes 131104 | tf_op jit(solution)/shard_map/ppermute | solution.py:185
  8.9 3.2 %collective-permute-start.4 = (f32[128,256]{1,0:T(8,128)S(1)}, f32[128,256]{1,0:T(8,128)S(1)}, u32[]{:S(2)}, u32[]{:S(2)}) collective-permute-start(f32[128,256]{1,0:T(8,128)S(1)} %add.24), channel_id=1, source_target_pairs={{0,104},{8,32},{16,120},{24,48},{32,8},{40,64},{48,24},{56,80},{64... | collective-permute-start | bytes 393224 | tf_op jit(solution)/shard_map/ppermute | solution.py:185
  12.1 0.6 %shard_map.52 = (f32[256,768]{1,0:T(8,128)S(1)}, f32[256,768]{1,0:T(8,128)S(1)}, f32[256,768]{1,0:T(8,128)S(1)}, f32[256,768]{1,0:T(8,128)S(1)}, f32[16,128]{1,0:T(8,128)S(1)}, /*index=5*/f32[16,128]{1,0:T(8,128)S(1)}) custom-call(bf16[768,512]{1,0:T(8,128)(2,1)S(1)} %get-tuple-element.22.steering, bf16[1,768]{1,0:T(2,128)(2,1)S(1)} %get-tuple-element.23.estimates, ...), custom_call_target="tpu_custom_call" | custom-call | flops 268435456 | bytes 1048576 | tf_op jit(solution)/shard_map/pallas_call | solution.py:27
  12.7 2.0 %collective-permute-done.4 = f32[128,256]{1,0:T(8,128)S(1)} collective-permute-done((f32[128,256]{1,0:T(8,128)S(1)}, f32[128,256]{1,0:T(8,128)S(1)}, u32[]{:S(2)}, u32[]{:S(2)}) %collective-permute-start.4) | collective-permute-done | bytes 131104 | tf_op jit(solution)/shard_map/ppermute | solution.py:185
  14.7 0.6 %collective-permute-start.5 = (f32[128,256]{1,0:T(8,128)S(1)}, f32[128,256]{1,0:T(8,128)S(1)}, u32[]{:S(2)}, u32[]{:S(2)}) collective-permute-start(f32[128,256]{1,0:T(8,128)S(1)} %add.25), channel_id=1, source_target_pairs={{0,40},{8,24},{16,56},{24,8},{32,48},{40,0},{48,32},{56,16},{64,10... | collective-permute-start | bytes 393224 | tf_op jit(solution)/shard_map/ppermute | solution.py:185
  15.4 3.8 %collective-permute-done.5 = f32[128,256]{1,0:T(8,128)S(1)} collective-permute-done((f32[128,256]{1,0:T(8,128)S(1)}, f32[128,256]{1,0:T(8,128)S(1)}, u32[]{:S(2)}, u32[]{:S(2)}) %collective-permute-start.5) | collective-permute-done | bytes 131104 | tf_op jit(solution)/shard_map/ppermute | solution.py:185
  19.2 0.6 %shard_map.53 = f32[16,128]{1,0:T(8,128)S(1)} custom-call(f32[128,256]{1,0:T(8,128)S(1)} %add.26.mine, bf16[768,512]{1,0:T(8,128)(2,1)S(1)} %get-tuple-element.22.steering, f32[256,768]{1,0:T(8,128)S(1)} %get-tuple-element.33.minus, f32[256,768]{1,0:T(8,128)S(1)} %get-tuple-element.34.plus, bf16[768,512]{1,0:T(8,128)(2,1)S(1)} %collective-permute-done.steering.twin_steering, ...), custom_call_target="tpu_custom_call" | custom-call | flops 268435456 | bytes 1048576 | tf_op jit(solution)/shard_map/pallas_call | solution.py:27
  19.9 0.2 collective-permute-start.6
  20.1 1.1 %collective-permute-done.6 = f32[16,128]{1,0:T(8,128)S(1)} collective-permute-done((f32[16,128]{1,0:T(8,128)S(1)}, f32[16,128]{1,0:T(8,128)S(1)}, u32[]{:S(2)}, u32[]{:S(2)}) %collective-permute-start.6) | collective-permute-done | bytes 8224 | tf_op jit(solution)/shard_map/ppermute | solution.py:193
  21.1 2.6 %collective-permute-start.7 = (f32[16,128]{1,0:T(8,128)S(1)}, f32[16,128]{1,0:T(8,128)S(1)}, u32[]{:S(2)}, u32[]{:S(2)}) collective-permute-start(f32[16,128]{1,0:T(8,128)S(1)} %fusion.3), channel_id=1, source_target_pairs={{0,14},{1,15},{2,12},{3,13},{4,10},{5,11},{6,8},{7,9},{8,6},{9,7},... | collective-permute-start | bytes 24584 | tf_op jit(solution)/shard_map/ppermute | solution.py:160
  23.7 1.8 %collective-permute-done.7 = f32[16,128]{1,0:T(8,128)S(1)} collective-permute-done((f32[16,128]{1,0:T(8,128)S(1)}, f32[16,128]{1,0:T(8,128)S(1)}, u32[]{:S(2)}, u32[]{:S(2)}) %collective-permute-start.7) | collective-permute-done | bytes 8224 | tf_op jit(solution)/shard_map/ppermute | solution.py:160
  25.5 3.0 %collective-permute-start.8 = (f32[16,128]{1,0:T(8,128)S(1)}, f32[16,128]{1,0:T(8,128)S(1)}, u32[]{:S(2)}, u32[]{:S(2)}) collective-permute-start(f32[16,128]{1,0:T(8,128)S(1)} %maximum_add_fusion.1), channel_id=1, source_target_pairs={{0,9},{1,8},{2,11},{3,10},{4,13},{5,12},{6,15},{7,14},{8,1},{9,0},... | collective-permute-start | bytes 24584 | tf_op jit(solution)/shard_map/ppermute | solution.py:160
  28.5 1.6 %collective-permute-done.8 = f32[16,128]{1,0:T(8,128)S(1)} collective-permute-done((f32[16,128]{1,0:T(8,128)S(1)}, f32[16,128]{1,0:T(8,128)S(1)}, u32[]{:S(2)}, u32[]{:S(2)}) %collective-permute-start.8) | collective-permute-done | bytes 8224 | tf_op jit(solution)/shard_map/ppermute | solution.py:160
  30.1 0.3 collective-permute-start.9
  30.4 0.6 %copy.7 = f32[1,1,6,128]{3,1,2,0:T(1,128)} copy(f32[1,1,6,128]{3,2,1,0:T(8,128)S(1)} %slice_bitcast_fusion) | data formatting | bytes 6144
  31.0 2.8 %collective-permute-done.9 = f32[16,128]{1,0:T(8,128)S(1)} collective-permute-done((f32[16,128]{1,0:T(8,128)S(1)}, f32[16,128]{1,0:T(8,128)S(1)}, u32[]{:S(2)}, u32[]{:S(2)}) %collective-permute-start.9) | collective-permute-done | bytes 8224 | tf_op jit(solution)/shard_map/ppermute | solution.py:160
  33.7 0.6 %fusion.4 = f32[768]{0:T(1024)} fusion(f32[16,128]{1,0:T(8,128)S(1)} %collective-permute-done.9, f32[16,128]{1,0:T(8,128)S(1)} %maximum_add_fusion.2), kind=kLoop, calls=%fused_computation.8 | loop fusion | flops 768 | bytes 9216 | tf_op jit(solution)/shard_map/reshape | solution.py:200
  (14 shorter events, 0.2 us)
Async XLA Ops:
  0.6 0.7 %copy-start = (bf16[1,768]{1,0:T(2,128)(2,1)S(1)}, bf16[1,768]{1,0:T(2,128)(2,1)}, u32[]{:S(2)}) copy-start(bf16[1,768]{1,0:T(2,128)(2,1)} %estimates_far.1) | copy-start | bytes 4612
  0.6 2.6 %collective-permute-start = (bf16[768,512]{1,0:T(8,128)(2,1)}, bf16[768,512]{1,0:T(8,128)(2,1)S(1)}, u32[]{:S(2)}, u32[]{:S(2)}) collective-permute-start(bf16[768,512]{1,0:T(8,128)(2,1)} %bitcast.11), channel_id=1, source_target_pairs={{0,8},{8,0},{16,24},{24,16},{32,40},{40,32},{48,56},{56,48},{64,72... | collective-permute-start | bytes 2359304 | tf_op jit(solution)/shard_map/ppermute | solution.py:171
  0.7 2.5 %collective-permute-start.2 = (f32[16,512]{1,0:T(8,128)}, f32[16,512]{1,0:T(8,128)S(1)}, u32[]{:S(2)}, u32[]{:S(2)}) collective-permute-start(f32[16,512]{1,0:T(8,128)} %bitcast.13), channel_id=1, source_target_pairs={{0,8},{8,0},{16,24},{24,16},{32,40},{40,32},{48,56},{56,48},{64,72... | collective-permute-start | bytes 98312 | tf_op jit(solution)/shard_map/ppermute | solution.py:171
  1.3 1.7 %collective-permute-start.1 = (bf16[1,768]{1,0:T(2,128)(2,1)S(1)}, bf16[1,768]{1,0:T(2,128)(2,1)S(1)}, u32[]{:S(2)}, u32[]{:S(2)}) collective-permute-start(bf16[1,768]{1,0:T(2,128)(2,1)S(1)} %copy-done), channel_id=1, source_target_pairs={{0,8},{8,0},{16,24},{24,16},{32,40},{40,32},{48,56},{56,48},{64,72... | collective-permute-start | bytes 4616 | tf_op jit(solution)/shard_map/ppermute | solution.py:171
  3.8 5.0 %collective-permute-start.3 = (f32[128,256]{1,0:T(8,128)S(1)}, f32[128,256]{1,0:T(8,128)S(1)}, u32[]{:S(2)}, u32[]{:S(2)}) collective-permute-start(f32[128,256]{1,0:T(8,128)S(1)} %shard_map.51), channel_id=1, source_target_pairs={{0,16},{8,96},{16,0},{24,112},{32,72},{40,56},{48,88},{56,40},{64,... | collective-permute-start | bytes 393224 | tf_op jit(solution)/shard_map/ppermute | solution.py:185
  8.9 5.8 %collective-permute-start.4 = (f32[128,256]{1,0:T(8,128)S(1)}, f32[128,256]{1,0:T(8,128)S(1)}, u32[]{:S(2)}, u32[]{:S(2)}) collective-permute-start(f32[128,256]{1,0:T(8,128)S(1)} %add.24), channel_id=1, source_target_pairs={{0,104},{8,32},{16,120},{24,48},{32,8},{40,64},{48,24},{56,80},{64... | collective-permute-start | bytes 393224 | tf_op jit(solution)/shard_map/ppermute | solution.py:185
  14.7 4.5 %collective-permute-start.5 = (f32[128,256]{1,0:T(8,128)S(1)}, f32[128,256]{1,0:T(8,128)S(1)}, u32[]{:S(2)}, u32[]{:S(2)}) collective-permute-start(f32[128,256]{1,0:T(8,128)S(1)} %add.25), channel_id=1, source_target_pairs={{0,40},{8,24},{16,56},{24,8},{32,48},{40,0},{48,32},{56,16},{64,10... | collective-permute-start | bytes 393224 | tf_op jit(solution)/shard_map/ppermute | solution.py:185
  19.9 1.3 %collective-permute-start.6 = (f32[16,128]{1,0:T(8,128)S(1)}, f32[16,128]{1,0:T(8,128)S(1)}, u32[]{:S(2)}, u32[]{:S(2)}) collective-permute-start(f32[16,128]{1,0:T(8,128)S(1)} %shard_map.53), channel_id=1, source_target_pairs={{0,8},{8,0},{16,24},{24,16},{32,40},{40,32},{48,56},{56,48},{64,72... | collective-permute-start | bytes 24584 | tf_op jit(solution)/shard_map/ppermute | solution.py:193
  21.1 4.4 %collective-permute-start.7 = (f32[16,128]{1,0:T(8,128)S(1)}, f32[16,128]{1,0:T(8,128)S(1)}, u32[]{:S(2)}, u32[]{:S(2)}) collective-permute-start(f32[16,128]{1,0:T(8,128)S(1)} %fusion.3), channel_id=1, source_target_pairs={{0,14},{1,15},{2,12},{3,13},{4,10},{5,11},{6,8},{7,9},{8,6},{9,7},... | collective-permute-start | bytes 24584 | tf_op jit(solution)/shard_map/ppermute | solution.py:160
  25.5 4.6 %collective-permute-start.8 = (f32[16,128]{1,0:T(8,128)S(1)}, f32[16,128]{1,0:T(8,128)S(1)}, u32[]{:S(2)}, u32[]{:S(2)}) collective-permute-start(f32[16,128]{1,0:T(8,128)S(1)} %maximum_add_fusion.1), channel_id=1, source_target_pairs={{0,9},{1,8},{2,11},{3,10},{4,13},{5,12},{6,15},{7,14},{8,1},{9,0},... | collective-permute-start | bytes 24584 | tf_op jit(solution)/shard_map/ppermute | solution.py:160
  30.1 3.7 %collective-permute-start.9 = (f32[16,128]{1,0:T(8,128)S(1)}, f32[16,128]{1,0:T(8,128)S(1)}, u32[]{:S(2)}, u32[]{:S(2)}) collective-permute-start(f32[16,128]{1,0:T(8,128)S(1)} %maximum_add_fusion.2), channel_id=1, source_target_pairs={{0,2},{1,3},{2,0},{3,1},{4,6},{5,7},{6,4},{7,5},{8,10},{9,11},{10,... | collective-permute-start | bytes 24584 | tf_op jit(solution)/shard_map/ppermute | solution.py:160

commit v8 on v7

--- a/solution.py
+++ b/solution.py
@@ -83,7 +83,7 @@
         pltpu.make_async_copy(spectra_far, spectra, sems.at[1]),
         pltpu.make_async_copy(steering_far, steering, sems.at[2]),
     ]
-    for load in loads:
+    for load in reversed(loads):
         load.start()
     index = lax.axis_index("band")
     half = place(index)

time: 34.5 us -> 34.4 us (level)
  transfers between devices with their start and end apart: 10 -> 10, of which waited for: 9 -> 9; matrix products, arithmetic and copies ran while one was open for 2% -> 2% of each run, Pallas kernels for 7% -> 6%
where the time goes in v8:
time: 34.4 us; the launch traced here: 34.2 us
  waiting for transfers between devices  16.5 us (48%)
  starting transfers between devices  12.3 us (36%)
  Pallas kernels  3.39 us (10%)
  between operations  0.7 us (2%)
  local copies, waits for them, and re-layouts  0.68 us (2%)
  other arithmetic  0.67 us (2%)
    ppermute x3, waiting for transfers between devices, body(): lax.ppermute(total, 'band', [(i, partner(i, step)) for i in range(16)])  9.24 us
    ppermute x3, starting transfers between devices, across(): moved = lax.ppermute(value, ('band', 'blk'), pairs)  6.1 us
    ppermute x3, waiting for transfers between devices, across(): moved = lax.ppermute(value, ('band', 'blk'), pairs)  5.91 us
    ppermute x3, starting transfers between devices, body(): lax.ppermute(total, 'band', [(i, partner(i, step)) for i in range(16)])  5.34 us
    pallas_call x4, Pallas kernels, call(): pl.pallas_call(kernel, out_shape=out_shape, in_specs=[spec] * len(operand...  3.39 us
    ppermute x1, waiting for transfers between devices, body(): forms = partial + swapped(lax.ppermute(partial, 'band', twins))  1.03 us
  transfers between devices with their start and end apart: 10, of which 9 were waited for; matrix products, arithmetic and copies ran while one was open for 2% of the time, Pallas kernels for 6%

profile of v8, /device:TPU:0, one launch (start us, length us, event | category | flops | bytes accessed | tf_op | source)
XLA Modules:
  0.0 34.2 jit_solution(1803391947260705455)
XLA Ops:
  0.6 0.1 collective-permute-start
  0.7 0.5 %collective-permute-start.2 = (f32[16,512]{1,0:T(8,128)}, f32[16,512]{1,0:T(8,128)S(1)}, u32[]{:S(2)}, u32[]{:S(2)}) collective-permute-start(f32[16,512]{1,0:T(8,128)} %bitcast.13), channel_id=1, source_target_pairs={{0,8},{8,0},{16,24},{24,16},{32,40},{40,32},{48,56},{56,48},{64,72... | collective-permute-start | bytes 98312 | tf_op jit(solution)/shard_map/ppermute | solution.py:171
  1.2 0.1 copy-done
  1.3 1.6 %shard_map.50 = (f32[128,256]{1,0:T(8,128)S(1)}, bf16[768,512]{1,0:T(8,128)(2,1)S(1)}, bf16[1,768]{1,0:T(2,128)(2,1)S(1)}) custom-call(bf16[768,512]{1,0:T(8,128)(2,1)} %bitcast.12, bf16[1,768]{1,0:T(2,128)(2,1)} %estimates_far.1, f32[16,512]{1,0:T(8,128)} %bitcast.14), custom_call_target="tpu_custom_call" | custom-call | flops 268435456 | bytes 1048576 | tf_op jit(solution)/shard_map/pallas_call | solution.py:27
  3.0 0.3 collective-permute-done.2.spectra
  3.3 0.6 %shard_map.51 = f32[128,256]{1,0:T(8,128)S(1)} custom-call(f32[128,256]{1,0:T(8,128)S(1)} %get-tuple-element.20.own, bf16[768,512]{1,0:T(8,128)(2,1)S(1)} %collective-permute-done.steering.twin_steering, bf16[1,768]{1,0:T(2,128)(2,1)S(1)} %collective-permute-done.1.estimates.twin_estimates, f32[16,512]{1,0:T(8,128)S(1)} %collective-permute-done.2.spectra), custom_call_target="tpu_custom_call" | custom-call | flops 268435456 | bytes 1048576 | tf_op jit(solution)/shard_map/pallas_call | solution.py:27
  3.8 1.7 %collective-permute-start.3 = (f32[128,256]{1,0:T(8,128)S(1)}, f32[128,256]{1,0:T(8,128)S(1)}, u32[]{:S(2)}, u32[]{:S(2)}) collective-permute-start(f32[128,256]{1,0:T(8,128)S(1)} %shard_map.51), channel_id=1, source_target_pairs={{0,16},{8,96},{16,0},{24,112},{32,72},{40,56},{48,88},{56,40},{64,... | collective-permute-start | bytes 393224 | tf_op jit(solution)/shard_map/ppermute | solution.py:185
  5.6 3.3 %collective-permute-done.3 = f32[128,256]{1,0:T(8,128)S(1)} collective-permute-done((f32[128,256]{1,0:T(8,128)S(1)}, f32[128,256]{1,0:T(8,128)S(1)}, u32[]{:S(2)}, u32[]{:S(2)}) %collective-permute-start.3) | collective-permute-done | bytes 131104 | tf_op jit(solution)/shard_map/ppermute | solution.py:185
  8.9 2.8 %collective-permute-start.4 = (f32[128,256]{1,0:T(8,128)S(1)}, f32[128,256]{1,0:T(8,128)S(1)}, u32[]{:S(2)}, u32[]{:S(2)}) collective-permute-start(f32[128,256]{1,0:T(8,128)S(1)} %add.24), channel_id=1, source_target_pairs={{0,104},{8,32},{16,120},{24,48},{32,8},{40,64},{48,24},{56,80},{64... | collective-permute-start | bytes 393224 | tf_op jit(solution)/shard_map/ppermute | solution.py:185
  11.7 0.6 %shard_map.52 = (f32[256,768]{1,0:T(8,128)S(1)}, f32[256,768]{1,0:T(8,128)S(1)}, f32[256,768]{1,0:T(8,128)S(1)}, f32[256,768]{1,0:T(8,128)S(1)}, f32[16,128]{1,0:T(8,128)S(1)}, /*index=5*/f32[16,128]{1,0:T(8,128)S(1)}) custom-call(bf16[768,512]{1,0:T(8,128)(2,1)S(1)} %get-tuple-element.22.steering, bf16[1,768]{1,0:T(2,128)(2,1)S(1)} %get-tuple-element.23.estimates, ...), custom_call_target="tpu_custom_call" | custom-call | flops 268435456 | bytes 1048576 | tf_op jit(solution)/shard_map/pallas_call | solution.py:27
  12.4 2.2 %collective-permute-done.4 = f32[128,256]{1,0:T(8,128)S(1)} collective-permute-done((f32[128,256]{1,0:T(8,128)S(1)}, f32[128,256]{1,0:T(8,128)S(1)}, u32[]{:S(2)}, u32[]{:S(2)}) %collective-permute-start.4) | collective-permute-done | bytes 131104 | tf_op jit(solution)/shard_map/ppermute | solution.py:185
  14.6 0.8 %collective-permute-start.5 = (f32[128,256]{1,0:T(8,128)S(1)}, f32[128,256]{1,0:T(8,128)S(1)}, u32[]{:S(2)}, u32[]{:S(2)}) collective-permute-start(f32[128,256]{1,0:T(8,128)S(1)} %add.25), channel_id=1, source_target_pairs={{0,40},{8,24},{16,56},{24,8},{32,48},{40,0},{48,32},{56,16},{64,10... | collective-permute-start | bytes 393224 | tf_op jit(solution)/shard_map/ppermute | solution.py:185
  15.4 3.7 %collective-permute-done.5 = f32[128,256]{1,0:T(8,128)S(1)} collective-permute-done((f32[128,256]{1,0:T(8,128)S(1)}, f32[128,256]{1,0:T(8,128)S(1)}, u32[]{:S(2)}, u32[]{:S(2)}) %collective-permute-start.5) | collective-permute-done | bytes 131104 | tf_op jit(solution)/shard_map/ppermute | solution.py:185
  19.1 0.6 %shard_map.53 = f32[16,128]{1,0:T(8,128)S(1)} custom-call(f32[128,256]{1,0:T(8,128)S(1)} %add.26.mine, bf16[768,512]{1,0:T(8,128)(2,1)S(1)} %get-tuple-element.22.steering, f32[256,768]{1,0:T(8,128)S(1)} %get-tuple-element.33.minus, f32[256,768]{1,0:T(8,128)S(1)} %get-tuple-element.34.plus, bf16[768,512]{1,0:T(8,128)(2,1)S(1)} %collective-permute-done.steering.twin_steering, ...), custom_call_target="tpu_custom_call" | custom-call | flops 268435456 | bytes 1048576 | tf_op jit(solution)/shard_map/pallas_call | solution.py:27
  19.7 0.2 collective-permute-start.6
  19.9 1.0 %collective-permute-done.6 = f32[16,128]{1,0:T(8,128)S(1)} collective-permute-done((f32[16,128]{1,0:T(8,128)S(1)}, f32[16,128]{1,0:T(8,128)S(1)}, u32[]{:S(2)}, u32[]{:S(2)}) %collective-permute-start.6) | collective-permute-done | bytes 8224 | tf_op jit(solution)/shard_map/ppermute | solution.py:193
  21.0 2.7 %collective-permute-start.7 = (f32[16,128]{1,0:T(8,128)S(1)}, f32[16,128]{1,0:T(8,128)S(1)}, u32[]{:S(2)}, u32[]{:S(2)}) collective-permute-start(f32[16,128]{1,0:T(8,128)S(1)} %fusion.3), channel_id=1, source_target_pairs={{0,14},{1,15},{2,12},{3,13},{4,10},{5,11},{6,8},{7,9},{8,6},{9,7},... | collective-permute-start | bytes 24584 | tf_op jit(solution)/shard_map/ppermute | solution.py:160
  23.7 1.7 %collective-permute-done.7 = f32[16,128]{1,0:T(8,128)S(1)} collective-permute-done((f32[16,128]{1,0:T(8,128)S(1)}, f32[16,128]{1,0:T(8,128)S(1)}, u32[]{:S(2)}, u32[]{:S(2)}) %collective-permute-start.7) | collective-permute-done | bytes 8224 | tf_op jit(solution)/shard_map/ppermute | solution.py:160
  25.4 3.0 %collective-permute-start.8 = (f32[16,128]{1,0:T(8,128)S(1)}, f32[16,128]{1,0:T(8,128)S(1)}, u32[]{:S(2)}, u32[]{:S(2)}) collective-permute-start(f32[16,128]{1,0:T(8,128)S(1)} %maximum_add_fusion.1), channel_id=1, source_target_pairs={{0,9},{1,8},{2,11},{3,10},{4,13},{5,12},{6,15},{7,14},{8,1},{9,0},... | collective-permute-start | bytes 24584 | tf_op jit(solution)/shard_map/ppermute | solution.py:160
  28.4 1.5 %collective-permute-done.8 = f32[16,128]{1,0:T(8,128)S(1)} collective-permute-done((f32[16,128]{1,0:T(8,128)S(1)}, f32[16,128]{1,0:T(8,128)S(1)}, u32[]{:S(2)}, u32[]{:S(2)}) %collective-permute-start.8) | collective-permute-done | bytes 8224 | tf_op jit(solution)/shard_map/ppermute | solution.py:160
  30.0 0.4 %collective-permute-start.9 = (f32[16,128]{1,0:T(8,128)S(1)}, f32[16,128]{1,0:T(8,128)S(1)}, u32[]{:S(2)}, u32[]{:S(2)}) collective-permute-start(f32[16,128]{1,0:T(8,128)S(1)} %maximum_add_fusion.2), channel_id=1, source_target_pairs={{0,2},{1,3},{2,0},{3,1},{4,6},{5,7},{6,4},{7,5},{8,10},{9,11},{10,... | collective-permute-start | bytes 24584 | tf_op jit(solution)/shard_map/ppermute | solution.py:160
  30.3 0.6 %copy.7 = f32[1,1,6,128]{3,1,2,0:T(1,128)} copy(f32[1,1,6,128]{3,2,1,0:T(8,128)S(1)} %slice_bitcast_fusion) | data formatting | bytes 6144
  30.9 2.7 %collective-permute-done.9 = f32[16,128]{1,0:T(8,128)S(1)} collective-permute-done((f32[16,128]{1,0:T(8,128)S(1)}, f32[16,128]{1,0:T(8,128)S(1)}, u32[]{:S(2)}, u32[]{:S(2)}) %collective-permute-start.9) | collective-permute-done | bytes 8224 | tf_op jit(solution)/shard_map/ppermute | solution.py:160
  33.6 0.6 %fusion.4 = f32[768]{0:T(1024)} fusion(f32[16,128]{1,0:T(8,128)S(1)} %collective-permute-done.9, f32[16,128]{1,0:T(8,128)S(1)} %maximum_add_fusion.2), kind=kLoop, calls=%fused_computation.8 | loop fusion | flops 768 | bytes 9216 | tf_op jit(solution)/shard_map/reshape | solution.py:200
  (14 shorter events, 0.2 us)
Async XLA Ops:
  0.6 0.7 %copy-start = (bf16[1,768]{1,0:T(2,128)(2,1)S(1)}, bf16[1,768]{1,0:T(2,128)(2,1)}, u32[]{:S(2)}) copy-start(bf16[1,768]{1,0:T(2,128)(2,1)} %estimates_far.1) | copy-start | bytes 4612
  0.6 2.6 %collective-permute-start = (bf16[768,512]{1,0:T(8,128)(2,1)}, bf16[768,512]{1,0:T(8,128)(2,1)S(1)}, u32[]{:S(2)}, u32[]{:S(2)}) collective-permute-start(bf16[768,512]{1,0:T(8,128)(2,1)} %bitcast.11), channel_id=1, source_target_pairs={{0,8},{8,0},{16,24},{24,16},{32,40},{40,32},{48,56},{56,48},{64,72... | collective-permute-start | bytes 2359304 | tf_op jit(solution)/shard_map/ppermute | solution.py:171
  0.7 2.5 %collective-permute-start.2 = (f32[16,512]{1,0:T(8,128)}, f32[16,512]{1,0:T(8,128)S(1)}, u32[]{:S(2)}, u32[]{:S(2)}) collective-permute-start(f32[16,512]{1,0:T(8,128)} %bitcast.13), channel_id=1, source_target_pairs={{0,8},{8,0},{16,24},{24,16},{32,40},{40,32},{48,56},{56,48},{64,72... | collective-permute-start | bytes 98312 | tf_op jit(solution)/shard_map/ppermute | solution.py:171
  1.3 1.7 %collective-permute-start.1 = (bf16[1,768]{1,0:T(2,128)(2,1)S(1)}, bf16[1,768]{1,0:T(2,128)(2,1)S(1)}, u32[]{:S(2)}, u32[]{:S(2)}) collective-permute-start(bf16[1,768]{1,0:T(2,128)(2,1)S(1)} %copy-done), channel_id=1, source_target_pairs={{0,8},{8,0},{16,24},{24,16},{32,40},{40,32},{48,56},{56,48},{64,72... | collective-permute-start | bytes 4616 | tf_op jit(solution)/shard_map/ppermute | solution.py:171
  3.8 5.0 %collective-permute-start.3 = (f32[128,256]{1,0:T(8,128)S(1)}, f32[128,256]{1,0:T(8,128)S(1)}, u32[]{:S(2)}, u32[]{:S(2)}) collective-permute-start(f32[128,256]{1,0:T(8,128)S(1)} %shard_map.51), channel_id=1, source_target_pairs={{0,16},{8,96},{16,0},{24,112},{32,72},{40,56},{48,88},{56,40},{64,... | collective-permute-start | bytes 393224 | tf_op jit(solution)/shard_map/ppermute | solution.py:185
  8.9 5.7 %collective-permute-start.4 = (f32[128,256]{1,0:T(8,128)S(1)}, f32[128,256]{1,0:T(8,128)S(1)}, u32[]{:S(2)}, u32[]{:S(2)}) collective-permute-start(f32[128,256]{1,0:T(8,128)S(1)} %add.24), channel_id=1, source_target_pairs={{0,104},{8,32},{16,120},{24,48},{32,8},{40,64},{48,24},{56,80},{64... | collective-permute-start | bytes 393224 | tf_op jit(solution)/shard_map/ppermute | solution.py:185
  14.6 4.5 %collective-permute-start.5 = (f32[128,256]{1,0:T(8,128)S(1)}, f32[128,256]{1,0:T(8,128)S(1)}, u32[]{:S(2)}, u32[]{:S(2)}) collective-permute-start(f32[128,256]{1,0:T(8,128)S(1)} %add.25), channel_id=1, source_target_pairs={{0,40},{8,24},{16,56},{24,8},{32,48},{40,0},{48,32},{56,16},{64,10... | collective-permute-start | bytes 393224 | tf_op jit(solution)/shard_map/ppermute | solution.py:185
  19.7 1.3 %collective-permute-start.6 = (f32[16,128]{1,0:T(8,128)S(1)}, f32[16,128]{1,0:T(8,128)S(1)}, u32[]{:S(2)}, u32[]{:S(2)}) collective-permute-start(f32[16,128]{1,0:T(8,128)S(1)} %shard_map.53), channel_id=1, source_target_pairs={{0,8},{8,0},{16,24},{24,16},{32,40},{40,32},{48,56},{56,48},{64,72... | collective-permute-start | bytes 24584 | tf_op jit(solution)/shard_map/ppermute | solution.py:193
  21.0 4.4 %collective-permute-start.7 = (f32[16,128]{1,0:T(8,128)S(1)}, f32[16,128]{1,0:T(8,128)S(1)}, u32[]{:S(2)}, u32[]{:S(2)}) collective-permute-start(f32[16,128]{1,0:T(8,128)S(1)} %fusion.3), channel_id=1, source_target_pairs={{0,14},{1,15},{2,12},{3,13},{4,10},{5,11},{6,8},{7,9},{8,6},{9,7},... | collective-permute-start | bytes 24584 | tf_op jit(solution)/shard_map/ppermute | solution.py:160
  25.4 4.6 %collective-permute-start.8 = (f32[16,128]{1,0:T(8,128)S(1)}, f32[16,128]{1,0:T(8,128)S(1)}, u32[]{:S(2)}, u32[]{:S(2)}) collective-permute-start(f32[16,128]{1,0:T(8,128)S(1)} %maximum_add_fusion.1), channel_id=1, source_target_pairs={{0,9},{1,8},{2,11},{3,10},{4,13},{5,12},{6,15},{7,14},{8,1},{9,0},... | collective-permute-start | bytes 24584 | tf_op jit(solution)/shard_map/ppermute | solution.py:160
  30.0 3.7 %collective-permute-start.9 = (f32[16,128]{1,0:T(8,128)S(1)}, f32[16,128]{1,0:T(8,128)S(1)}, u32[]{:S(2)}, u32[]{:S(2)}) collective-permute-start(f32[16,128]{1,0:T(8,128)S(1)} %maximum_add_fusion.2), channel_id=1, source_target_pairs={{0,2},{1,3},{2,0},{3,1},{4,6},{5,7},{6,4},{7,5},{8,10},{9,11},{10,... | collective-permute-start | bytes 24584 | tf_op jit(solution)/shard_map/ppermute | solution.py:160
